TPU v7x, 32 devices: a whole 2x2x4 slice. The times are simulated.
32 devices in a mesh: groups: 2 (over x), node: 8 (over z, y), local: 2 (over core).
Axes of the slice: x: 2, y: 2, z: 4, core: 2. Of those that a mesh axis runs over, the one named last changes fastest.
Arguments:
- tokens: bfloat16 [2048, 3584], P(('groups', 'node'), 'local'), parts along dimension 0, may hold values from -6 to 6
- out_grad: bfloat16 [2048, 3584], P(('groups', 'node'), 'local'), parts along dimension 0, may hold values from -6 to 6
- route_weight: float32 [2048, 4], P(('groups', 'node')), parts along dimension 0, may hold values from 0.1 to 1
- expert_ids: int32 [2048, 4], P(('groups', 'node')), parts along dimension 0, may hold values from 0 to 7, all different within a row; in each aligned block of 128 rows (0 to 127, 128 to 255, ...) at most 96 rows name the same one
- w_gate: bfloat16 [8, 3584, 1024], P('node', None, 'local'), may hold values from -0.09375 to 0.09375
- w_up: bfloat16 [8, 3584, 1024], P('node', None, 'local'), may hold values from -0.09375 to 0.09375
- w_down: bfloat16 [8, 1024, 3584], P('node', 'local'), may hold values from -0.1875 to 0.1875
Outputs:
- in_grad: bfloat16 [2048, 3584], P(('groups', 'node'), 'local'), parts along dimension 0
There are 2 independent parts, one for each index of `groups`. A program takes and returns all parts, laid end to end along the dimension named above; an argument that names none is the same for every part. Nothing has to cross between parts.
Inputs may be any that keep to these rules, and one draw needn't show every extreme that they name: `expert_ids`: A token names 4 different experts. Among the 128 tokens of one index of node no expert is named by more than 96 tokens, and in every draw some expert is named by exactly 96 of them.
All inputs are finite; a program needn't handle non-finite values.
Results may differ from a plain program's by a relative error of at most 0.0058.
Values may be sent and summed in bfloat16 or wider, within the bound.
No kernel may reach another device: no remote copies, remote signals or barrier semaphores. Data moves between devices by JAX's collectives and lax.ppermute only.
A program may use at most 128 MiB of HBM per device.

v0:
```python
import jax
import jax.numpy as jnp
from jax import lax
from jax.sharding import PartitionSpec as P


def expert_grad(feat_rows, cot_rows, gate_mat, up_mat, down_mat):
    numbers = (((1,), (1,)), ((), ()))
    gate_pre = jnp.dot(feat_rows, gate_mat, preferred_element_type=jnp.float32)
    up_pre = jnp.dot(feat_rows, up_mat, preferred_element_type=jnp.float32)
    hidden_grad = lax.dot_general(cot_rows, down_mat, numbers, preferred_element_type=jnp.float32)
    gate_sig = jax.nn.sigmoid(gate_pre)
    gate_grad = (hidden_grad * up_pre * gate_sig * (1.0 + gate_pre * (1.0 - gate_sig))).astype(
        jnp.bfloat16
    )
    up_grad = (hidden_grad * gate_pre * gate_sig).astype(jnp.bfloat16)
    summed = lax.dot_general(gate_grad, gate_mat, numbers, preferred_element_type=jnp.float32)
    return summed + lax.dot_general(up_grad, up_mat, numbers, preferred_element_type=jnp.float32)


def local(tokens, out_grad, route_weight, expert_ids, w_gate, w_up, w_down):
    tok_rows, half_width = tokens.shape
    top_count = expert_ids.shape[1]
    experts = lax.axis_size("node")
    capacity = 3 * tok_rows * top_count // (2 * experts)
    flat_ids = expert_ids.reshape(-1)
    onehot = (flat_ids[:, None] == jnp.arange(experts, dtype=jnp.int32)[None, :]).astype(jnp.int32)
    earlier = jnp.cumsum(onehot, axis=0) - onehot
    slot_index = jnp.sum(earlier * onehot, axis=1)
    target = flat_ids * capacity + slot_index
    scaled = (
        route_weight.reshape(-1)[:, None]
        * jnp.repeat(out_grad, top_count, axis=0).astype(jnp.float32)
    ).astype(jnp.bfloat16)
    copies = jnp.repeat(tokens, top_count, axis=0)
    feat_send = jnp.zeros((experts * capacity, half_width), jnp.bfloat16).at[target].set(copies)
    cot_send = jnp.zeros((experts * capacity, half_width), jnp.bfloat16).at[target].set(scaled)
    feat_send = feat_send.reshape(experts, capacity, half_width)
    cot_send = cot_send.reshape(experts, capacity, half_width)
    gate_half = w_gate[0]
    up_half = w_up[0]
    down_half = w_down[0]
    feat_full = lax.all_gather(
        lax.all_to_all(feat_send, "node", split_axis=0, concat_axis=0, tiled=True),
        "local",
        axis=2,
        tiled=True,
    )
    cot_full = lax.all_gather(
        lax.all_to_all(cot_send, "node", split_axis=0, concat_axis=0, tiled=True),
        "local",
        axis=2,
        tiled=True,
    )
    sources, slot_count, feat_width = feat_full.shape
    partial_value = expert_grad(
        feat_full.reshape(-1, feat_width),
        cot_full.reshape(-1, feat_width),
        gate_half,
        up_half,
        down_half,
    )
    own_sum = lax.psum_scatter(
        partial_value.reshape(sources, slot_count, feat_width),
        "local",
        scatter_dimension=2,
        tiled=True,
    )
    returned = lax.all_to_all(
        own_sum.astype(jnp.bfloat16), "node", split_axis=0, concat_axis=0, tiled=True
    )
    picked = returned.reshape(experts * capacity, half_width)[target]
    summed = out_grad.astype(jnp.float32) + jnp.sum(
        picked.reshape(tok_rows, top_count, half_width).astype(jnp.float32), axis=1
    )
    return summed.astype(jnp.bfloat16)


def solution(mesh):
    placed = (
        P(("groups", "node"), "local"),
        P(("groups", "node"), "local"),
        P(("groups", "node"), None),
        P(("groups", "node"), None),
        P("node", None, "local"),
        P("node", None, "local"),
        P("node", "local", None),
    )
    return jax.shard_map(
        local, mesh=mesh, in_specs=placed, out_specs=P(("groups", "node"), "local"), check_vma=False
    )
```

profile of v0, /device:TPU:8, one launch (start us, length us, event | category | flops | bytes accessed | tf_op | source)
XLA Modules:
  0.0 313.3 jit_solution(831772874723707125)
XLA Ops:
  6.5 0.0 all-gather.5.cloned.1.call-start
  6.5 0.8 copy.9
  7.3 0.1 eq.29
  7.4 0.1 eq.25
  7.5 0.7 broadcast_multiply_fusion
  8.2 1.1 reduce-window.6
  9.4 0.2 slice_reduce_fusion
  9.6 0.1 copy.8
  9.7 0.1 mul.49
  9.8 1.5 broadcast_in_dim.5
  11.3 1.5 reshape.102
  12.8 0.1 fusion.18
  12.9 5.1 %scatter_custom_fusion.1 = bf16[768,1792]{1,0:T(8,128)(2,1)S(1)} fusion(s32[512]{0:T(512)S(1)} %bitcast.39, bf16[512,1792]{1,0:T(8,128)(2,1)} %reshape.102, bf16[]{:T(256)} %constant.6.clone.1), kind=kCustom, calls=%fused_computation.19 | custom fusion | bytes 2753024 | tf_op jit(solution)/shard_map/scatter | solution.py:36
  18.1 67.7 %all_to_all.15 = bf16[8,96,1792]{2,1,0:T(8,128)(2,1)} all-to-all(bf16[8,96,1792]{2,1,0:T(8,128)(2,1)S(1)} %bitcast.38), channel_id=1, replica_groups=mesh['groups'=2,'node'=8,'local'=2] {'node'}, dimensions={0} | all-to-all | bytes 5505024 | tf_op jit(solution)/shard_map/all_to_all | solution.py:44
  85.8 0.0 copy-start.1
  85.8 0.0 all-gather.5.cloned.1.call-update
  85.8 0.0 all-gather.3.cloned.1.call-start
  85.9 0.9 copy-done.1
  86.8 2.4 broadcast_in_dim.4
  89.2 0.0 copy-start.2
  89.2 5.2 %convert_element_type.39 = f32[512,1792]{1,0:T(8,128)} reshape(f32[128,4,1792]{2,1,0:T(4,128)} %broadcast_in_dim.4) | data formatting | bytes 7340032 | tf_op jit(solution)/shard_map/convert_element_type | solution.py:33
  94.4 0.0 copy-done.2
  94.4 0.1 copy.11
  94.5 0.1 mul.51
  94.6 6.1 %scatter_custom_fusion = bf16[768,1792]{1,0:T(8,128)(2,1)S(1)} fusion(s32[512]{0:T(512)S(1)} %bitcast.40, f32[512,1792]{1,0:T(8,128)} %convert_element_type.39, f32[512]{0:T(512)S(1)} %mul.51, bf16[]{:T(256)} %constant.6.clone.1), kind=kCustom, calls=%fused_computation.14 | custom fusion | flops 1835008 | bytes 6424578 | tf_op jit(solution)/shard_map/scatter | solution.py:37
  100.8 65.8 %all_to_all.16 = bf16[8,96,1792]{2,1,0:T(8,128)(2,1)} all-to-all(bf16[8,96,1792]{2,1,0:T(8,128)(2,1)S(1)} %bitcast.37), channel_id=1, replica_groups=mesh['groups'=2,'node'=8,'local'=2] {'node'}, dimensions={0} | all-to-all | bytes 5505024 | tf_op jit(solution)/shard_map/all_to_all | solution.py:50
  166.6 0.0 all-gather.3.cloned.1.call-update
  166.6 0.2 reduce-scatter.2.cloned.1.call-start
  166.9 0.0 all-gather.5.cloned.1.call-done
  166.9 6.1 %fusion.2 = f32[768,512]{1,0:T(8,128)S(1)} fusion(bf16[768,3584]{1,0:T(8,128)(2,1)} %bitcast.43, bf16[1,3584,512]{2,1,0:T(8,128)(2,1)} %param.11), kind=kOutput, calls=%fused_computation.6 | convolution fusion | flops 2818572288 | bytes 10747904 | tf_op jit(solution)/shard_map/dot_general | solution.py:9
  173.0 8.9 %all-gather.3.cloned.1.call-done = bf16[8,96,3584]{2,1,0:T(8,128)(2,1)} async-done(((bf16[8,96,1792]{2,1,0:T(8,128)(2,1)}), bf16[8,96,3584]{2,1,0:T(8,128)(2,1)}) %all-gather.3.cloned.1.call-update) | async-done | bytes 5505040 | tf_op jit(solution)/shard_map/all_gather | solution.py:49
  181.8 0.0 copy-start
  181.8 6.3 %fusion.7 = f32[768,512]{1,0:T(8,128)S(1)} fusion(bf16[768,3584]{1,0:T(8,128)(2,1)} %bitcast.45, bf16[1,512,3584]{2,1,0:T(8,128)(2,1)} %param.13), kind=kOutput, calls=%fused_computation.11 | convolution fusion | flops 2818572288 | bytes 10747904 | tf_op jit(solution)/shard_map/dot_general | solution.py:11
  188.1 0.0 copy-done
  188.1 0.1 copy-done.3
  188.2 3.4 %multiply_convert_fusion.3 = bf16[768,512]{1,0:T(8,128)(2,1)S(1)} fusion(f32[768,512]{1,0:T(8,128)S(1)} %fusion.2, f32[768,512]{1,0:T(8,128)S(1)} %fusion.7, bf16[768,3584]{1,0:T(8,128)(2,1)S(1)} %bitcast.44, bf16[1,3584,512]{2,1,0:T(8,128)(2,1)S(1)} %copy-done), kind=kOutput, calls=%fused_computation.17 | convolution fusion | flops 2822504448 | bytes 13107200 | tf_op jit(solution)/shard_map/dot_general | solution.py:10
  191.5 0.0 copy-done.4
  191.5 3.1 fusion
  194.6 7.8 %convolution_add_fusion = f32[768,3584]{1,0:T(8,128)} fusion(f32[768,3584]{1,0:T(8,128)S(1)} %fusion, bf16[1,3584,512]{2,1,0:T(8,128)(2,1)} %param.12, f32[768,512]{1,0:T(8,128)S(1)} %fusion.7, f32[768,512]{1,0:T(8,128)S(1)} %fusion.2), kind=kOutput, calls=%fused_computation.3 | convolution fusion | flops 2823684096 | bytes 28835840 | tf_op jit(solution)/shard_map/dot_general | solution.py:18
  202.4 0.0 reduce-scatter.2.cloned.1.call-update
  202.4 21.0 %reduce-scatter.2.cloned.1.call-done = f32[8,96,1792]{2,1,0:T(8,128)} async-done(((f32[8,96,3584]{2,1,0:T(8,128)}), f32[8,96,1792]{2,1,0:T(8,128)}) %reduce-scatter.2.cloned.1.call-update) | async-done | bytes 5505040 | tf_op jit(solution)/shard_map/reduce_scatter | solution.py:63
  223.4 4.4 %convert_element_type.43 = bf16[8,96,1792]{2,1,0:T(8,128)(2,1)} convert(f32[8,96,1792]{2,1,0:T(8,128)} %reduce-scatter.2.cloned.1.call-done) | non-fusion elementwise | flops 1376256 | bytes 8257536 | tf_op jit(solution)/shard_map/convert_element_type | solution.py:70
  227.8 6.1 %all-to-all-start.2 = ((bf16[8,96,1792]{2,1,0:T(8,128)(2,1)}), bf16[8,96,1792]{2,1,0:T(8,128)(2,1)S(1)}, u32[]{:S(2)}, u32[]{:S(2)}) async-start(bf16[8,96,1792]{2,1,0:T(8,128)(2,1)} %convert_element_type.43), calls=%async_computation.3 | async-start | bytes 5505024 | tf_op jit(solution)/shard_map/all_to_all | solution.py:69
  233.9 60.2 %all-to-all-done.2 = bf16[8,96,1792]{2,1,0:T(8,128)(2,1)S(1)} async-done(((bf16[8,96,1792]{2,1,0:T(8,128)(2,1)}), bf16[8,96,1792]{2,1,0:T(8,128)(2,1)S(1)}, u32[]{:S(2)}, u32[]{:S(2)}) %all-to-all-start.2) | async-done | bytes 2752544 | tf_op jit(solution)/shard_map/all_to_all | solution.py:69
  294.1 3.1 %gather_fusion = bf16[512,1792]{1,0:T(8,128)(2,1)} fusion(bf16[768,1792]{1,0:T(8,128)(2,1)S(1)} %bitcast.35, s32[1024]{0:T(1024)S(1)} %pad_clamp_fusion), kind=kCustom, calls=%fused_computation | custom fusion | bytes 3672064 | tf_op jit(solution)/shard_map/gather | solution.py:72
  297.2 4.5 %reshape.81 = f32[128,4,1792]{2,1,0:T(4,128)} reshape(bf16[512,1792]{1,0:T(8,128)(2,1)} %gather_fusion) | data formatting | bytes 5505024 | tf_op jit(solution)/shard_map/convert_element_type | solution.py:74
  301.7 4.2 %reduce_sum.22 = f32[128,1792]{1,0:T(8,128)S(1)} reduce(f32[128,4,1792]{2,1,0:T(4,128)} %reshape.81, f32[]{:T(128)} %constant.16.clone.1), dimensions={1}, to_apply=%region_6.7 | reduce | flops 688128 | bytes 4587524 | tf_op jit(solution)/shard_map/reduce_sum | solution.py:73
  305.9 0.8 add_convert_fusion
  (7 shorter events, 0.1 us)
Async XLA Ops:
  6.5 160.3 %all-gather.5.cloned.1.call-start = ((), (), s32[]{:S(2)}) async-start(), calls=%async_computation.5 | async-start | bytes 8257536 | tf_op jit(solution)/shard_map/all_gather | solution.py:43
  85.8 1.0 copy-start.1
  85.8 96.0 %all-gather.3.cloned.1.call-start = ((), (), s32[]{:S(2)}) async-start(), calls=%async_computation.4 | async-start | bytes 8257536 | tf_op jit(solution)/shard_map/all_gather | solution.py:49
  89.2 5.2 %copy-start.2 = (f32[128,4]{0,1:T(4,128)S(1)}, f32[128,4]{0,1:T(4,128)}, u32[]{:S(2)}) copy-start(f32[128,4]{0,1:T(4,128)} %param.9) | copy-start | bytes 6148
  166.6 56.8 %reduce-scatter.2.cloned.1.call-start = ((), (), s32[]{:S(2)}) async-start(), calls=%async_computation.6 | async-start | bytes 16515072 | tf_op jit(solution)/shard_map/reduce_scatter | solution.py:63
  181.8 6.3 %copy-start = (bf16[1,3584,512]{2,1,0:T(8,128)(2,1)S(1)}, bf16[1,3584,512]{2,1,0:T(8,128)(2,1)}, u32[]{:S(2)}) copy-start(bf16[1,3584,512]{2,1,0:T(8,128)(2,1)} %param.12) | copy-start | bytes 11010052
  181.8 6.3 %copy-start.3 = (bf16[8,96,3584]{2,1,0:T(8,128)(2,1)S(1)}, bf16[8,96,3584]{2,1,0:T(8,128)(2,1)}, u32[]{:S(2)}) copy-start(bf16[8,96,3584]{2,1,0:T(8,128)(2,1)} %all-gather.5.cloned.1.call-done) | copy-start | bytes 16515076
  188.2 3.4 %copy-start.4 = (bf16[1,3584,512]{2,1,0:T(8,128)(2,1)S(1)}, bf16[1,3584,512]{2,1,0:T(8,128)(2,1)}, u32[]{:S(2)}) copy-start(bf16[1,3584,512]{2,1,0:T(8,128)(2,1)} %param.11) | copy-start | bytes 11010052
  227.8 66.3 %all-to-all-start.2 = ((bf16[8,96,1792]{2,1,0:T(8,128)(2,1)}), bf16[8,96,1792]{2,1,0:T(8,128)(2,1)S(1)}, u32[]{:S(2)}, u32[]{:S(2)}) async-start(bf16[8,96,1792]{2,1,0:T(8,128)(2,1)} %convert_element_type.43), calls=%async_computation.3 | async-start | bytes 5505024 | tf_op jit(solution)/shard_map/all_to_all | solution.py:69
Sparse Core Ops, SparseCore 0:
  85.9 15.0 all-gather.4
  166.7 15.0 all-gather.2
  202.5 20.8 reduce-scatter.1
where the time goes:
time: 317 us; the launch traced here: 313 us
  blocking collectives  134 us (42%)
  waiting for transfers between devices  90.1 us (28%)
  matrix products  26.5 us (8%)
  local copies, waits for them, and re-layouts  26 us (8%)
  other arithmetic  17.6 us (6%)
  between operations  13.2 us (4%)
  starting transfers between devices  6.34 us (2%)
    all_to_all x1, blocking collectives, local(): lax.all_to_all(feat_send, 'node', split_axis=0, concat_axis=0, tiled=True)  67.7 us
    all_to_all x1, blocking collectives, local(): lax.all_to_all(cot_send, 'node', split_axis=0, concat_axis=0, tiled=True)  65.8 us
    all_to_all x1, waiting for transfers between devices, local(): lax.all_to_all(own_sum.astype(jnp.bfloat16), 'node', split_axis=0, concat...  60.2 us
    reduce_scatter x1, waiting for transfers between devices, local(): lax.psum_scatter(partial_value.reshape(sources, slot_count, feat_width),...  21 us
    all_gather x1, waiting for transfers between devices, local(): lax.all_gather(lax.all_to_all(cot_send, 'node', split_axis=0, concat_axis...  8.86 us
    dot_general x1, matrix products, expert_grad(): lax.dot_general(up_grad, up_mat, numbers, preferred_element_type=jnp.floa...  7.76 us
  transfers between devices with their start and end apart: 4, of which 3 were waited for; matrix products, arithmetic and copies ran while one was open for 6% of the time, Pallas kernels for 0%

commit v1 on v0

--- a/solution.py
+++ b/solution.py
@@ -18,7 +18,7 @@
     return summed + lax.dot_general(up_grad, up_mat, numbers, preferred_element_type=jnp.float32)
 
 
-def local(tokens, out_grad, route_weight, expert_ids, w_gate, w_up, w_down):
+def exchanged(tokens, out_grad, route_weight, expert_ids, w_gate, w_up, w_down):
     tok_rows, half_width = tokens.shape
     top_count = expert_ids.shape[1]
     experts = lax.axis_size("node")
@@ -37,28 +37,20 @@
     cot_send = jnp.zeros((experts * capacity, half_width), jnp.bfloat16).at[target].set(scaled)
     feat_send = feat_send.reshape(experts, capacity, half_width)
     cot_send = cot_send.reshape(experts, capacity, half_width)
-    gate_half = w_gate[0]
-    up_half = w_up[0]
-    down_half = w_down[0]
-    feat_full = lax.all_gather(
-        lax.all_to_all(feat_send, "node", split_axis=0, concat_axis=0, tiled=True),
-        "local",
-        axis=2,
-        tiled=True,
-    )
-    cot_full = lax.all_gather(
-        lax.all_to_all(cot_send, "node", split_axis=0, concat_axis=0, tiled=True),
-        "local",
-        axis=2,
-        tiled=True,
-    )
+
+    def to_experts(sent):
+        moved = lax.all_to_all(sent, "node", split_axis=0, concat_axis=0, tiled=True)
+        return lax.all_gather(moved, "local", axis=2, tiled=True)
+
+    feat_full = to_experts(feat_send)
+    cot_full = to_experts(cot_send)
     sources, slot_count, feat_width = feat_full.shape
     partial_value = expert_grad(
         feat_full.reshape(-1, feat_width),
         cot_full.reshape(-1, feat_width),
-        gate_half,
-        up_half,
-        down_half,
+        w_gate[0],
+        w_up[0],
+        w_down[0],
     )
     own_sum = lax.psum_scatter(
         partial_value.reshape(sources, slot_count, feat_width),
@@ -74,6 +66,171 @@
         picked.reshape(tok_rows, top_count, half_width).astype(jnp.float32), axis=1
     )
     return summed.astype(jnp.bfloat16)
+
+
+def node(z, y):
+    return 2 * z + y
+
+
+def along(pairs):
+    return [(node(a, y), node(b, y)) for a, b in pairs for y in range(2)]
+
+
+def across(places):
+    return [(node(z, y), node(z, 1 - y)) for z in places for y in range(2)]
+
+
+UP1 = along([(0, 1), (1, 2), (2, 3)])
+DOWN1 = along([(1, 0), (2, 1), (3, 2)])
+UP2 = along([(1, 2), (2, 3)])
+DOWN2 = along([(2, 1), (1, 0)])
+ENDS = along([(2, 3), (1, 0)])
+SKIP = along([(0, 2), (1, 3), (2, 0), (3, 1)])
+FAR = along([(0, 3), (3, 0)])
+Y_ALL, Y_UP, Y_DOWN, Y_ENDS = across(range(4)), across([1, 2, 3]), across([0, 1, 2]), across([0, 3])
+
+
+def move(value, pairs):
+    return lax.ppermute(value, "node", pairs)
+
+
+def swap(value):
+    return lax.ppermute(value, "local", [(0, 1), (1, 0)])
+
+
+def one_hot_slots(weights, capacity):
+    tokens = weights.shape[-1]
+    routed = weights > 0.0
+    earlier = jnp.arange(tokens)[:, None] < jnp.arange(tokens)[None, :]
+    place = jnp.einsum(
+        "...s,st->...t",
+        routed.astype(jnp.bfloat16),
+        earlier.astype(jnp.bfloat16),
+        preferred_element_type=jnp.float32,
+    )
+    place = jnp.where(routed, place, -1.0)
+    slots = jnp.arange(capacity, dtype=jnp.float32)
+    return (place[..., None, :] == slots[:, None]).astype(jnp.bfloat16)
+
+
+def lines(tokens, out_grad, route_weight, expert_ids, w_gate, w_up, w_down):
+    tok_rows, half = tokens.shape
+    experts = lax.axis_size("node")
+    top_count = expert_ids.shape[1]
+    capacity = 3 * tok_rows * top_count // (2 * experts)
+    me = lax.axis_index("node")
+    z, y = me // 2, me % 2
+    side = lax.axis_index("local")
+    bf, f32 = jnp.bfloat16, jnp.float32
+
+    t_up, t_down = move(tokens, UP1), move(tokens, DOWN1)
+    g_up, g_down = move(out_grad, UP1), move(out_grad, DOWN1)
+
+    table = jnp.sum(
+        jnp.where(
+            expert_ids[None] == jnp.arange(experts, dtype=jnp.int32)[:, None, None],
+            route_weight[None],
+            0.0,
+        ),
+        axis=2,
+    )
+    pairs = table.reshape(experts // 2, 1, 2, tok_rows)
+    routes = lax.all_to_all(
+        jnp.broadcast_to(pairs, (experts // 2, 2, 2, tok_rows)).reshape(experts, 2, tok_rows),
+        "node",
+        split_axis=0,
+        concat_axis=0,
+        tiled=True,
+    )
+    own_pick = one_hot_slots(lax.dynamic_index_in_dim(table, me ^ 1, 0, False), capacity)
+    places = jnp.stack([z, z - 1, z + 1, z ^ 2, 3 - z]) % 4
+    mine = routes[places * 2 + y]
+    theirs = routes[places * 2 + 1 - y]
+    dense_weight = jnp.take(mine, y, axis=1)
+    picks = one_hot_slots(jnp.take(mine, 1 - y, axis=1), capacity)
+    slot_weights = jnp.take(theirs, y, axis=1)
+    slot_picks = one_hot_slots(slot_weights, capacity)
+    slot_weight = jnp.sum(slot_picks.astype(f32) * slot_weights[:, None, :], axis=2)
+
+    gate, up, down = w_gate[0], w_up[0], w_down[0]
+    own_at, other_at = side * half, (1 - side) * half
+    rows = lambda mat, at: lax.dynamic_slice_in_dim(mat, at, half, 0)
+    cols = lambda mat, at: lax.dynamic_slice_in_dim(mat, at, half, 1)
+    both = [jnp.concatenate([rows(gate, at), rows(up, at)], axis=1) for at in (own_at, other_at)]
+    back = jnp.concatenate([both[0], swap(both[1])], axis=1)
+    downs = [cols(down, own_at), cols(down, other_at)]
+    numbers = (((1,), (1,)), ((), ()))
+    ff = gate.shape[1]
+
+    def dot(a, b):
+        return jnp.dot(a, b, preferred_element_type=f32)
+
+    def dot_t(a, b):
+        return lax.dot_general(a, b, numbers, preferred_element_type=f32)
+
+    def compute(feat, cot, weight):
+        feat, cot = jnp.concatenate(feat, 0), jnp.concatenate(cot, 0)
+        feat_other, cot_other = swap(feat), swap(cot)
+        pre = dot(feat, both[0]) + dot(feat_other, both[1])
+        hidden = (dot_t(cot, downs[0]) + dot_t(cot_other, downs[1])) * weight[:, None]
+        gate_pre, up_pre = pre[:, :ff], pre[:, ff:]
+        sig = jax.nn.sigmoid(gate_pre)
+        gate_grad = (hidden * up_pre * sig * (1.0 + gate_pre * (1.0 - sig))).astype(bf)
+        up_grad = (hidden * gate_pre * sig).astype(bf)
+        grads = jnp.concatenate([gate_grad, up_grad], axis=1)
+        grads = jnp.concatenate([grads, swap(grads)], axis=1)
+        return dot_t(grads, back)
+
+    def across_rows(index, block, pairs, pick=None):
+        pick = picks[index] if pick is None else pick
+        return move(dot(pick, block).astype(bf), pairs)
+
+    def finish(index, dense, slots, pairs, pick=None):
+        pick = picks[index] if pick is None else pick
+        came = move(slots.astype(bf), pairs)
+        return dense + lax.dot_general(
+            pick, came, (((0,), (0,)), ((), ())), preferred_element_type=f32
+        )
+
+    t_own_y = across_rows(0, tokens, Y_ALL, own_pick)
+    g_own_y = across_rows(0, out_grad, Y_ALL, own_pick)
+    t2u, t2d = move(t_up, UP2), move(t_down, DOWN2)
+    t_up_y, t_down_y = across_rows(1, t_up, Y_UP), across_rows(2, t_down, Y_DOWN)
+    g2u, g2d = move(g_up, UP2), move(g_down, DOWN2)
+    g_up_y, g_down_y = across_rows(1, g_up, Y_UP), across_rows(2, g_down, Y_DOWN)
+    t_two = jnp.where(z >= 2, t2u, t2d)
+    g_two = jnp.where(z >= 2, g2u, g2d)
+    t_far = move(t_two, ENDS)
+    t_two_y = across_rows(3, t_two, Y_ALL)
+    g_far = move(g_two, ENDS)
+    g_two_y = across_rows(3, g_two, Y_ALL)
+    t_far_y = across_rows(4, t_far, Y_ENDS)
+    g_far_y = across_rows(4, g_far, Y_ENDS)
+
+    n, c = tok_rows, capacity
+    first = compute(
+        [tokens, t_up, t_down, t_own_y, t_up_y, t_down_y],
+        [out_grad, g_up, g_down, g_own_y, g_up_y, g_down_y],
+        jnp.concatenate([dense_weight[:3].reshape(-1), slot_weight[:3].reshape(-1)]),
+    )
+    s = 3 * n
+    own = finish(0, first[:n], first[s : s + c], Y_ALL, own_pick)
+    from_up = move(finish(1, first[n : 2 * n], first[s + c : s + 2 * c], Y_UP).astype(bf), DOWN1)
+    from_down = move(
+        finish(2, first[2 * n : s], first[s + 2 * c :], Y_DOWN).astype(bf), UP1
+    )
+    second = compute(
+        [t_two, t_two_y], [g_two, g_two_y], jnp.concatenate([dense_weight[3], slot_weight[3]])
+    )
+    from_two = move(finish(3, second[:n], second[n:], Y_ALL).astype(bf), SKIP)
+    third = compute(
+        [t_far, t_far_y], [g_far, g_far_y], jnp.concatenate([dense_weight[4], slot_weight[4]])
+    )
+    from_far = move(finish(4, third[:n], third[n:], Y_ENDS).astype(bf), FAR)
+    summed = out_grad.astype(f32) + own
+    for part in (from_up, from_down, from_two, from_far):
+        summed = summed + part.astype(f32)
+    return summed.astype(bf)
 
 
 def solution(mesh):
@@ -86,6 +243,7 @@
         P("node", None, "local"),
         P("node", "local", None),
     )
+    body = lines if mesh.shape["node"] == 8 else exchanged
     return jax.shard_map(
-        local, mesh=mesh, in_specs=placed, out_specs=P(("groups", "node"), "local"), check_vma=False
-    )
+        body, mesh=mesh, in_specs=placed, out_specs=P(("groups", "node"), "local"), check_vma=False
+    )

time: 317 us -> 225 us (0.71)
  blocking collectives: 134 us -> 0 us
  starting transfers between devices: 6.34 us -> 82.6 us
  waiting for transfers between devices: 90.1 us -> 71.6 us
  matrix products: 26.5 us -> 39.9 us
  between operations: 13.2 us -> 0.78 us
  other arithmetic: 17.6 us -> 9 us
  local copies, waits for them, and re-layouts: 26 us -> 19.8 us
    all_to_all x2 -> x0, blocking collectives: 134 us -> none  [the longest x1 67.7 us: local(): lax.all_to_all(feat_send, 'node', split_axis=0, concat_axis=0, tiled=True)]
    ppermute x0 -> x39, starting transfers between devices: none -> 76.9 us  [the longest x29 74.9 us: move(): return lax.ppermute(value, 'node', pairs)]
    ppermute x0 -> x39, waiting for transfers between devices: none -> 71.6 us  [the longest x29 69.5 us: move(): return lax.ppermute(value, 'node', pairs)]
    all_to_all x1, waiting for transfers between devices: 60.2 us -> 0.01 us  [lines(): lax.all_to_all(jnp.broadcast_to(pairs, (experts // 2, 2, 2, tok_rows)).re...]
    reduce_scatter x1 -> x0, waiting for transfers between devices: 21 us -> none  [local(): lax.psum_scatter(partial_value.reshape(sources, slot_count, feat_width),...]
    dot_general x5 -> x33, matrix products: 26.5 us -> 39.9 us  [the longest x9 18.7 us: dot_t(): return lax.dot_general(a, b, numbers, preferred_element_type=f32)]
    convert_element_type x2 -> x0, local copies, waits for them, and re-layouts: 9.7 us -> none  [the longest x1 5.23 us: local(): jnp.repeat(out_grad, top_count, axis=0).astype(jnp.float32)]
    all_gather x2 -> x0, waiting for transfers between devices: 8.88 us -> none  [the longest x1 8.86 us: local(): lax.all_gather(lax.all_to_all(cot_send, 'node', split_axis=0, concat_axis...]
  transfers between devices with their start and end apart: 4 -> 40, of which waited for: 3 -> 13; matrix products, arithmetic and copies ran while one was open for 6% -> 30% of each run, Pallas kernels for 0% -> 0%
where the time goes in v1:
time: 225 us; the launch traced here: 224 us
  starting transfers between devices  82.6 us (37%)
  waiting for transfers between devices  71.6 us (32%)
  matrix products  39.9 us (18%)
  local copies, waits for them, and re-layouts  19.8 us (9%)
  other arithmetic  9 us (4%)
    ppermute x29, starting transfers between devices, move(): return lax.ppermute(value, 'node', pairs)  74.9 us
    ppermute x29, waiting for transfers between devices, move(): return lax.ppermute(value, 'node', pairs)  69.5 us
    dot_general x9, matrix products, dot_t(): return lax.dot_general(a, b, numbers, preferred_element_type=f32)  18.7 us
    dot_general x16, matrix products, dot(): return jnp.dot(a, b, preferred_element_type=f32)  17.3 us
    unnamed x37, local copies, waits for them, and re-layouts  5.95 us
    all_to_all x1, starting transfers between devices, lines(): lax.all_to_all(jnp.broadcast_to(pairs, (experts // 2, 2, 2, tok_rows)).re...  5.73 us
    dynamic_slice x1, local copies, waits for them, and re-layouts, lines(): rows = lambda mat, at: lax.dynamic_slice_in_dim(mat, at, half, 0)  5.57 us
  transfers between devices with their start and end apart: 40, of which 13 were waited for; matrix products, arithmetic and copies ran while one was open for 30% of the time, Pallas kernels for 0%

profile of v1, /device:TPU:8, one launch (start us, length us, event | category | flops | bytes accessed | tf_op | source)
XLA Modules:
  0.0 223.7 jit_solution(8851599606249141446)
XLA Ops:
  0.0 2.0 collective-permute-start.7
  2.1 3.9 %collective-permute-start.6 = (bf16[128,1792]{1,0:T(8,128)(2,1)}, bf16[128,1792]{1,0:T(8,128)(2,1)}, u32[]{:S(2)}, u32[]{:S(2)}) collective-permute-start(bf16[128,1792]{1,0:T(8,128)(2,1)} %param.9), channel_id=1, source_target_pairs={{0,4},{2,6},{4,8},{6,10},{8,12},{10,14},{1,5},{3,7},{5,9},{7,11},{... | collective-permute-start | bytes 1376264 | tf_op jit(solution)/shard_map/ppermute | solution.py:94
  6.0 2.7 %collective-permute-start.1 = (bf16[128,1792]{1,0:T(8,128)(2,1)}, bf16[128,1792]{1,0:T(8,128)(2,1)S(1)}, u32[]{:S(2)}, u32[]{:S(2)}) collective-permute-start(bf16[128,1792]{1,0:T(8,128)(2,1)} %param.10), channel_id=1, source_target_pairs={{4,0},{6,2},{8,4},{10,6},{12,8},{14,10},{5,1},{7,3},{9,5},{11,7},{... | collective-permute-start | bytes 1376264 | tf_op jit(solution)/shard_map/ppermute | solution.py:94
  8.7 3.5 %collective-permute-start = (bf16[128,1792]{1,0:T(8,128)(2,1)}, bf16[128,1792]{1,0:T(8,128)(2,1)S(1)}, u32[]{:S(2)}, u32[]{:S(2)}) collective-permute-start(bf16[128,1792]{1,0:T(8,128)(2,1)} %param.10), channel_id=1, source_target_pairs={{0,4},{2,6},{4,8},{6,10},{8,12},{10,14},{1,5},{3,7},{5,9},{7,11},{... | collective-permute-start | bytes 1376264 | tf_op jit(solution)/shard_map/ppermute | solution.py:94
  13.5 5.7 %all-to-all-start = ((f32[8,2,128]{2,1,0:T(2,128)}), f32[8,2,128]{2,1,0:T(2,128)}, u32[]{:S(2)}, u32[]{:S(2)}) async-start(f32[8,2,128]{2,1,0:T(2,128)} %bitcast.4), calls=%async_computation | async-start | bytes 16384 | tf_op jit(solution)/shard_map/all_to_all | solution.py:138
  19.4 2.0 convolution_convert_fusion.9
  21.4 1.5 collective-permute-start.2
  22.8 2.0 convolution_convert_fusion.6
  24.8 1.8 constant_dynamic-update-slice_fusion.11
  28.7 5.6 %dynamic-slice_bitcast_fusion.2 = (bf16[1792,512]{1,0:T(8,128)(2,1)}, bf16[1792,512]{1,0:T(8,128)(2,1)S(1)}, bf16[1792,512]{1,0:T(8,128)(2,1)S(1)}, bf16[1792,512]{1,0:T(8,128)(2,1)}) fusion(bf16[1,3584,512]{2,1,0:T(8,128)(2,1)} %param.14, s32[]{:T(128)S(6)} %select_n.103, s32[]{:T(128)S(6)} %select_n.104, bf16[1,3584,512]{2,1,0:T(8,128)(2,1)} %param.13), kind=kLoop, calls=%fused_computation.35 | loop fusion | bytes 14680072 | tf_op jit(solution)/shard_map/dynamic_slice | solution.py:157
  34.3 2.4 %pad_maximum_fusion.2 = bf16[1792,1024]{1,0:T(8,128)(2,1)} fusion(bf16[1792,512]{1,0:T(8,128)(2,1)S(1)} %get-tuple-element.24, bf16[1792,512]{1,0:T(8,128)(2,1)S(1)} %get-tuple-element.40), kind=kLoop, calls=%fused_computation.4 | loop fusion | flops 7340032 | bytes 7340032 | tf_op jit(solution)/shard_map/concatenate | solution.py:159
  37.3 2.0 gather_fusion.1
  39.2 2.0 gather_fusion
  52.7 3.3 %collective-permute-start.10 = (bf16[96,1792]{1,0:T(8,128)(2,1)S(1)}, bf16[96,1792]{1,0:T(8,128)(2,1)S(1)}, u32[]{:S(2)}, u32[]{:S(2)}) collective-permute-start(bf16[96,1792]{1,0:T(8,128)(2,1)S(1)} %convolution_convert_fusion.4), channel_id=1, source_target_pairs={{0,2},{2,0},{4,6},{6,4},{8,10},{10,8},{1,3},{3,1},{5,7},{7,5},{9,1... | collective-permute-start | bytes 1032200 | tf_op jit(solution)/shard_map/ppermute | solution.py:94
  56.3 2.5 %collective-permute-start.9 = (bf16[96,1792]{1,0:T(8,128)(2,1)S(1)}, bf16[96,1792]{1,0:T(8,128)(2,1)S(1)}, u32[]{:S(2)}, u32[]{:S(2)}) collective-permute-start(bf16[96,1792]{1,0:T(8,128)(2,1)S(1)} %convolution_convert_fusion.5), channel_id=1, source_target_pairs={{4,6},{6,4},{8,10},{10,8},{12,14},{14,12},{5,7},{7,5},{9,11},{11,9... | collective-permute-start | bytes 1032200 | tf_op jit(solution)/shard_map/ppermute | solution.py:94
  61.3 3.3 %collective-permute-start.4 = (bf16[96,1792]{1,0:T(8,128)(2,1)S(1)}, bf16[96,1792]{1,0:T(8,128)(2,1)S(1)}, u32[]{:S(2)}, u32[]{:S(2)}) collective-permute-start(bf16[96,1792]{1,0:T(8,128)(2,1)S(1)} %convolution_convert_fusion.7), channel_id=1, source_target_pairs={{0,2},{2,0},{4,6},{6,4},{8,10},{10,8},{1,3},{3,1},{5,7},{7,5},{9,1... | collective-permute-start | bytes 1032200 | tf_op jit(solution)/shard_map/ppermute | solution.py:94
  64.7 2.5 %collective-permute-start.3 = (bf16[96,1792]{1,0:T(8,128)(2,1)S(1)}, bf16[96,1792]{1,0:T(8,128)(2,1)S(1)}, u32[]{:S(2)}, u32[]{:S(2)}) collective-permute-start(bf16[96,1792]{1,0:T(8,128)(2,1)S(1)} %convolution_convert_fusion.8), channel_id=1, source_target_pairs={{4,6},{6,4},{8,10},{10,8},{12,14},{14,12},{5,7},{7,5},{9,11},{11,9... | collective-permute-start | bytes 1032200 | tf_op jit(solution)/shard_map/ppermute | solution.py:94
  67.2 5.6 %collective-permute-done.9 = bf16[96,1792]{1,0:T(8,128)(2,1)S(1)} collective-permute-done((bf16[96,1792]{1,0:T(8,128)(2,1)S(1)}, bf16[96,1792]{1,0:T(8,128)(2,1)S(1)}, u32[]{:S(2)}, u32[]{:S(2)}) %collective-permute-start.9) | collective-permute-done | bytes 344096 | tf_op jit(solution)/shard_map/ppermute | solution.py:94
  72.8 1.9 collective-permute-start.24
  74.8 12.4 %collective-permute-done.3 = bf16[96,1792]{1,0:T(8,128)(2,1)S(1)} collective-permute-done((bf16[96,1792]{1,0:T(8,128)(2,1)S(1)}, bf16[96,1792]{1,0:T(8,128)(2,1)S(1)}, u32[]{:S(2)}, u32[]{:S(2)}) %collective-permute-start.3) | collective-permute-done | bytes 344096 | tf_op jit(solution)/shard_map/ppermute | solution.py:94
  87.2 3.4 %collective-permute-start.23 = (bf16[128,1792]{1,0:T(8,128)(2,1)}, bf16[128,1792]{1,0:T(8,128)(2,1)S(1)}, u32[]{:S(2)}, u32[]{:S(2)}) collective-permute-start(bf16[128,1792]{1,0:T(8,128)(2,1)} %collective-permute-done.6), channel_id=1, source_target_pairs={{4,8},{6,10},{8,12},{10,14},{5,9},{7,11},{9,13},{11,15},{20,24},{2... | collective-permute-start | bytes 1376264 | tf_op jit(solution)/shard_map/ppermute | solution.py:94
  90.6 1.9 collective-permute-start.20
  92.6 4.0 %collective-permute-start.19 = (bf16[128,1792]{1,0:T(8,128)(2,1)S(1)}, bf16[128,1792]{1,0:T(8,128)(2,1)S(1)}, u32[]{:S(2)}, u32[]{:S(2)}) collective-permute-start(bf16[128,1792]{1,0:T(8,128)(2,1)S(1)} %collective-permute-done), channel_id=1, source_target_pairs={{4,8},{6,10},{8,12},{10,14},{5,9},{7,11},{9,13},{11,15},{20,24},{2... | collective-permute-start | bytes 1376264 | tf_op jit(solution)/shard_map/ppermute | solution.py:94
  96.6 5.2 %collective-permute-done.23 = bf16[128,1792]{1,0:T(8,128)(2,1)S(1)} collective-permute-done((bf16[128,1792]{1,0:T(8,128)(2,1)}, bf16[128,1792]{1,0:T(8,128)(2,1)S(1)}, u32[]{:S(2)}, u32[]{:S(2)}) %collective-permute-start.23) | collective-permute-done | bytes 458784 | tf_op jit(solution)/shard_map/ppermute | solution.py:94
  102.1 2.3 %collective-permute-done.20 = bf16[128,1792]{1,0:T(8,128)(2,1)S(1)} collective-permute-done((bf16[128,1792]{1,0:T(8,128)(2,1)S(1)}, bf16[128,1792]{1,0:T(8,128)(2,1)S(1)}, u32[]{:S(2)}, u32[]{:S(2)}) %collective-permute-start.20) | collective-permute-done | bytes 458784 | tf_op jit(solution)/shard_map/ppermute | solution.py:94
  104.4 1.4 collective-permute-start.25
  105.8 4.5 %collective-permute-done.19 = bf16[128,1792]{1,0:T(8,128)(2,1)S(1)} collective-permute-done((bf16[128,1792]{1,0:T(8,128)(2,1)S(1)}, bf16[128,1792]{1,0:T(8,128)(2,1)S(1)}, u32[]{:S(2)}, u32[]{:S(2)}) %collective-permute-start.19) | collective-permute-done | bytes 458784 | tf_op jit(solution)/shard_map/ppermute | solution.py:94
  110.5 1.4 collective-permute-start.21
  113.6 4.0 %collective-permute-start.30 = (bf16[128,1792]{1,0:T(8,128)(2,1)S(1)}, bf16[128,1792]{1,0:T(8,128)(2,1)S(1)}, u32[]{:S(2)}, u32[]{:S(2)}) collective-permute-start(bf16[128,1792]{1,0:T(8,128)(2,1)S(1)} %broadcast_select_fusion.1), channel_id=1, source_target_pairs={{8,12},{10,14},{4,0},{6,2},{9,13},{11,15},{5,1},{7,3},{24,28},{26,... | collective-permute-start | bytes 1376264 | tf_op jit(solution)/shard_map/ppermute | solution.py:94
  117.7 2.6 %collective-permute-done.21 = bf16[96,1792]{1,0:T(8,128)(2,1)S(1)} collective-permute-done((bf16[96,1792]{1,0:T(8,128)(2,1)S(1)}, bf16[96,1792]{1,0:T(8,128)(2,1)S(1)}, u32[]{:S(2)}, u32[]{:S(2)}) %collective-permute-start.21) | collective-permute-done | bytes 344096 | tf_op jit(solution)/shard_map/ppermute | solution.py:94
  120.3 4.0 %collective-permute-done.33 = bf16[128,1792]{1,0:T(8,128)(2,1)S(1)} collective-permute-done((bf16[128,1792]{1,0:T(8,128)(2,1)S(1)}, bf16[128,1792]{1,0:T(8,128)(2,1)S(1)}, u32[]{:S(2)}, u32[]{:S(2)}) %collective-permute-start.33) | collective-permute-done | bytes 458784 | tf_op jit(solution)/shard_map/ppermute | solution.py:94
  125.2 6.7 %collective-permute-done.30 = bf16[128,1792]{1,0:T(8,128)(2,1)S(1)} collective-permute-done((bf16[128,1792]{1,0:T(8,128)(2,1)S(1)}, bf16[128,1792]{1,0:T(8,128)(2,1)S(1)}, u32[]{:S(2)}, u32[]{:S(2)}) %collective-permute-start.30) | collective-permute-done | bytes 458784 | tf_op jit(solution)/shard_map/ppermute | solution.py:94
  136.9 2.1 collective-permute-done.22
  144.7 1.4 fusion.10
  146.1 2.6 %fusion.115 = f32[672,1024]{1,0:T(8,128)S(1)} fusion(bf16[672,1792]{1,0:T(8,128)(2,1)S(1)} %collective-permute-done.11, bf16[1792,512]{1,0:T(8,128)(2,1)S(1)} %get-tuple-element.24, bf16[1792,512]{1,0:T(8,128)(2,1)S(1)} %copy-done.1), kind=kOutput, calls=%fused_computation.201 | convolution fusion | flops 2473590784 | bytes 8830976 | tf_op jit(solution)/shard_map/dot_general | solution.py:166
  148.8 2.7 %convolution_add_fusion = f32[672,1024]{1,0:T(8,128)S(1)} fusion(f32[672,1024]{1,0:T(8,128)S(1)} %fusion.115, bf16[672,1792]{1,0:T(8,128)(2,1)S(1)} %constant_dynamic-update-slice_fusion.6, bf16[1792,512]{1,0:T(8,128)(2,1)S(1)} %copy-done.4, bf16[1792,512]{1,0:T(8,128)(2,1)S(1)} %copy-done.5), kind=kOutput, calls=%fused_computation.37 | convolution fusion | flops 2474278912 | bytes 11583488 | tf_op jit(solution)/shard_map/dot_general | solution.py:166
  151.4 1.9 fusion.26
  154.3 2.4 %fusion.52 = f32[224,1792]{1,0:T(8,128)S(1)} fusion(bf16[224,1024]{1,0:T(8,128)(2,1)S(1)} %collective-permute-done.27, bf16[224,512]{1,0:T(8,128)(2,1)S(1)} %get-tuple-element.29, bf16[224,512]{1,0:T(8,128)(2,1)S(1)} %get-tuple-element.28, bf16[1792,1024]{1,0:T(8,128)(2,1)S(1)} %collective-permute-done.13, bf16[1792,512]{1,0:T(8,128)(2,1)S(1)} %copy-done.4, ...), kind=kOutput, calls=%fused_computation.77 | convolution fusion | flops 1668939776 | bytes 9863168 | tf_op jit(solution)/shard_map/dot_general | solution.py:169
  157.5 2.6 %fusion.58 = f32[224,1792]{1,0:T(8,128)S(1)} fusion(bf16[224,1024]{1,0:T(8,128)(2,1)S(1)} %collective-permute-done.36, bf16[224,512]{1,0:T(8,128)(2,1)S(1)} %get-tuple-element.31, bf16[224,512]{1,0:T(8,128)(2,1)S(1)} %get-tuple-element.30, bf16[1792,1024]{1,0:T(8,128)(2,1)S(1)} %collective-permute-done.13, bf16[1792,512]{1,0:T(8,128)(2,1)S(1)} %copy-done.4, ...), kind=kOutput, calls=%fused_computation.83 | convolution fusion | flops 1668939776 | bytes 9863168 | tf_op jit(solution)/shard_map/dot_general | solution.py:169
  160.8 7.2 %fusion.118 = (bf16[672,1792]{1,0:T(8,128)(2,1)S(1)}, f32[672,1792]{1,0:T(8,128)S(1)}) fusion(bf16[1792,1024]{1,0:T(8,128)(2,1)} %copy-done.11, bf16[1792,512]{1,0:T(8,128)(2,1)S(1)} %copy-done.4, bf16[1792,512]{1,0:T(8,128)(2,1)S(1)} %copy-done.5, bf16[672,1024]{1,0:T(8,128)(2,1)S(1)} %collective-permute-done.12, ...), kind=kOutput, calls=%fused_computation.203 | convolution fusion | flops 4963983360 | bytes 17317888 | tf_op jit(solution)/shard_map/dot_general | solution.py:169
  168.2 3.3 %collective-permute-start.15 = (bf16[96,1792]{1,0:T(8,128)(2,1)S(1)}, bf16[96,1792]{1,0:T(8,128)(2,1)S(1)}, u32[]{:S(2)}, u32[]{:S(2)}) collective-permute-start(bf16[96,1792]{1,0:T(8,128)(2,1)S(1)} %get-tuple-element.27), channel_id=1, source_target_pairs={{4,6},{6,4},{8,10},{10,8},{12,14},{14,12},{5,7},{7,5},{9,11},{11,9... | collective-permute-start | bytes 1032200 | tf_op jit(solution)/shard_map/ppermute | solution.py:94
  171.8 14.4 %collective-permute-start.29 = (bf16[128,1792]{1,0:T(8,128)(2,1)S(1)}, bf16[128,1792]{1,0:T(8,128)(2,1)S(1)}, u32[]{:S(2)}, u32[]{:S(2)}) collective-permute-start(bf16[128,1792]{1,0:T(8,128)(2,1)S(1)} %fusion.43), channel_id=1, source_target_pairs={{0,8},{2,10},{4,12},{6,14},{8,0},{10,2},{12,4},{14,6},{1,9},{3,11}... | collective-permute-start | bytes 1376264 | tf_op jit(solution)/shard_map/ppermute | solution.py:94
  186.2 3.4 %collective-permute-start.17 = (bf16[96,1792]{1,0:T(8,128)(2,1)S(1)}, bf16[96,1792]{1,0:T(8,128)(2,1)S(1)}, u32[]{:S(2)}, u32[]{:S(2)}) collective-permute-start(bf16[96,1792]{1,0:T(8,128)(2,1)S(1)} %get-tuple-element.26), channel_id=1, source_target_pairs={{0,2},{2,0},{4,6},{6,4},{8,10},{10,8},{1,3},{3,1},{5,7},{7,5},{9,1... | collective-permute-start | bytes 1032200 | tf_op jit(solution)/shard_map/ppermute | solution.py:94
  191.0 1.9 collective-permute-start.16
  193.0 4.5 %collective-permute-done.17 = bf16[96,1792]{1,0:T(8,128)(2,1)S(1)} collective-permute-done((bf16[96,1792]{1,0:T(8,128)(2,1)S(1)}, bf16[96,1792]{1,0:T(8,128)(2,1)S(1)}, u32[]{:S(2)}, u32[]{:S(2)}) %collective-permute-start.17) | collective-permute-done | bytes 344096 | tf_op jit(solution)/shard_map/ppermute | solution.py:94
  197.8 1.9 collective-permute-start.18
  200.8 9.5 %collective-permute-done.29 = bf16[128,1792]{1,0:T(8,128)(2,1)S(1)} collective-permute-done((bf16[128,1792]{1,0:T(8,128)(2,1)S(1)}, bf16[128,1792]{1,0:T(8,128)(2,1)S(1)}, u32[]{:S(2)}, u32[]{:S(2)}) %collective-permute-start.29) | collective-permute-done | bytes 458784 | tf_op jit(solution)/shard_map/ppermute | solution.py:94
  210.4 11.9 %collective-permute-done.16 = bf16[128,1792]{1,0:T(8,128)(2,1)S(1)} collective-permute-done((bf16[128,1792]{1,0:T(8,128)(2,1)S(1)}, bf16[128,1792]{1,0:T(8,128)(2,1)S(1)}, u32[]{:S(2)}, u32[]{:S(2)}) %collective-permute-start.16) | collective-permute-done | bytes 458784 | tf_op jit(solution)/shard_map/ppermute | solution.py:94
  (139 shorter events, 39.0 us)
Async XLA Ops:
  0.0 26.6 %copy-start.2 = (bf16[128,1792]{1,0:T(8,128)(2,1)S(1)}, bf16[128,1792]{1,0:T(8,128)(2,1)}, u32[]{:S(2)}) copy-start(bf16[128,1792]{1,0:T(8,128)(2,1)} %param.10) | copy-start | bytes 1376260
  0.0 49.4 %collective-permute-start.7 = (bf16[128,1792]{1,0:T(8,128)(2,1)}, bf16[128,1792]{1,0:T(8,128)(2,1)}, u32[]{:S(2)}, u32[]{:S(2)}) collective-permute-start(bf16[128,1792]{1,0:T(8,128)(2,1)} %param.9), channel_id=1, source_target_pairs={{4,0},{6,2},{8,4},{10,6},{12,8},{14,10},{5,1},{7,3},{9,5},{11,7},{... | collective-permute-start | bytes 1376264 | tf_op jit(solution)/shard_map/ppermute | solution.py:94
  2.1 49.3 %collective-permute-start.6 = (bf16[128,1792]{1,0:T(8,128)(2,1)}, bf16[128,1792]{1,0:T(8,128)(2,1)}, u32[]{:S(2)}, u32[]{:S(2)}) collective-permute-start(bf16[128,1792]{1,0:T(8,128)(2,1)} %param.9), channel_id=1, source_target_pairs={{0,4},{2,6},{4,8},{6,10},{8,12},{10,14},{1,5},{3,7},{5,9},{7,11},{... | collective-permute-start | bytes 1376264 | tf_op jit(solution)/shard_map/ppermute | solution.py:94
  6.0 46.7 %collective-permute-start.1 = (bf16[128,1792]{1,0:T(8,128)(2,1)}, bf16[128,1792]{1,0:T(8,128)(2,1)S(1)}, u32[]{:S(2)}, u32[]{:S(2)}) collective-permute-start(bf16[128,1792]{1,0:T(8,128)(2,1)} %param.10), channel_id=1, source_target_pairs={{4,0},{6,2},{8,4},{10,6},{12,8},{14,10},{5,1},{7,3},{9,5},{11,7},{... | collective-permute-start | bytes 1376264 | tf_op jit(solution)/shard_map/ppermute | solution.py:94
  8.7 47.6 %collective-permute-start = (bf16[128,1792]{1,0:T(8,128)(2,1)}, bf16[128,1792]{1,0:T(8,128)(2,1)S(1)}, u32[]{:S(2)}, u32[]{:S(2)}) collective-permute-start(bf16[128,1792]{1,0:T(8,128)(2,1)} %param.10), channel_id=1, source_target_pairs={{0,4},{2,6},{4,8},{6,10},{8,12},{10,14},{1,5},{3,7},{5,9},{7,11},{... | collective-permute-start | bytes 1376264 | tf_op jit(solution)/shard_map/ppermute | solution.py:94
  13.5 23.8 %all-to-all-start = ((f32[8,2,128]{2,1,0:T(2,128)}), f32[8,2,128]{2,1,0:T(2,128)}, u32[]{:S(2)}, u32[]{:S(2)}) async-start(f32[8,2,128]{2,1,0:T(2,128)} %bitcast.4), calls=%async_computation | async-start | bytes 16384 | tf_op jit(solution)/shard_map/all_to_all | solution.py:138
  19.4 9.3 %copy-start.8 = (f32[128]{0:T(128)}, f32[128]{0:T(128)S(1)}, u32[]{:S(2)}) copy-start(f32[128]{0:T(128)S(1)} %fusion.41) | copy-start | bytes 1540
  21.4 43.3 %collective-permute-start.2 = (bf16[96,1792]{1,0:T(8,128)(2,1)}, bf16[96,1792]{1,0:T(8,128)(2,1)S(1)}, u32[]{:S(2)}, u32[]{:S(2)}) collective-permute-start(bf16[96,1792]{1,0:T(8,128)(2,1)} %convolution_convert_fusion.9), channel_id=1, source_target_pairs={{0,2},{2,0},{4,6},{6,4},{8,10},{10,8},{12,14},{14,12},{1,3},{3,1},... | collective-permute-start | bytes 1032200 | tf_op jit(solution)/shard_map/ppermute | solution.py:94
  46.3 12.8 %copy-start.7 = (bf16[672,1792]{1,0:T(8,128)(2,1)S(1)}, bf16[672,1792]{1,0:T(8,128)(2,1)}, u32[]{:S(2)}) copy-start(bf16[672,1792]{1,0:T(8,128)(2,1)} %constant_dynamic-update-slice_fusion.11) | copy-start | bytes 7225348
  49.4 11.9 %copy-start.6 = (bf16[672,1792]{1,0:T(8,128)(2,1)S(1)}, bf16[672,1792]{1,0:T(8,128)(2,1)}, u32[]{:S(2)}) copy-start(bf16[672,1792]{1,0:T(8,128)(2,1)} %constant_dynamic-update-slice_fusion.5) | copy-start | bytes 7225348
  49.4 11.9 %collective-permute-start.8 = (bf16[96,1792]{1,0:T(8,128)(2,1)}, bf16[96,1792]{1,0:T(8,128)(2,1)S(1)}, u32[]{:S(2)}, u32[]{:S(2)}) collective-permute-start(bf16[96,1792]{1,0:T(8,128)(2,1)} %convolution_convert_fusion.6), channel_id=1, source_target_pairs={{0,2},{2,0},{4,6},{6,4},{8,10},{10,8},{12,14},{14,12},{1,3},{3,1},... | collective-permute-start | bytes 1032200 | tf_op jit(solution)/shard_map/ppermute | solution.py:94
  51.4 102.9 %collective-permute-start.13 = (bf16[1792,1024]{1,0:T(8,128)(2,1)}, bf16[1792,1024]{1,0:T(8,128)(2,1)S(1)}, u32[]{:S(2)}, u32[]{:S(2)}) collective-permute-start(bf16[1792,1024]{1,0:T(8,128)(2,1)} %pad_maximum_fusion.2), channel_id=1, source_target_pairs={{0,1},{1,0},{2,3},{3,2},{4,5},{5,4},{6,7},{7,6},{8,9},{9,8},{10,11... | collective-permute-start | bytes 11010056 | tf_op jit(solution)/shard_map/ppermute | solution.py:98
  52.7 59.3 %collective-permute-start.10 = (bf16[96,1792]{1,0:T(8,128)(2,1)S(1)}, bf16[96,1792]{1,0:T(8,128)(2,1)S(1)}, u32[]{:S(2)}, u32[]{:S(2)}) collective-permute-start(bf16[96,1792]{1,0:T(8,128)(2,1)S(1)} %convolution_convert_fusion.4), channel_id=1, source_target_pairs={{0,2},{2,0},{4,6},{6,4},{8,10},{10,8},{1,3},{3,1},{5,7},{7,5},{9,1... | collective-permute-start | bytes 1032200 | tf_op jit(solution)/shard_map/ppermute | solution.py:94
  56.3 16.6 %collective-permute-start.9 = (bf16[96,1792]{1,0:T(8,128)(2,1)S(1)}, bf16[96,1792]{1,0:T(8,128)(2,1)S(1)}, u32[]{:S(2)}, u32[]{:S(2)}) collective-permute-start(bf16[96,1792]{1,0:T(8,128)(2,1)S(1)} %convolution_convert_fusion.5), channel_id=1, source_target_pairs={{4,6},{6,4},{8,10},{10,8},{12,14},{14,12},{5,7},{7,5},{9,11},{11,9... | collective-permute-start | bytes 1032200 | tf_op jit(solution)/shard_map/ppermute | solution.py:94
  61.3 29.3 %collective-permute-start.4 = (bf16[96,1792]{1,0:T(8,128)(2,1)S(1)}, bf16[96,1792]{1,0:T(8,128)(2,1)S(1)}, u32[]{:S(2)}, u32[]{:S(2)}) collective-permute-start(bf16[96,1792]{1,0:T(8,128)(2,1)S(1)} %convolution_convert_fusion.7), channel_id=1, source_target_pairs={{0,2},{2,0},{4,6},{6,4},{8,10},{10,8},{1,3},{3,1},{5,7},{7,5},{9,1... | collective-permute-start | bytes 1032200 | tf_op jit(solution)/shard_map/ppermute | solution.py:94
  64.7 22.5 %collective-permute-start.3 = (bf16[96,1792]{1,0:T(8,128)(2,1)S(1)}, bf16[96,1792]{1,0:T(8,128)(2,1)S(1)}, u32[]{:S(2)}, u32[]{:S(2)}) collective-permute-start(bf16[96,1792]{1,0:T(8,128)(2,1)S(1)} %convolution_convert_fusion.8), channel_id=1, source_target_pairs={{4,6},{6,4},{8,10},{10,8},{12,14},{14,12},{5,7},{7,5},{9,11},{11,9... | collective-permute-start | bytes 1032200 | tf_op jit(solution)/shard_map/ppermute | solution.py:94
  72.8 19.8 %collective-permute-start.24 = (bf16[128,1792]{1,0:T(8,128)(2,1)}, bf16[128,1792]{1,0:T(8,128)(2,1)S(1)}, u32[]{:S(2)}, u32[]{:S(2)}) collective-permute-start(bf16[128,1792]{1,0:T(8,128)(2,1)} %collective-permute-done.7), channel_id=1, source_target_pairs={{8,4},{10,6},{4,0},{6,2},{9,5},{11,7},{5,1},{7,3},{24,20},{26,22},... | collective-permute-start | bytes 1376264 | tf_op jit(solution)/shard_map/ppermute | solution.py:94
  87.2 14.6 %collective-permute-start.23 = (bf16[128,1792]{1,0:T(8,128)(2,1)}, bf16[128,1792]{1,0:T(8,128)(2,1)S(1)}, u32[]{:S(2)}, u32[]{:S(2)}) collective-permute-start(bf16[128,1792]{1,0:T(8,128)(2,1)} %collective-permute-done.6), channel_id=1, source_target_pairs={{4,8},{6,10},{8,12},{10,14},{5,9},{7,11},{9,13},{11,15},{20,24},{2... | collective-permute-start | bytes 1376264 | tf_op jit(solution)/shard_map/ppermute | solution.py:94
  90.6 13.8 %collective-permute-start.20 = (bf16[128,1792]{1,0:T(8,128)(2,1)S(1)}, bf16[128,1792]{1,0:T(8,128)(2,1)S(1)}, u32[]{:S(2)}, u32[]{:S(2)}) collective-permute-start(bf16[128,1792]{1,0:T(8,128)(2,1)S(1)} %collective-permute-done.1), channel_id=1, source_target_pairs={{8,4},{10,6},{4,0},{6,2},{9,5},{11,7},{5,1},{7,3},{24,20},{26,22},... | collective-permute-start | bytes 1376264 | tf_op jit(solution)/shard_map/ppermute | solution.py:94
  92.6 17.6 %collective-permute-start.19 = (bf16[128,1792]{1,0:T(8,128)(2,1)S(1)}, bf16[128,1792]{1,0:T(8,128)(2,1)S(1)}, u32[]{:S(2)}, u32[]{:S(2)}) collective-permute-start(bf16[128,1792]{1,0:T(8,128)(2,1)S(1)} %collective-permute-done), channel_id=1, source_target_pairs={{4,8},{6,10},{8,12},{10,14},{5,9},{7,11},{9,13},{11,15},{20,24},{2... | collective-permute-start | bytes 1376264 | tf_op jit(solution)/shard_map/ppermute | solution.py:94
  101.8 42.9 %collective-permute-start.5 = (bf16[672,1792]{1,0:T(8,128)(2,1)S(1)}, bf16[672,1792]{1,0:T(8,128)(2,1)S(1)}, u32[]{:S(2)}, u32[]{:S(2)}) collective-permute-start(bf16[672,1792]{1,0:T(8,128)(2,1)S(1)} %constant_dynamic-update-slice_fusion), channel_id=1, source_target_pairs={{0,1},{1,0},{2,3},{3,2},{4,5},{5,4},{6,7},{7,6},{8,9},{9,8},{10,11... | collective-permute-start | bytes 7225352 | tf_op jit(solution)/shard_map/ppermute | solution.py:98
  104.4 9.2 %collective-permute-start.25 = (bf16[96,1792]{1,0:T(8,128)(2,1)S(1)}, bf16[96,1792]{1,0:T(8,128)(2,1)S(1)}, u32[]{:S(2)}, u32[]{:S(2)}) collective-permute-start(bf16[96,1792]{1,0:T(8,128)(2,1)S(1)} %convolution_convert_fusion.2), channel_id=1, source_target_pairs={{0,2},{2,0},{4,6},{6,4},{8,10},{10,8},{12,14},{14,12},{1,3},{3,1},... | collective-permute-start | bytes 1032200 | tf_op jit(solution)/shard_map/ppermute | solution.py:94
  110.5 9.7 %collective-permute-start.21 = (bf16[96,1792]{1,0:T(8,128)(2,1)S(1)}, bf16[96,1792]{1,0:T(8,128)(2,1)S(1)}, u32[]{:S(2)}, u32[]{:S(2)}) collective-permute-start(bf16[96,1792]{1,0:T(8,128)(2,1)S(1)} %convolution_convert_fusion.3), channel_id=1, source_target_pairs={{0,2},{2,0},{4,6},{6,4},{8,10},{10,8},{12,14},{14,12},{1,3},{3,1},... | collective-permute-start | bytes 1032200 | tf_op jit(solution)/shard_map/ppermute | solution.py:94
  112.0 12.3 %collective-permute-start.33 = (bf16[128,1792]{1,0:T(8,128)(2,1)S(1)}, bf16[128,1792]{1,0:T(8,128)(2,1)S(1)}, u32[]{:S(2)}, u32[]{:S(2)}) collective-permute-start(bf16[128,1792]{1,0:T(8,128)(2,1)S(1)} %broadcast_select_fusion), channel_id=1, source_target_pairs={{8,12},{10,14},{4,0},{6,2},{9,13},{11,15},{5,1},{7,3},{24,28},{26,... | collective-permute-start | bytes 1376264 | tf_op jit(solution)/shard_map/ppermute | solution.py:94
  113.6 18.3 %collective-permute-start.30 = (bf16[128,1792]{1,0:T(8,128)(2,1)S(1)}, bf16[128,1792]{1,0:T(8,128)(2,1)S(1)}, u32[]{:S(2)}, u32[]{:S(2)}) collective-permute-start(bf16[128,1792]{1,0:T(8,128)(2,1)S(1)} %broadcast_select_fusion.1), channel_id=1, source_target_pairs={{8,12},{10,14},{4,0},{6,2},{9,13},{11,15},{5,1},{7,3},{24,28},{26,... | collective-permute-start | bytes 1376264 | tf_op jit(solution)/shard_map/ppermute | solution.py:94
  120.2 13.6 %collective-permute-start.26 = (bf16[224,1792]{1,0:T(8,128)(2,1)S(1)}, bf16[224,1792]{1,0:T(8,128)(2,1)S(1)}, u32[]{:S(2)}, u32[]{:S(2)}) collective-permute-start(bf16[224,1792]{1,0:T(8,128)(2,1)S(1)} %pad_maximum_fusion.8), channel_id=1, source_target_pairs={{0,1},{1,0},{2,3},{3,2},{4,5},{5,4},{6,7},{7,6},{8,9},{9,8},{10,11... | collective-permute-start | bytes 2408456 | tf_op jit(solution)/shard_map/ppermute | solution.py:98
  120.3 13.6 %copy-start.1 = (bf16[1792,512]{1,0:T(8,128)(2,1)S(1)}, bf16[1792,512]{1,0:T(8,128)(2,1)}, u32[]{:S(2)}) copy-start(bf16[1792,512]{1,0:T(8,128)(2,1)} %copy-done) | copy-start | bytes 5505028
  124.5 8.6 %collective-permute-start.34 = (bf16[96,1792]{1,0:T(8,128)(2,1)S(1)}, bf16[96,1792]{1,0:T(8,128)(2,1)S(1)}, u32[]{:S(2)}, u32[]{:S(2)}) collective-permute-start(bf16[96,1792]{1,0:T(8,128)(2,1)S(1)} %convolution_convert_fusion), channel_id=1, source_target_pairs={{0,2},{2,0},{12,14},{14,12},{1,3},{3,1},{13,15},{15,13},{16,18},{1... | collective-permute-start | bytes 1032200 | tf_op jit(solution)/shard_map/ppermute | solution.py:94
  132.2 1.1 collective-permute-start.31
  133.1 13.0 %collective-permute-start.11 = (bf16[672,1792]{1,0:T(8,128)(2,1)S(1)}, bf16[672,1792]{1,0:T(8,128)(2,1)S(1)}, u32[]{:S(2)}, u32[]{:S(2)}) collective-permute-start(bf16[672,1792]{1,0:T(8,128)(2,1)S(1)} %constant_dynamic-update-slice_fusion.6), channel_id=1, source_target_pairs={{0,1},{1,0},{2,3},{3,2},{4,5},{5,4},{6,7},{7,6},{8,9},{9,8},{10,11... | collective-permute-start | bytes 7225352 | tf_op jit(solution)/shard_map/ppermute | solution.py:98
  133.2 5.7 %collective-permute-start.22 = (bf16[224,1792]{1,0:T(8,128)(2,1)S(1)}, bf16[224,1792]{1,0:T(8,128)(2,1)S(1)}, u32[]{:S(2)}, u32[]{:S(2)}) collective-permute-start(bf16[224,1792]{1,0:T(8,128)(2,1)S(1)} %pad_maximum_fusion.7), channel_id=1, source_target_pairs={{0,1},{1,0},{2,3},{3,2},{4,5},{5,4},{6,7},{7,6},{8,9},{9,8},{10,11... | collective-permute-start | bytes 2408456 | tf_op jit(solution)/shard_map/ppermute | solution.py:98
  133.9 6.8 %collective-permute-start.32 = (bf16[224,1792]{1,0:T(8,128)(2,1)S(1)}, bf16[224,1792]{1,0:T(8,128)(2,1)S(1)}, u32[]{:S(2)}, u32[]{:S(2)}) collective-permute-start(bf16[224,1792]{1,0:T(8,128)(2,1)S(1)} %constant_dynamic-update-slice_fusion.12), channel_id=1, source_target_pairs={{0,1},{1,0},{2,3},{3,2},{4,5},{5,4},{6,7},{7,6},{8,9},{9,8},{10,11... | collective-permute-start | bytes 2408456 | tf_op jit(solution)/shard_map/ppermute | solution.py:98
  135.9 3.2 %copy-start.3 = (bf16[1,512,3584]{2,1,0:T(8,128)(2,1)S(1)}, bf16[1,512,3584]{2,1,0:T(8,128)(2,1)}, u32[]{:S(2)}) copy-start(bf16[1,512,3584]{2,1,0:T(8,128)(2,1)} %param.15) | copy-start | bytes 11010052
  138.9 2.9 %collective-permute-start.35 = (bf16[224,1792]{1,0:T(8,128)(2,1)S(1)}, bf16[224,1792]{1,0:T(8,128)(2,1)S(1)}, u32[]{:S(2)}, u32[]{:S(2)}) collective-permute-start(bf16[224,1792]{1,0:T(8,128)(2,1)S(1)} %constant_dynamic-update-slice_fusion.14), channel_id=1, source_target_pairs={{0,1},{1,0},{2,3},{3,2},{4,5},{5,4},{6,7},{7,6},{8,9},{9,8},{10,11... | collective-permute-start | bytes 2408456 | tf_op jit(solution)/shard_map/ppermute | solution.py:98
  140.7 13.6 %collective-permute-start.27 = (bf16[224,1024]{1,0:T(8,128)(2,1)S(1)}, bf16[224,1024]{1,0:T(8,128)(2,1)S(1)}, u32[]{:S(2)}, u32[]{:S(2)}) collective-permute-start(bf16[224,1024]{1,0:T(8,128)(2,1)S(1)} %pad_maximum_fusion.9), channel_id=1, source_target_pairs={{0,1},{1,0},{2,3},{3,2},{4,5},{5,4},{6,7},{7,6},{8,9},{9,8},{10,11... | collective-permute-start | bytes 1376264 | tf_op jit(solution)/shard_map/ppermute | solution.py:98
  153.6 7.2 %collective-permute-start.12 = (bf16[672,1024]{1,0:T(8,128)(2,1)S(1)}, bf16[672,1024]{1,0:T(8,128)(2,1)S(1)}, u32[]{:S(2)}, u32[]{:S(2)}) collective-permute-start(bf16[672,1024]{1,0:T(8,128)(2,1)S(1)} %pad_maximum_fusion.3), channel_id=1, source_target_pairs={{0,1},{1,0},{2,3},{3,2},{4,5},{5,4},{6,7},{7,6},{8,9},{9,8},{10,11... | collective-permute-start | bytes 4128776 | tf_op jit(solution)/shard_map/ppermute | solution.py:98
  153.9 3.6 %collective-permute-start.36 = (bf16[224,1024]{1,0:T(8,128)(2,1)S(1)}, bf16[224,1024]{1,0:T(8,128)(2,1)S(1)}, u32[]{:S(2)}, u32[]{:S(2)}) collective-permute-start(bf16[224,1024]{1,0:T(8,128)(2,1)S(1)} %pad_maximum_fusion.10), channel_id=1, source_target_pairs={{0,1},{1,0},{2,3},{3,2},{4,5},{5,4},{6,7},{7,6},{8,9},{9,8},{10,11... | collective-permute-start | bytes 1376264 | tf_op jit(solution)/shard_map/ppermute | solution.py:98
  154.3 3.2 %copy-start.11 = (bf16[1792,1024]{1,0:T(8,128)(2,1)}, bf16[1792,1024]{1,0:T(8,128)(2,1)S(1)}, u32[]{:S(2)}) copy-start(bf16[1792,1024]{1,0:T(8,128)(2,1)S(1)} %collective-permute-done.13) | copy-start | bytes 11010052
  156.7 14.7 %collective-permute-start.28 = (bf16[96,1792]{1,0:T(8,128)(2,1)S(1)}, bf16[96,1792]{1,0:T(8,128)(2,1)S(1)}, u32[]{:S(2)}, u32[]{:S(2)}) collective-permute-start(bf16[96,1792]{1,0:T(8,128)(2,1)S(1)} %slice.234), channel_id=1, source_target_pairs={{0,2},{2,0},{4,6},{6,4},{8,10},{10,8},{12,14},{14,12},{1,3},{3,1},... | collective-permute-start | bytes 1032200 | tf_op jit(solution)/shard_map/ppermute | solution.py:94
  160.1 29.5 %collective-permute-start.37 = (bf16[96,1792]{1,0:T(8,128)(2,1)S(1)}, bf16[96,1792]{1,0:T(8,128)(2,1)S(1)}, u32[]{:S(2)}, u32[]{:S(2)}) collective-permute-start(bf16[96,1792]{1,0:T(8,128)(2,1)S(1)} %slice.233), channel_id=1, source_target_pairs={{0,2},{2,0},{12,14},{14,12},{1,3},{3,1},{13,15},{15,13},{16,18},{1... | collective-permute-start | bytes 1032200 | tf_op jit(solution)/shard_map/ppermute | solution.py:94
  168.2 22.5 %collective-permute-start.15 = (bf16[96,1792]{1,0:T(8,128)(2,1)S(1)}, bf16[96,1792]{1,0:T(8,128)(2,1)S(1)}, u32[]{:S(2)}, u32[]{:S(2)}) collective-permute-start(bf16[96,1792]{1,0:T(8,128)(2,1)S(1)} %get-tuple-element.27), channel_id=1, source_target_pairs={{4,6},{6,4},{8,10},{10,8},{12,14},{14,12},{5,7},{7,5},{9,11},{11,9... | collective-permute-start | bytes 1032200 | tf_op jit(solution)/shard_map/ppermute | solution.py:94
  171.8 38.6 %collective-permute-start.29 = (bf16[128,1792]{1,0:T(8,128)(2,1)S(1)}, bf16[128,1792]{1,0:T(8,128)(2,1)S(1)}, u32[]{:S(2)}, u32[]{:S(2)}) collective-permute-start(bf16[128,1792]{1,0:T(8,128)(2,1)S(1)} %fusion.43), channel_id=1, source_target_pairs={{0,8},{2,10},{4,12},{6,14},{8,0},{10,2},{12,4},{14,6},{1,9},{3,11}... | collective-permute-start | bytes 1376264 | tf_op jit(solution)/shard_map/ppermute | solution.py:94
  186.2 36.1 %copy-start.9 = (f32[128]{0:T(128)S(1)}, f32[128]{0:T(128)}, u32[]{:S(2)}) copy-start(f32[128]{0:T(128)} %copy-done.8) | copy-start | bytes 1540
  186.2 11.3 %collective-permute-start.17 = (bf16[96,1792]{1,0:T(8,128)(2,1)S(1)}, bf16[96,1792]{1,0:T(8,128)(2,1)S(1)}, u32[]{:S(2)}, u32[]{:S(2)}) collective-permute-start(bf16[96,1792]{1,0:T(8,128)(2,1)S(1)} %get-tuple-element.26), channel_id=1, source_target_pairs={{0,2},{2,0},{4,6},{6,4},{8,10},{10,8},{1,3},{3,1},{5,7},{7,5},{9,1... | collective-permute-start | bytes 1032200 | tf_op jit(solution)/shard_map/ppermute | solution.py:94
  190.0 20.4 %collective-permute-start.38 = (bf16[128,1792]{1,0:T(8,128)(2,1)S(1)}, bf16[128,1792]{1,0:T(8,128)(2,1)S(1)}, u32[]{:S(2)}, u32[]{:S(2)}) collective-permute-start(bf16[128,1792]{1,0:T(8,128)(2,1)S(1)} %fusion.42), channel_id=1, source_target_pairs={{0,12},{2,14},{12,0},{14,2},{1,13},{3,15},{13,1},{15,3},{16,28},{1... | collective-permute-start | bytes 1376264 | tf_op jit(solution)/shard_map/ppermute | solution.py:94
  191.0 31.3 %collective-permute-start.16 = (bf16[128,1792]{1,0:T(8,128)(2,1)S(1)}, bf16[128,1792]{1,0:T(8,128)(2,1)S(1)}, u32[]{:S(2)}, u32[]{:S(2)}) collective-permute-start(bf16[128,1792]{1,0:T(8,128)(2,1)S(1)} %fusion.45), channel_id=1, source_target_pairs={{4,0},{6,2},{8,4},{10,6},{12,8},{14,10},{5,1},{7,3},{9,5},{11,7},{... | collective-permute-start | bytes 1376264 | tf_op jit(solution)/shard_map/ppermute | solution.py:94
  197.8 24.5 %collective-permute-start.18 = (bf16[128,1792]{1,0:T(8,128)(2,1)S(1)}, bf16[128,1792]{1,0:T(8,128)(2,1)S(1)}, u32[]{:S(2)}, u32[]{:S(2)}) collective-permute-start(bf16[128,1792]{1,0:T(8,128)(2,1)S(1)} %fusion.44), channel_id=1, source_target_pairs={{0,4},{2,6},{4,8},{6,10},{8,12},{10,14},{1,5},{3,7},{5,9},{7,11},{... | collective-permute-start | bytes 1376264 | tf_op jit(solution)/shard_map/ppermute | solution.py:94
  199.8 10.6 %collective-permute-start.14 = (bf16[96,1792]{1,0:T(8,128)(2,1)S(1)}, bf16[96,1792]{1,0:T(8,128)(2,1)S(1)}, u32[]{:S(2)}, u32[]{:S(2)}) collective-permute-start(bf16[96,1792]{1,0:T(8,128)(2,1)S(1)} %get-tuple-element.25), channel_id=1, source_target_pairs={{0,2},{2,0},{4,6},{6,4},{8,10},{10,8},{12,14},{14,12},{1,3},{3,1},... | collective-permute-start | bytes 1032200 | tf_op jit(solution)/shard_map/ppermute | solution.py:94
  (4 other events, 8.3 us)

commit v2 on v0

--- a/solution.py
+++ b/solution.py
@@ -1,6 +1,10 @@
+import functools
+
 import jax
 import jax.numpy as jnp
 from jax import lax
+from jax.experimental import pallas as pl
+from jax.experimental.pallas import tpu as pltpu
 from jax.sharding import PartitionSpec as P
 
 
@@ -18,7 +22,7 @@
     return summed + lax.dot_general(up_grad, up_mat, numbers, preferred_element_type=jnp.float32)
 
 
-def local(tokens, out_grad, route_weight, expert_ids, w_gate, w_up, w_down):
+def exchanged(tokens, out_grad, route_weight, expert_ids, w_gate, w_up, w_down):
     tok_rows, half_width = tokens.shape
     top_count = expert_ids.shape[1]
     experts = lax.axis_size("node")
@@ -37,28 +41,20 @@
     cot_send = jnp.zeros((experts * capacity, half_width), jnp.bfloat16).at[target].set(scaled)
     feat_send = feat_send.reshape(experts, capacity, half_width)
     cot_send = cot_send.reshape(experts, capacity, half_width)
-    gate_half = w_gate[0]
-    up_half = w_up[0]
-    down_half = w_down[0]
-    feat_full = lax.all_gather(
-        lax.all_to_all(feat_send, "node", split_axis=0, concat_axis=0, tiled=True),
-        "local",
-        axis=2,
-        tiled=True,
-    )
-    cot_full = lax.all_gather(
-        lax.all_to_all(cot_send, "node", split_axis=0, concat_axis=0, tiled=True),
-        "local",
-        axis=2,
-        tiled=True,
-    )
+
+    def to_experts(sent):
+        moved = lax.all_to_all(sent, "node", split_axis=0, concat_axis=0, tiled=True)
+        return lax.all_gather(moved, "local", axis=2, tiled=True)
+
+    feat_full = to_experts(feat_send)
+    cot_full = to_experts(cot_send)
     sources, slot_count, feat_width = feat_full.shape
     partial_value = expert_grad(
         feat_full.reshape(-1, feat_width),
         cot_full.reshape(-1, feat_width),
-        gate_half,
-        up_half,
-        down_half,
+        w_gate[0],
+        w_up[0],
+        w_down[0],
     )
     own_sum = lax.psum_scatter(
         partial_value.reshape(sources, slot_count, feat_width),
@@ -74,6 +70,329 @@
         picked.reshape(tok_rows, top_count, half_width).astype(jnp.float32), axis=1
     )
     return summed.astype(jnp.bfloat16)
+
+
+def node(z, y):
+    return 2 * z + y
+
+
+def along(pairs):
+    return [(node(a, y), node(b, y)) for a, b in pairs for y in range(2)]
+
+
+def across(places):
+    return [(node(z, y), node(z, 1 - y)) for z in places for y in range(2)]
+
+
+UP1 = along([(0, 1), (1, 2), (2, 3)])
+DOWN1 = along([(1, 0), (2, 1), (3, 2)])
+UP2 = along([(1, 2), (2, 3)])
+DOWN2 = along([(2, 1), (1, 0)])
+ENDS = along([(2, 3), (1, 0)])
+SKIP = along([(0, 2), (1, 3), (2, 0), (3, 1)])
+FAR = along([(0, 3), (3, 0)])
+Y_ALL, Y_UP, Y_DOWN, Y_ENDS = across(range(4)), across([1, 2, 3]), across([0, 1, 2]), across([0, 3])
+SLOTS = 5
+BF, F32 = jnp.bfloat16, jnp.float32
+ON_CHIP = pl.BlockSpec(memory_space=pltpu.VMEM)
+ON_CHIP_SCALARS = pl.BlockSpec(memory_space=pltpu.SMEM)
+ANYWHERE = pl.BlockSpec(memory_space=pl.ANY)
+SMALL = pl.CostEstimate(flops=1024, bytes_accessed=1024, transcendentals=0)
+
+
+def move(value, pairs):
+    return lax.ppermute(value, "node", pairs)
+
+
+def swap(value):
+    return lax.ppermute(value, "local", [(0, 1), (1, 0)])
+
+
+def dot(a, b):
+    return jnp.dot(a, b, preferred_element_type=F32)
+
+
+def dot_t(a, b):
+    return lax.dot_general(a, b, (((1,), (1,)), ((), ())), preferred_element_type=F32)
+
+
+def params():
+    return pltpu.CompilerParams(vmem_limit_bytes=16 * 1024 * 1024)
+
+
+def places_of(weights):
+    tokens = weights.shape[-1]
+    earlier = lax.broadcasted_iota(jnp.int32, (tokens, tokens), 0) < lax.broadcasted_iota(
+        jnp.int32, (tokens, tokens), 1
+    )
+    routed = (weights > 0.0).astype(F32)
+    place = dot(routed.astype(BF), earlier.astype(F32).astype(BF))
+    return jnp.where(weights > 0.0, place, -1.0)
+
+
+def pick_of(place, capacity):
+    slots = lax.broadcasted_iota(jnp.int32, (capacity, place.shape[-1]), 0).astype(F32)
+    return jnp.where(slots == place, 1.0, 0.0).astype(F32)
+
+
+def routes_kernel(capacity, at, routes, place_out, weight_out):
+    z, y = at[0], at[1]
+    first = y == 0
+    tokens = routes.shape[-1]
+    sent, dense, slots = [], [], []
+    for where in (z, z + 3, z + 1, z ^ 2, 3 - z):
+        where = lax.rem(where, 4)
+        mine, theirs = routes[2 * where + y], routes[2 * where + 1 - y]
+        dense.append(jnp.where(first, mine[0:1], mine[1:2]))
+        sent.append(jnp.where(first, mine[1:2], mine[0:1]))
+        slots.append(jnp.where(first, theirs[0:1], theirs[1:2]))
+    pad = [jnp.zeros((16 - 2 * SLOTS, tokens), F32)]
+    place = places_of(jnp.concatenate(sent + slots + pad, axis=0))
+    same = lax.broadcasted_iota(jnp.int32, (tokens, tokens), 0) == lax.broadcasted_iota(
+        jnp.int32, (tokens, tokens), 1
+    )
+    for i in range(SLOTS):
+        place_out[i] = place[i : i + 1]
+        weight_out[i, :tokens] = jnp.sum(jnp.where(same, dense[i], 0.0), axis=1, keepdims=True)
+        pick = pick_of(place[SLOTS + i : SLOTS + i + 1], capacity)
+        weight_out[i, tokens:] = jnp.sum(pick * slots[i], axis=1, keepdims=True)
+
+
+def route_tables(at, routes, capacity):
+    tokens = routes.shape[-1]
+    return pl.pallas_call(
+        functools.partial(routes_kernel, capacity),
+        out_shape=[
+            jax.ShapeDtypeStruct((SLOTS, 1, tokens), F32),
+            jax.ShapeDtypeStruct((SLOTS, tokens + capacity, 1), F32),
+        ],
+        in_specs=[pl.BlockSpec(memory_space=pltpu.SMEM), pl.BlockSpec(memory_space=pltpu.VMEM)],
+        out_specs=[pl.BlockSpec(memory_space=pltpu.VMEM)] * 2,
+        compiler_params=params(),
+        cost_estimate=SMALL,
+        name="routes",
+    )(at, routes)
+
+
+def pick_kernel(capacity, place, both, *rest):
+    out = rest[-1]
+    tokens = place.shape[-1]
+    pick = pick_of(place[...], capacity).astype(BF)
+    out[:capacity] = dot(pick, both[:tokens]).astype(BF)
+    out[capacity:] = dot(pick, both[tokens:]).astype(BF)
+
+
+def picked_rows(place, both, capacity, after=()):
+    return pl.pallas_call(
+        functools.partial(pick_kernel, capacity),
+        out_shape=jax.ShapeDtypeStruct((2 * capacity, both.shape[1]), BF),
+        in_specs=[pl.BlockSpec(memory_space=pltpu.VMEM)] * 2 + [ANYWHERE] * len(after),
+        out_specs=pl.BlockSpec(memory_space=pltpu.VMEM),
+        compiler_params=params(),
+        cost_estimate=SMALL,
+        name="pick",
+    )(place, both, *after)
+
+
+def grads_kernel(side, block, block_far, slots, slots_far, weight, gate, up, down, *rest):
+    out = rest[-1]
+    capacity, tokens, half = slots.shape[0] // 2, block.shape[0] // 2, block.shape[1]
+    ff = gate.shape[1]
+    near = pl.ds(pl.multiple_of(side[0] * half, 256), half)
+    far = pl.ds(pl.multiple_of((1 - side[0]) * half, 256), half)
+
+    def feats(block, slots):
+        return jnp.concatenate([block[:tokens], slots[:capacity]], axis=0)
+
+    def cots(block, slots):
+        return jnp.concatenate([block[tokens:], slots[capacity:]], axis=0)
+
+    width = ff // 2
+    for at in range(0, ff, width):
+        cols = slice(at, at + width)
+        rows, rows_far = feats(block, slots), feats(block_far, slots_far)
+        gate_pre = dot(rows, gate[near, cols]) + dot(rows_far, gate[far, cols])
+        up_pre = dot(rows, up[near, cols]) + dot(rows_far, up[far, cols])
+        rows, rows_far = cots(block, slots), cots(block_far, slots_far)
+        hidden = dot_t(rows, down[cols, near]) + dot_t(rows_far, down[cols, far])
+        hidden = hidden * weight[...]
+        sig = jax.nn.sigmoid(gate_pre)
+        out[:, cols] = (hidden * up_pre * sig * (1.0 + gate_pre * (1.0 - sig))).astype(BF)
+        out[:, ff + at : ff + at + width] = (hidden * gate_pre * sig).astype(BF)
+
+
+def grads_of(side, block, slots, weight, mats, after=()):
+    rows = (block[0].shape[0] + slots[0].shape[0]) // 2
+    return pl.pallas_call(
+        grads_kernel,
+        out_shape=jax.ShapeDtypeStruct((rows, 2 * mats[0].shape[1]), BF),
+        in_specs=[ON_CHIP_SCALARS] + [ON_CHIP] * 8 + [ANYWHERE] * len(after),
+        out_specs=ON_CHIP,
+        compiler_params=params(),
+        cost_estimate=SMALL,
+        name="grads",
+    )(side, *block, *slots, weight, *mats, *after)
+
+
+def back_kernel(side, own, other, gate, up, far, *rest):
+    dense, slots = rest[-2:]
+    tokens, half = dense.shape
+    ff = gate.shape[1]
+    width = 256
+    for at in range(0, half, width):
+        near, cols = pl.ds(pl.multiple_of(side[0] * half + at, 256), width), slice(at, at + width)
+        total = dot_t(own[:, :ff], gate[near, :]) + dot_t(own[:, ff:], up[near, :])
+        total += dot_t(other[:, :ff], far[0, cols]) + dot_t(other[:, ff:], far[1, cols])
+        dense[:, cols] = total[:tokens]
+        slots[:, cols] = total[tokens:].astype(BF)
+
+
+def back_of(side, own, other, mats, mats_far, tokens, after=()):
+    rows, half = own.shape[0], mats_far.shape[1]
+    return pl.pallas_call(
+        back_kernel,
+        out_shape=[
+            jax.ShapeDtypeStruct((tokens, half), F32),
+            jax.ShapeDtypeStruct((rows - tokens, half), BF),
+        ],
+        in_specs=[ON_CHIP_SCALARS] + [ON_CHIP] * 5 + [ANYWHERE] * len(after),
+        out_specs=[ON_CHIP] * 2,
+        compiler_params=params(),
+        cost_estimate=SMALL,
+        name="back",
+    )(side, own, other, *mats, mats_far, *after)
+
+
+def spread(place, came):
+    pick = pick_of(place, came.shape[0]).astype(BF)
+    return lax.dot_general(pick, came, (((0,), (0,)), ((), ())), preferred_element_type=F32)
+
+
+def join_kernel(parts, place, came, dense, *rest):
+    out = rest[-1]
+    total = dense[...] + spread(place[...], came[...])
+    for part in rest[:parts]:
+        total = total + part[...].astype(F32)
+    out[...] = total.astype(out.dtype)
+
+
+def joined(place, came, dense, parts=(), dtype=BF, after=()):
+    return pl.pallas_call(
+        functools.partial(join_kernel, len(parts)),
+        out_shape=jax.ShapeDtypeStruct(dense.shape, dtype),
+        in_specs=[pl.BlockSpec(memory_space=pltpu.VMEM)] * (3 + len(parts))
+        + [ANYWHERE] * len(after),
+        out_specs=pl.BlockSpec(memory_space=pltpu.VMEM),
+        compiler_params=params(),
+        cost_estimate=SMALL,
+        name="join",
+    )(place, came, dense, *parts, *after)
+
+
+def lines(tokens, out_grad, route_weight, expert_ids, w_gate, w_up, w_down):
+    tok_rows, half = tokens.shape
+    experts = lax.axis_size("node")
+    top_count = expert_ids.shape[1]
+    capacity = 3 * tok_rows * top_count // (2 * experts)
+    me = lax.axis_index("node")
+    z, y = me // 2, me % 2
+    at = jnp.stack([z, y]).astype(jnp.int32)
+    side = lax.axis_index("local").astype(jnp.int32)
+    side1 = side[None]
+
+    both = jnp.concatenate([tokens, out_grad], axis=0)
+    b_up, b_down = move(both, UP1), move(both, DOWN1)
+
+    table = jnp.sum(
+        jnp.where(
+            expert_ids[None] == jnp.arange(experts, dtype=jnp.int32)[:, None, None],
+            route_weight[None],
+            0.0,
+        ),
+        axis=2,
+    )
+    own_place = places_of(lax.dynamic_slice_in_dim(table, me ^ 1, 1, 0))
+    own_rows = picked_rows(own_place, both, capacity)
+    pairs = table.reshape(experts // 2, 1, 2, tok_rows)
+    routes = lax.all_to_all(
+        jnp.broadcast_to(pairs, (experts // 2, 2, 2, tok_rows)).reshape(experts, 2, tok_rows),
+        "node",
+        split_axis=0,
+        concat_axis=0,
+        tiled=True,
+    )
+    places, weights = route_tables(at, routes, capacity)
+
+    gate, up, down = w_gate[0], w_up[0], w_down[0]
+    gate_late, up_late, own_rows = lax.optimization_barrier((gate, up, own_rows))
+    other = lambda mat: lax.dynamic_slice_in_dim(mat, (1 - side) * half, half, 0)
+    far_mats = swap(jnp.stack([other(gate_late), other(up_late)]))
+
+    def halves(block):
+        return block, swap(block)
+
+    def late(value, *before):
+        return lax.optimization_barrier((value, *before))[0]
+
+    def back(own, other, after=()):
+        return back_of(side1, own, other, (gate, up), far_mats, tok_rows, after)
+
+    def grads(index, block, slots, after=()):
+        return grads_of(side1, block, slots, weights[index], (gate, up, down), after)
+
+    own_y = move(own_rows, Y_ALL)
+    own_halves, own_slots = halves(both), halves(own_y)
+
+    b_up, b_down, places, *_ = lax.optimization_barrier(
+        (b_up, b_down, places, far_mats, own_halves, own_slots)
+    )
+    up_two, down_two = move(b_up, UP2), move(b_down, DOWN2)
+    up_rows = picked_rows(places[1], b_up, capacity)
+    up_y = move(up_rows, Y_UP)
+    down_rows = picked_rows(places[2], b_down, capacity, (up_rows,))
+    down_y = move(down_rows, Y_DOWN)
+    grads0 = grads(0, own_halves, own_slots, (down_rows,))
+
+    up_two, down_two, grads0, up_y = lax.optimization_barrier((up_two, down_two, grads0, up_y))
+    b_two = jnp.where(z >= 2, up_two, down_two)
+    b_far = move(b_two, ENDS)
+    two_rows = picked_rows(places[3], b_two, capacity)
+    two_y = move(two_rows, Y_ALL)
+    dense0, slots0 = back(grads0, swap(grads0), (two_rows,))
+    grads1 = grads(1, halves(late(b_up, up_two)), halves(up_y), (dense0,))
+    grads2 = grads(2, halves(late(b_down, up_two)), halves(down_y), (grads1,))
+
+    b_far, grads1, grads2, slots0, two_y = lax.optimization_barrier(
+        (b_far, grads1, grads2, slots0, two_y)
+    )
+    far_rows = picked_rows(places[4], b_far, capacity)
+    far_y = move(far_rows, Y_ENDS)
+    dense1, slots1 = back(grads1, swap(grads1), (far_rows,))
+    came1 = move(slots1, Y_UP)
+    dense2, slots2 = back(grads2, swap(grads2), (dense1,))
+    grads3 = grads(3, halves(b_two), halves(two_y), (dense2,))
+    far_halves = halves(b_far)
+
+    far_y, grads3, came1, far_halves, dense2, slots2 = lax.optimization_barrier(
+        (far_y, grads3, came1, far_halves, dense2, slots2)
+    )
+    came2 = move(slots2, Y_DOWN)
+    home1 = move(joined(places[1], came1, dense1), DOWN1)
+    dense3, slots3 = back(grads3, swap(grads3))
+    grads4 = grads(4, far_halves, halves(far_y), (dense3,))
+    came2, slots3, grads4 = lax.optimization_barrier((came2, slots3, grads4))
+    came3 = move(slots3, Y_ALL)
+    home2 = move(joined(places[2], came2, dense2), UP1)
+    dense4, slots4 = back(grads4, swap(grads4))
+    came4 = move(slots4, Y_ENDS)
+    home3 = move(joined(places[3], came3, dense3), SKIP)
+    came0 = move(late(slots0, dense4), Y_ALL)
+    own = joined(own_place, came0, dense0, (out_grad,), F32)
+    summed = own + home1.astype(F32)
+    home4 = move(joined(places[4], came4, dense4), FAR)
+    for value in (home2, home3, home4):
+        summed = summed + value.astype(F32)
+    return summed.astype(BF)
 
 
 def solution(mesh):
@@ -86,6 +405,7 @@
         P("node", None, "local"),
         P("node", "local", None),
     )
+    body = lines if mesh.shape["node"] == 8 else exchanged
     return jax.shard_map(
-        local, mesh=mesh, in_specs=placed, out_specs=P(("groups", "node"), "local"), check_vma=False
-    )
+        body, mesh=mesh, in_specs=placed, out_specs=P(("groups", "node"), "local"), check_vma=False
+    )

time: 317 us -> 190 us (0.60)
  blocking collectives: 134 us -> 0 us
  starting transfers between devices: 6.34 us -> 55.4 us
  Pallas kernels: 0 us -> 43.2 us
  matrix products: 26.5 us -> 0.13 us
  waiting for transfers between devices: 90.1 us -> 69.2 us
  between operations: 13.2 us -> 0.51 us
  other arithmetic: 17.6 us -> 5.22 us
  local copies, waits for them, and re-layouts: 26 us -> 14 us
    all_to_all x2 -> x0, blocking collectives: 134 us -> none  [the longest x1 67.7 us: local(): lax.all_to_all(feat_send, 'node', split_axis=0, concat_axis=0, tiled=True)]
    ppermute x0 -> x35, waiting for transfers between devices: none -> 64.3 us  [the longest x19 62.7 us: move(): return lax.ppermute(value, 'node', pairs)]
    all_to_all x1, waiting for transfers between devices: 60.2 us -> 4.94 us  [lines(): lax.all_to_all(jnp.broadcast_to(pairs, (experts // 2, 2, 2, tok_rows)).re...]
    ppermute x0 -> x35, starting transfers between devices: none -> 49.2 us  [the longest x19 46.3 us: move(): return lax.ppermute(value, 'node', pairs)]
    pallas_call x0 -> x21, Pallas kernels: none -> 43.2 us  [the longest x5 22.3 us: back_of(): pl.pallas_call(back_kernel, out_shape=[jax.ShapeDtypeStruct((tokens, half...]
    dot_general x5 -> x1, matrix products: 26.5 us -> 0.13 us  [dot(): return jnp.dot(a, b, preferred_element_type=F32)]
    reduce_scatter x1 -> x0, waiting for transfers between devices: 21 us -> none  [local(): lax.psum_scatter(partial_value.reshape(sources, slot_count, feat_width),...]
    convert_element_type x2 -> x0, local copies, waits for them, and re-layouts: 9.7 us -> none  [the longest x1 5.23 us: local(): jnp.repeat(out_grad, top_count, axis=0).astype(jnp.float32)]
  transfers between devices with their start and end apart: 4 -> 36, of which waited for: 3 -> 12; matrix products, arithmetic and copies ran while one was open for 6% -> 2% of each run, Pallas kernels for 0% -> 23%
where the time goes in v2:
time: 190 us; the launch traced here: 188 us
  waiting for transfers between devices  69.2 us (36%)
  starting transfers between devices  55.4 us (29%)
  Pallas kernels  43.2 us (23%)
  local copies, waits for them, and re-layouts  14 us (7%)
  other arithmetic  5.22 us (3%)
    ppermute x19, waiting for transfers between devices, move(): return lax.ppermute(value, 'node', pairs)  62.7 us
    ppermute x19, starting transfers between devices, move(): return lax.ppermute(value, 'node', pairs)  46.3 us
    pallas_call x5, Pallas kernels, back_of(): pl.pallas_call(back_kernel, out_shape=[jax.ShapeDtypeStruct((tokens, half...  22.3 us
    pallas_call x5, Pallas kernels, grads_of(): pl.pallas_call(grads_kernel, out_shape=jax.ShapeDtypeStruct((rows, 2 * ma...  16.8 us
    unnamed x17, local copies, waits for them, and re-layouts  8.84 us
    all_to_all x1, starting transfers between devices, lines(): lax.all_to_all(jnp.broadcast_to(pairs, (experts // 2, 2, 2, tok_rows)).re...  6.28 us
    all_to_all x1, waiting for transfers between devices, lines(): lax.all_to_all(jnp.broadcast_to(pairs, (experts // 2, 2, 2, tok_rows)).re...  4.94 us
  transfers between devices with their start and end apart: 36, of which 12 were waited for; matrix products, arithmetic and copies ran while one was open for 2% of the time, Pallas kernels for 23%

profile of v2, /device:TPU:8, one launch (start us, length us, event | category | flops | bytes accessed | tf_op | source)
XLA Modules:
  0.0 187.7 jit_solution(3569561548206485465)
XLA Ops:
  0.0 1.0 constant_dynamic-update-slice_fusion.1
  1.9 1.1 constant_dynamic-update-slice_fusion.both.block
  3.3 2.3 %dynamic-slice_bitcast_fusion = (bf16[1,1792,512]{2,1,0:T(8,128)(2,1)S(1)}, bf16[1,1792,512]{2,1,0:T(8,128)(2,1)S(1)}) fusion(bf16[3584,512]{1,0:T(8,128)(2,1)} %bitcast.46, s32[]{:T(128)S(6)} %select_n.40, bf16[3584,512]{1,0:T(8,128)(2,1)} %bitcast.35), kind=kLoop, calls=%fused_computation.1 | loop fusion | bytes 7340036 | tf_op jit(solution)/shard_map/stack | solution.py:329
  5.6 2.1 %pad_maximum_fusion = bf16[2,1792,512]{2,1,0:T(8,128)(2,1)} fusion(bf16[1,1792,512]{2,1,0:T(8,128)(2,1)S(1)} %get-tuple-element.94, bf16[1,1792,512]{2,1,0:T(8,128)(2,1)S(1)} %get-tuple-element.95), kind=kLoop, calls=%fused_computation | loop fusion | flops 1835008 | bytes 7340032 | tf_op jit(solution)/shard_map/stack | solution.py:329
  7.7 1.5 collective-permute-start.4
  9.4 2.3 %collective-permute-start.1 = (bf16[256,1792]{1,0:T(8,128)(2,1)S(1)}, bf16[256,1792]{1,0:T(8,128)(2,1)S(1)}, u32[]{:S(2)}, u32[]{:S(2)}) collective-permute-start(bf16[256,1792]{1,0:T(8,128)(2,1)S(1)} %constant_dynamic-update-slice_fusion.both.block), channel_id=1, source_target_pairs={{4,0},{6,2},{8,4},{10,6},{12,8},{14,10},{5,1},{7,3},{9,5},{11,7},{... | collective-permute-start | bytes 2752520 | tf_op jit(solution)/shard_map/ppermute | solution.py:104
  11.8 3.5 %collective-permute-start = (bf16[256,1792]{1,0:T(8,128)(2,1)S(1)}, bf16[256,1792]{1,0:T(8,128)(2,1)S(1)}, u32[]{:S(2)}, u32[]{:S(2)}) collective-permute-start(bf16[256,1792]{1,0:T(8,128)(2,1)S(1)} %constant_dynamic-update-slice_fusion.both.block), channel_id=1, source_target_pairs={{0,4},{2,6},{4,8},{6,10},{8,12},{10,14},{1,5},{3,7},{5,9},{7,11},{... | collective-permute-start | bytes 2752520 | tf_op jit(solution)/shard_map/ppermute | solution.py:104
  15.3 10.4 %collective-permute-done.4.slots = bf16[192,1792]{1,0:T(8,128)(2,1)} collective-permute-done((bf16[192,1792]{1,0:T(8,128)(2,1)S(1)}, bf16[192,1792]{1,0:T(8,128)(2,1)}, u32[]{:S(2)}, u32[]{:S(2)}) %collective-permute-start.4) | collective-permute-done | bytes 688160 | tf_op jit(solution)/shard_map/ppermute | solution.py:104
  26.3 6.3 %all-to-all-start = ((f32[8,2,128]{2,1,0:T(2,128)}), f32[8,2,128]{2,1,0:T(2,128)S(1)}, u32[]{:S(2)}, u32[]{:S(2)}) async-start(f32[8,2,128]{2,1,0:T(2,128)} %bitcast.6), calls=%async_computation | async-start | bytes 16384 | tf_op jit(solution)/shard_map/all_to_all | solution.py:317
  32.6 4.9 %all-to-all-done.routes = f32[8,2,128]{2,1,0:T(2,128)S(1)} async-done(((f32[8,2,128]{2,1,0:T(2,128)}), f32[8,2,128]{2,1,0:T(2,128)S(1)}, u32[]{:S(2)}, u32[]{:S(2)}) %all-to-all-start) | async-done | bytes 8224 | tf_op jit(solution)/shard_map/all_to_all | solution.py:317
  37.6 0.8 routes.1
  38.4 0.8 copy-done.7
  39.2 0.8 copy-done.5
  40.1 3.4 %collective-permute-start.6 = (bf16[256,1792]{1,0:T(8,128)(2,1)S(1)}, bf16[256,1792]{1,0:T(8,128)(2,1)}, u32[]{:S(2)}, u32[]{:S(2)}) collective-permute-start(bf16[256,1792]{1,0:T(8,128)(2,1)S(1)} %collective-permute-done.both.block), channel_id=1, source_target_pairs={{4,8},{6,10},{8,12},{10,14},{5,9},{7,11},{9,13},{11,15},{20,24},{2... | collective-permute-start | bytes 2752520 | tf_op jit(solution)/shard_map/ppermute | solution.py:104
  43.5 1.9 %collective-permute-start.7 = (bf16[256,1792]{1,0:T(8,128)(2,1)S(1)}, bf16[256,1792]{1,0:T(8,128)(2,1)}, u32[]{:S(2)}, u32[]{:S(2)}) collective-permute-start(bf16[256,1792]{1,0:T(8,128)(2,1)S(1)} %collective-permute-done.1.both.block), channel_id=1, source_target_pairs={{8,4},{10,6},{4,0},{6,2},{9,5},{11,7},{5,1},{7,3},{24,20},{26,22},... | collective-permute-start | bytes 2752520 | tf_op jit(solution)/shard_map/ppermute | solution.py:104
  45.8 2.9 %collective-permute-start.8 = (bf16[192,1792]{1,0:T(8,128)(2,1)S(1)}, bf16[192,1792]{1,0:T(8,128)(2,1)}, u32[]{:S(2)}, u32[]{:S(2)}) collective-permute-start(bf16[192,1792]{1,0:T(8,128)(2,1)S(1)} %pick.6.rest_0_), channel_id=1, source_target_pairs={{4,6},{6,4},{8,10},{10,8},{12,14},{14,12},{5,7},{7,5},{9,11},{11,9... | collective-permute-start | bytes 2064392 | tf_op jit(solution)/shard_map/ppermute | solution.py:104
  49.0 3.0 %collective-permute-start.14 = (bf16[192,1792]{1,0:T(8,128)(2,1)S(1)}, bf16[192,1792]{1,0:T(8,128)(2,1)S(1)}, u32[]{:S(2)}, u32[]{:S(2)}) collective-permute-start(bf16[192,1792]{1,0:T(8,128)(2,1)S(1)} %pick.7.rest_0_), channel_id=1, source_target_pairs={{0,2},{2,0},{4,6},{6,4},{8,10},{10,8},{1,3},{3,1},{5,7},{7,5},{9,1... | collective-permute-start | bytes 2064392 | tf_op jit(solution)/shard_map/ppermute | solution.py:104
  52.0 1.2 slice_bitcast_fusion
  53.2 2.0 %copy-done = bf16[1,3584,512]{2,1,0:T(8,128)(2,1)S(1)} copy-done((bf16[1,3584,512]{2,1,0:T(8,128)(2,1)S(1)}, bf16[1,3584,512]{2,1,0:T(8,128)(2,1)}, u32[]{:S(2)}) %copy-start) | copy-done | bytes 3670040
  55.2 2.0 %copy-done.1 = bf16[1,3584,512]{2,1,0:T(8,128)(2,1)S(1)} copy-done((bf16[1,3584,512]{2,1,0:T(8,128)(2,1)S(1)}, bf16[1,3584,512]{2,1,0:T(8,128)(2,1)}, u32[]{:S(2)}) %copy-start.1) | copy-done | bytes 3670040
  57.3 2.0 %copy-done.2 = bf16[1,512,3584]{2,1,0:T(8,128)(2,1)S(1)} copy-done((bf16[1,512,3584]{2,1,0:T(8,128)(2,1)S(1)}, bf16[1,512,3584]{2,1,0:T(8,128)(2,1)}, u32[]{:S(2)}) %copy-start.2) | copy-done | bytes 3670040
  59.3 4.2 %grads.5.own = bf16[224,1024]{1,0:T(8,128)(2,1)S(1)} custom-call(s32[1]{0:T(128)} %bitcast.11.side, bf16[256,1792]{1,0:T(8,128)(2,1)S(1)} %constant_dynamic-update-slice_fusion.both.block, bf16[256,1792]{1,0:T(8,128)(2,1)} %collective-permute-done.3.block_far, bf16[192,1792]{1,0:T(8,128)(2,1)} %collective-permute-done.4.slots, ...), custom_call_target="tpu_custom_call" | custom-call | flops 1024 | bytes 1024 | tf_op jit(solution)/shard_map/grads/pallas_call | solution.py:226
  63.5 2.6 %collective-permute-done.8.slots = bf16[192,1792]{1,0:T(8,128)(2,1)} collective-permute-done((bf16[192,1792]{1,0:T(8,128)(2,1)S(1)}, bf16[192,1792]{1,0:T(8,128)(2,1)}, u32[]{:S(2)}, u32[]{:S(2)}) %collective-permute-start.8) | collective-permute-done | bytes 688160 | tf_op jit(solution)/shard_map/ppermute | solution.py:104
  67.7 1.3 broadcast_select_fusion.both.block
  69.0 9.7 %collective-permute-done.14.slots = bf16[192,1792]{1,0:T(8,128)(2,1)S(1)} collective-permute-done((bf16[192,1792]{1,0:T(8,128)(2,1)S(1)}, bf16[192,1792]{1,0:T(8,128)(2,1)S(1)}, u32[]{:S(2)}, u32[]{:S(2)}) %collective-permute-start.14) | collective-permute-done | bytes 688160 | tf_op jit(solution)/shard_map/ppermute | solution.py:104
  78.7 1.5 collective-permute-start.9
  81.4 4.7 %back.5 = (f32[128,1792]{1,0:T(8,128)S(1)}, bf16[96,1792]{1,0:T(8,128)(2,1)S(1)}) custom-call(s32[1]{0:T(128)} %bitcast.11.side, bf16[224,1024]{1,0:T(8,128)(2,1)S(1)} %grads.5.own, bf16[224,1024]{1,0:T(8,128)(2,1)S(1)} %collective-permute-done.12.other, bf16[3584,512]{1,0:T(8,128)(2,1)S(1)} %bitcast.37, bf16[3584,512]{1,0:T(8,128)(2,1)S(1)} %bitcast.48, ...), custom_call_target="tpu_custom_call" | custom-call | flops 1024 | bytes 1024 | tf_op jit(solution)/shard_map/back/pallas_call | solution.py:252
  86.2 4.0 %grads.6.rest_0_.own = bf16[224,1024]{1,0:T(8,128)(2,1)S(1)} custom-call(s32[1]{0:T(128)} %bitcast.11.side, bf16[256,1792]{1,0:T(8,128)(2,1)S(1)} %collective-permute-done.both.block, bf16[256,1792]{1,0:T(8,128)(2,1)S(1)} %collective-permute-done.10.block_far, bf16[192,1792]{1,0:T(8,128)(2,1)} %collective-permute-done.8.slots, ...), custom_call_target="tpu_custom_call" | custom-call | flops 1024 | bytes 1024 | tf_op jit(solution)/shard_map/grads/pallas_call | solution.py:226
  90.2 2.9 %grads.7.own = bf16[224,1024]{1,0:T(8,128)(2,1)S(1)} custom-call(s32[1]{0:T(128)} %bitcast.11.side, bf16[256,1792]{1,0:T(8,128)(2,1)S(1)} %collective-permute-done.1.both.block, bf16[256,1792]{1,0:T(8,128)(2,1)S(1)} %collective-permute-done.13.block_far, bf16[192,1792]{1,0:T(8,128)(2,1)S(1)} %collective-permute-done.14.slots, ...), custom_call_target="tpu_custom_call" | custom-call | flops 1024 | bytes 1024 | tf_op jit(solution)/shard_map/grads/pallas_call | solution.py:226
  93.1 5.5 %collective-permute-done.16.slots = bf16[192,1792]{1,0:T(8,128)(2,1)S(1)} collective-permute-done((bf16[192,1792]{1,0:T(8,128)(2,1)S(1)}, bf16[192,1792]{1,0:T(8,128)(2,1)S(1)}, u32[]{:S(2)}, u32[]{:S(2)}) %collective-permute-start.16) | collective-permute-done | bytes 688160 | tf_op jit(solution)/shard_map/ppermute | solution.py:104
  101.1 4.4 %back.6 = (f32[128,1792]{1,0:T(8,128)S(1)}, bf16[96,1792]{1,0:T(8,128)(2,1)S(1)}) custom-call(s32[1]{0:T(128)} %bitcast.11.side, bf16[224,1024]{1,0:T(8,128)(2,1)S(1)} %grads.6.rest_0_.own, bf16[224,1024]{1,0:T(8,128)(2,1)S(1)} %collective-permute-done.21.other, bf16[3584,512]{1,0:T(8,128)(2,1)S(1)} %bitcast.40, bf16[3584,512]{1,0:T(8,128)(2,1)S(1)} %bitcast.51, ...), custom_call_target="tpu_custom_call" | custom-call | flops 1024 | bytes 1024 | tf_op jit(solution)/shard_map/back/pallas_call | solution.py:252
  105.5 2.8 %collective-permute-start.22 = (bf16[96,1792]{1,0:T(8,128)(2,1)S(1)}, bf16[96,1792]{1,0:T(8,128)(2,1)S(1)}, u32[]{:S(2)}, u32[]{:S(2)}) collective-permute-start(bf16[96,1792]{1,0:T(8,128)(2,1)S(1)} %get-tuple-element.68), channel_id=1, source_target_pairs={{4,6},{6,4},{8,10},{10,8},{12,14},{14,12},{5,7},{7,5},{9,11},{11,9... | collective-permute-start | bytes 1032200 | tf_op jit(solution)/shard_map/ppermute | solution.py:104
  108.3 4.4 %back.7 = (f32[128,1792]{1,0:T(8,128)S(1)}, bf16[96,1792]{1,0:T(8,128)(2,1)S(1)}) custom-call(s32[1]{0:T(128)} %bitcast.11.side, bf16[224,1024]{1,0:T(8,128)(2,1)S(1)} %grads.7.own, bf16[224,1024]{1,0:T(8,128)(2,1)S(1)} %collective-permute-done.20.other, bf16[3584,512]{1,0:T(8,128)(2,1)S(1)} %bitcast.41, bf16[3584,512]{1,0:T(8,128)(2,1)S(1)} %bitcast.52, ...), custom_call_target="tpu_custom_call" | custom-call | flops 1024 | bytes 1024 | tf_op jit(solution)/shard_map/back/pallas_call | solution.py:252
  112.7 2.9 %grads.8.own = bf16[224,1024]{1,0:T(8,128)(2,1)S(1)} custom-call(s32[1]{0:T(128)} %bitcast.11.side, bf16[256,1792]{1,0:T(8,128)(2,1)S(1)} %broadcast_select_fusion.both.block, bf16[256,1792]{1,0:T(8,128)(2,1)S(1)} %collective-permute-done.18.block_far, bf16[192,1792]{1,0:T(8,128)(2,1)S(1)} %collective-permute-done.16.slots, ...), custom_call_target="tpu_custom_call" | custom-call | flops 1024 | bytes 1024 | tf_op jit(solution)/shard_map/grads/pallas_call | solution.py:226
  115.6 1.9 %collective-permute-done.22.came = bf16[96,1792]{1,0:T(8,128)(2,1)S(1)} collective-permute-done((bf16[96,1792]{1,0:T(8,128)(2,1)S(1)}, bf16[96,1792]{1,0:T(8,128)(2,1)S(1)}, u32[]{:S(2)}, u32[]{:S(2)}) %collective-permute-start.22) | collective-permute-done | bytes 344096 | tf_op jit(solution)/shard_map/ppermute | solution.py:104
  118.0 2.6 %collective-permute-start.24 = (bf16[96,1792]{1,0:T(8,128)(2,1)S(1)}, bf16[96,1792]{1,0:T(8,128)(2,1)S(1)}, u32[]{:S(2)}, u32[]{:S(2)}) collective-permute-start(bf16[96,1792]{1,0:T(8,128)(2,1)S(1)} %get-tuple-element.70), channel_id=1, source_target_pairs={{0,2},{2,0},{4,6},{6,4},{8,10},{10,8},{1,3},{3,1},{5,7},{7,5},{9,1... | collective-permute-start | bytes 1032200 | tf_op jit(solution)/shard_map/ppermute | solution.py:104
  120.7 4.4 %back.8 = (f32[128,1792]{1,0:T(8,128)S(1)}, bf16[96,1792]{1,0:T(8,128)(2,1)S(1)}) custom-call(s32[1]{0:T(128)} %bitcast.11.side, bf16[224,1024]{1,0:T(8,128)(2,1)S(1)} %grads.8.own, bf16[224,1024]{1,0:T(8,128)(2,1)S(1)} %collective-permute-done.25.other, bf16[3584,512]{1,0:T(8,128)(2,1)S(1)} %bitcast.43, bf16[3584,512]{1,0:T(8,128)(2,1)S(1)} %bitcast.54, ...), custom_call_target="tpu_custom_call" | custom-call | flops 1024 | bytes 1024 | tf_op jit(solution)/shard_map/back/pallas_call | solution.py:252
  125.1 2.9 %grads.9.own = bf16[224,1024]{1,0:T(8,128)(2,1)S(1)} custom-call(s32[1]{0:T(128)} %bitcast.11.side, bf16[256,1792]{1,0:T(8,128)(2,1)S(1)} %collective-permute-done.9.both.block, bf16[256,1792]{1,0:T(8,128)(2,1)S(1)} %collective-permute-done.23.block_far, bf16[192,1792]{1,0:T(8,128)(2,1)S(1)} %collective-permute-done.17.slots, ...), custom_call_target="tpu_custom_call" | custom-call | flops 1024 | bytes 1024 | tf_op jit(solution)/shard_map/grads/pallas_call | solution.py:226
  127.9 1.9 %collective-permute-done.24.came = bf16[96,1792]{1,0:T(8,128)(2,1)S(1)} collective-permute-done((bf16[96,1792]{1,0:T(8,128)(2,1)S(1)}, bf16[96,1792]{1,0:T(8,128)(2,1)S(1)}, u32[]{:S(2)}, u32[]{:S(2)}) %collective-permute-start.24) | collective-permute-done | bytes 344096 | tf_op jit(solution)/shard_map/ppermute | solution.py:104
  130.6 1.1 collective-permute-done.27.other
  131.7 4.4 %back.9 = (f32[128,1792]{1,0:T(8,128)S(1)}, bf16[96,1792]{1,0:T(8,128)(2,1)S(1)}) custom-call(s32[1]{0:T(128)} %bitcast.11.side, bf16[224,1024]{1,0:T(8,128)(2,1)S(1)} %grads.9.own, bf16[224,1024]{1,0:T(8,128)(2,1)S(1)} %collective-permute-done.27.other, bf16[3584,512]{1,0:T(8,128)(2,1)S(1)} %bitcast.45, bf16[3584,512]{1,0:T(8,128)(2,1)S(1)} %bitcast.56, ...), custom_call_target="tpu_custom_call" | custom-call | flops 1024 | bytes 1024 | tf_op jit(solution)/shard_map/back/pallas_call | solution.py:252
  137.3 7.8 %collective-permute-start.29 = (bf16[128,1792]{1,0:T(8,128)(2,1)S(1)}, bf16[128,1792]{1,0:T(8,128)(2,1)S(1)}, u32[]{:S(2)}, u32[]{:S(2)}) collective-permute-start(bf16[128,1792]{1,0:T(8,128)(2,1)S(1)} %join.6), channel_id=1, source_target_pairs={{4,0},{6,2},{8,4},{10,6},{12,8},{14,10},{5,1},{7,3},{9,5},{11,7},{... | collective-permute-start | bytes 1376264 | tf_op jit(solution)/shard_map/ppermute | solution.py:104
  145.4 1.9 %collective-permute-start.30 = (bf16[128,1792]{1,0:T(8,128)(2,1)S(1)}, bf16[128,1792]{1,0:T(8,128)(2,1)S(1)}, u32[]{:S(2)}, u32[]{:S(2)}) collective-permute-start(bf16[128,1792]{1,0:T(8,128)(2,1)S(1)} %join.7), channel_id=1, source_target_pairs={{0,4},{2,6},{4,8},{6,10},{8,12},{10,14},{1,5},{3,7},{5,9},{7,11},{... | collective-permute-start | bytes 1376264 | tf_op jit(solution)/shard_map/ppermute | solution.py:104
  147.7 5.8 %collective-permute-start.32 = (bf16[128,1792]{1,0:T(8,128)(2,1)S(1)}, bf16[128,1792]{1,0:T(8,128)(2,1)S(1)}, u32[]{:S(2)}, u32[]{:S(2)}) collective-permute-start(bf16[128,1792]{1,0:T(8,128)(2,1)S(1)} %join.8), channel_id=1, source_target_pairs={{0,8},{2,10},{4,12},{6,14},{8,0},{10,2},{12,4},{14,6},{1,9},{3,11}... | collective-permute-start | bytes 1376264 | tf_op jit(solution)/shard_map/ppermute | solution.py:104
  154.5 1.7 collective-permute-start.28
  156.2 7.9 %collective-permute-done.28.came = bf16[96,1792]{1,0:T(8,128)(2,1)S(1)} collective-permute-done((bf16[96,1792]{1,0:T(8,128)(2,1)S(1)}, bf16[96,1792]{1,0:T(8,128)(2,1)S(1)}, u32[]{:S(2)}, u32[]{:S(2)}) %collective-permute-start.28) | collective-permute-done | bytes 344096 | tf_op jit(solution)/shard_map/ppermute | solution.py:104
  164.5 22.2 %collective-permute-done.32 = bf16[128,1792]{1,0:T(8,128)(2,1)S(1)} collective-permute-done((bf16[128,1792]{1,0:T(8,128)(2,1)S(1)}, bf16[128,1792]{1,0:T(8,128)(2,1)S(1)}, u32[]{:S(2)}, u32[]{:S(2)}) %collective-permute-start.32) | collective-permute-done | bytes 458784 | tf_op jit(solution)/shard_map/ppermute | solution.py:104
  186.6 1.1 add_convert_fusion
  (73 shorter events, 12.4 us)
Async XLA Ops:
  7.7 32.4 %collective-permute-start.2 = (bf16[2,1792,512]{2,1,0:T(8,128)(2,1)}, bf16[2,1792,512]{2,1,0:T(8,128)(2,1)}, u32[]{:S(2)}, u32[]{:S(2)}) collective-permute-start(bf16[2,1792,512]{2,1,0:T(8,128)(2,1)} %pad_maximum_fusion), channel_id=1, source_target_pairs={{0,1},{1,0},{2,3},{3,2},{4,5},{5,4},{6,7},{7,6},{8,9},{9,8},{10,11... | collective-permute-start | bytes 11010056 | tf_op jit(solution)/shard_map/ppermute | solution.py:108
  7.7 18.0 %collective-permute-start.4 = (bf16[192,1792]{1,0:T(8,128)(2,1)S(1)}, bf16[192,1792]{1,0:T(8,128)(2,1)}, u32[]{:S(2)}, u32[]{:S(2)}) collective-permute-start(bf16[192,1792]{1,0:T(8,128)(2,1)S(1)} %pick.5), channel_id=1, source_target_pairs={{0,2},{2,0},{4,6},{6,4},{8,10},{10,8},{12,14},{14,12},{1,3},{3,1},... | collective-permute-start | bytes 2064392 | tf_op jit(solution)/shard_map/ppermute | solution.py:104
  9.2 30.0 %collective-permute-start.3 = (bf16[256,1792]{1,0:T(8,128)(2,1)S(1)}, bf16[256,1792]{1,0:T(8,128)(2,1)}, u32[]{:S(2)}, u32[]{:S(2)}) collective-permute-start(bf16[256,1792]{1,0:T(8,128)(2,1)S(1)} %constant_dynamic-update-slice_fusion.both.block), channel_id=1, source_target_pairs={{0,1},{1,0},{2,3},{3,2},{4,5},{5,4},{6,7},{7,6},{8,9},{9,8},{10,11... | collective-permute-start | bytes 2752520 | tf_op jit(solution)/shard_map/ppermute | solution.py:108
  9.4 29.8 %collective-permute-start.1 = (bf16[256,1792]{1,0:T(8,128)(2,1)S(1)}, bf16[256,1792]{1,0:T(8,128)(2,1)S(1)}, u32[]{:S(2)}, u32[]{:S(2)}) collective-permute-start(bf16[256,1792]{1,0:T(8,128)(2,1)S(1)} %constant_dynamic-update-slice_fusion.both.block), channel_id=1, source_target_pairs={{4,0},{6,2},{8,4},{10,6},{12,8},{14,10},{5,1},{7,3},{9,5},{11,7},{... | collective-permute-start | bytes 2752520 | tf_op jit(solution)/shard_map/ppermute | solution.py:104
  11.8 27.4 %collective-permute-start = (bf16[256,1792]{1,0:T(8,128)(2,1)S(1)}, bf16[256,1792]{1,0:T(8,128)(2,1)S(1)}, u32[]{:S(2)}, u32[]{:S(2)}) collective-permute-start(bf16[256,1792]{1,0:T(8,128)(2,1)S(1)} %constant_dynamic-update-slice_fusion.both.block), channel_id=1, source_target_pairs={{0,4},{2,6},{4,8},{6,10},{8,12},{10,14},{1,5},{3,7},{5,9},{7,11},{... | collective-permute-start | bytes 2752520 | tf_op jit(solution)/shard_map/ppermute | solution.py:104
  25.7 13.6 %collective-permute-start.5 = (bf16[192,1792]{1,0:T(8,128)(2,1)}, bf16[192,1792]{1,0:T(8,128)(2,1)S(1)}, u32[]{:S(2)}, u32[]{:S(2)}) collective-permute-start(bf16[192,1792]{1,0:T(8,128)(2,1)} %collective-permute-done.4.slots), channel_id=1, source_target_pairs={{0,1},{1,0},{2,3},{3,2},{4,5},{5,4},{6,7},{7,6},{8,9},{9,8},{10,11... | collective-permute-start | bytes 2064392 | tf_op jit(solution)/shard_map/ppermute | solution.py:108
  26.3 11.3 %all-to-all-start = ((f32[8,2,128]{2,1,0:T(2,128)}), f32[8,2,128]{2,1,0:T(2,128)S(1)}, u32[]{:S(2)}, u32[]{:S(2)}) async-start(f32[8,2,128]{2,1,0:T(2,128)} %bitcast.6), calls=%async_computation | async-start | bytes 16384 | tf_op jit(solution)/shard_map/all_to_all | solution.py:317
  38.4 0.8 copy-start.7
  39.2 0.9 copy-start.5
  40.1 26.1 %collective-permute-start.6 = (bf16[256,1792]{1,0:T(8,128)(2,1)S(1)}, bf16[256,1792]{1,0:T(8,128)(2,1)}, u32[]{:S(2)}, u32[]{:S(2)}) collective-permute-start(bf16[256,1792]{1,0:T(8,128)(2,1)S(1)} %collective-permute-done.both.block), channel_id=1, source_target_pairs={{4,8},{6,10},{8,12},{10,14},{5,9},{7,11},{9,13},{11,15},{20,24},{2... | collective-permute-start | bytes 2752520 | tf_op jit(solution)/shard_map/ppermute | solution.py:104
  43.5 23.2 %collective-permute-start.7 = (bf16[256,1792]{1,0:T(8,128)(2,1)S(1)}, bf16[256,1792]{1,0:T(8,128)(2,1)}, u32[]{:S(2)}, u32[]{:S(2)}) collective-permute-start(bf16[256,1792]{1,0:T(8,128)(2,1)S(1)} %collective-permute-done.1.both.block), channel_id=1, source_target_pairs={{8,4},{10,6},{4,0},{6,2},{9,5},{11,7},{5,1},{7,3},{24,20},{26,22},... | collective-permute-start | bytes 2752520 | tf_op jit(solution)/shard_map/ppermute | solution.py:104
  45.8 20.4 %collective-permute-start.8 = (bf16[192,1792]{1,0:T(8,128)(2,1)S(1)}, bf16[192,1792]{1,0:T(8,128)(2,1)}, u32[]{:S(2)}, u32[]{:S(2)}) collective-permute-start(bf16[192,1792]{1,0:T(8,128)(2,1)S(1)} %pick.6.rest_0_), channel_id=1, source_target_pairs={{4,6},{6,4},{8,10},{10,8},{12,14},{14,12},{5,7},{7,5},{9,11},{11,9... | collective-permute-start | bytes 2064392 | tf_op jit(solution)/shard_map/ppermute | solution.py:104
  48.7 4.5 %copy-start.6 = (bf16[192,1792]{1,0:T(8,128)(2,1)S(1)}, bf16[192,1792]{1,0:T(8,128)(2,1)}, u32[]{:S(2)}) copy-start(bf16[192,1792]{1,0:T(8,128)(2,1)} %copy-done.5) | copy-start | bytes 2064388
  49.0 29.7 %collective-permute-start.14 = (bf16[192,1792]{1,0:T(8,128)(2,1)S(1)}, bf16[192,1792]{1,0:T(8,128)(2,1)S(1)}, u32[]{:S(2)}, u32[]{:S(2)}) collective-permute-start(bf16[192,1792]{1,0:T(8,128)(2,1)S(1)} %pick.7.rest_0_), channel_id=1, source_target_pairs={{0,2},{2,0},{4,6},{6,4},{8,10},{10,8},{1,3},{3,1},{5,7},{7,5},{9,1... | collective-permute-start | bytes 2064392 | tf_op jit(solution)/shard_map/ppermute | solution.py:104
  53.2 2.0 %copy-start = (bf16[1,3584,512]{2,1,0:T(8,128)(2,1)S(1)}, bf16[1,3584,512]{2,1,0:T(8,128)(2,1)}, u32[]{:S(2)}) copy-start(bf16[1,3584,512]{2,1,0:T(8,128)(2,1)} %param.11) | copy-start | bytes 11010052
  55.2 2.0 %copy-start.1 = (bf16[1,3584,512]{2,1,0:T(8,128)(2,1)S(1)}, bf16[1,3584,512]{2,1,0:T(8,128)(2,1)}, u32[]{:S(2)}) copy-start(bf16[1,3584,512]{2,1,0:T(8,128)(2,1)} %param.12) | copy-start | bytes 11010052
  57.3 2.0 %copy-start.2 = (bf16[1,512,3584]{2,1,0:T(8,128)(2,1)S(1)}, bf16[1,512,3584]{2,1,0:T(8,128)(2,1)}, u32[]{:S(2)}) copy-start(bf16[1,512,3584]{2,1,0:T(8,128)(2,1)} %param.13) | copy-start | bytes 11010052
  66.7 13.5 %collective-permute-start.12 = (bf16[224,1024]{1,0:T(8,128)(2,1)S(1)}, bf16[224,1024]{1,0:T(8,128)(2,1)S(1)}, u32[]{:S(2)}, u32[]{:S(2)}) collective-permute-start(bf16[224,1024]{1,0:T(8,128)(2,1)S(1)} %grads.5.own), channel_id=1, source_target_pairs={{0,1},{1,0},{2,3},{3,2},{4,5},{5,4},{6,7},{7,6},{8,9},{9,8},{10,11... | collective-permute-start | bytes 1376264 | tf_op jit(solution)/shard_map/ppermute | solution.py:108
  66.7 14.0 %collective-permute-start.11 = (bf16[192,1792]{1,0:T(8,128)(2,1)}, bf16[192,1792]{1,0:T(8,128)(2,1)S(1)}, u32[]{:S(2)}, u32[]{:S(2)}) collective-permute-start(bf16[192,1792]{1,0:T(8,128)(2,1)} %collective-permute-done.8.slots), channel_id=1, source_target_pairs={{0,1},{1,0},{2,3},{3,2},{4,5},{5,4},{6,7},{7,6},{8,9},{9,8},{10,11... | collective-permute-start | bytes 2064392 | tf_op jit(solution)/shard_map/ppermute | solution.py:108
  67.2 18.9 %collective-permute-start.10 = (bf16[256,1792]{1,0:T(8,128)(2,1)S(1)}, bf16[256,1792]{1,0:T(8,128)(2,1)S(1)}, u32[]{:S(2)}, u32[]{:S(2)}) collective-permute-start(bf16[256,1792]{1,0:T(8,128)(2,1)S(1)} %collective-permute-done.both.block), channel_id=1, source_target_pairs={{0,1},{1,0},{2,3},{3,2},{4,5},{5,4},{6,7},{7,6},{8,9},{9,8},{10,11... | collective-permute-start | bytes 2752520 | tf_op jit(solution)/shard_map/ppermute | solution.py:108
  67.2 22.9 %collective-permute-start.13 = (bf16[256,1792]{1,0:T(8,128)(2,1)S(1)}, bf16[256,1792]{1,0:T(8,128)(2,1)S(1)}, u32[]{:S(2)}, u32[]{:S(2)}) collective-permute-start(bf16[256,1792]{1,0:T(8,128)(2,1)S(1)} %collective-permute-done.1.both.block), channel_id=1, source_target_pairs={{0,1},{1,0},{2,3},{3,2},{4,5},{5,4},{6,7},{7,6},{8,9},{9,8},{10,11... | collective-permute-start | bytes 2752520 | tf_op jit(solution)/shard_map/ppermute | solution.py:108
  78.7 19.9 %collective-permute-start.9 = (bf16[256,1792]{1,0:T(8,128)(2,1)S(1)}, bf16[256,1792]{1,0:T(8,128)(2,1)S(1)}, u32[]{:S(2)}, u32[]{:S(2)}) collective-permute-start(bf16[256,1792]{1,0:T(8,128)(2,1)S(1)} %broadcast_select_fusion.both.block), channel_id=1, source_target_pairs={{8,12},{10,14},{4,0},{6,2},{9,13},{11,15},{5,1},{7,3},{24,28},{26,... | collective-permute-start | bytes 2752520 | tf_op jit(solution)/shard_map/ppermute | solution.py:104
  80.3 9.9 %collective-permute-start.15 = (bf16[192,1792]{1,0:T(8,128)(2,1)S(1)}, bf16[192,1792]{1,0:T(8,128)(2,1)S(1)}, u32[]{:S(2)}, u32[]{:S(2)}) collective-permute-start(bf16[192,1792]{1,0:T(8,128)(2,1)S(1)} %collective-permute-done.14.slots), channel_id=1, source_target_pairs={{0,1},{1,0},{2,3},{3,2},{4,5},{5,4},{6,7},{7,6},{8,9},{9,8},{10,11... | collective-permute-start | bytes 2064392 | tf_op jit(solution)/shard_map/ppermute | solution.py:108
  80.7 5.5 %copy-start.3 = (bf16[1,512,3584]{2,1,0:T(8,128)(2,1)S(1)}, bf16[1,512,3584]{2,1,0:T(8,128)(2,1)}, u32[]{:S(2)}) copy-start(bf16[1,512,3584]{2,1,0:T(8,128)(2,1)} %param.13) | copy-start | bytes 11010052
  80.7 17.9 %collective-permute-start.16 = (bf16[192,1792]{1,0:T(8,128)(2,1)S(1)}, bf16[192,1792]{1,0:T(8,128)(2,1)S(1)}, u32[]{:S(2)}, u32[]{:S(2)}) collective-permute-start(bf16[192,1792]{1,0:T(8,128)(2,1)S(1)} %pick.8.rest_0_), channel_id=1, source_target_pairs={{0,2},{2,0},{4,6},{6,4},{8,10},{10,8},{12,14},{14,12},{1,3},{3,1},... | collective-permute-start | bytes 2064392 | tf_op jit(solution)/shard_map/ppermute | solution.py:104
  98.6 1.8 collective-permute-start.21
  98.6 14.1 %collective-permute-start.18 = (bf16[256,1792]{1,0:T(8,128)(2,1)S(1)}, bf16[256,1792]{1,0:T(8,128)(2,1)S(1)}, u32[]{:S(2)}, u32[]{:S(2)}) collective-permute-start(bf16[256,1792]{1,0:T(8,128)(2,1)S(1)} %broadcast_select_fusion.both.block), channel_id=1, source_target_pairs={{0,1},{1,0},{2,3},{3,2},{4,5},{5,4},{6,7},{7,6},{8,9},{9,8},{10,11... | collective-permute-start | bytes 2752520 | tf_op jit(solution)/shard_map/ppermute | solution.py:108
  99.1 18.4 %collective-permute-start.23 = (bf16[256,1792]{1,0:T(8,128)(2,1)S(1)}, bf16[256,1792]{1,0:T(8,128)(2,1)S(1)}, u32[]{:S(2)}, u32[]{:S(2)}) collective-permute-start(bf16[256,1792]{1,0:T(8,128)(2,1)S(1)} %collective-permute-done.9.both.block), channel_id=1, source_target_pairs={{0,1},{1,0},{2,3},{3,2},{4,5},{5,4},{6,7},{7,6},{8,9},{9,8},{10,11... | collective-permute-start | bytes 2752520 | tf_op jit(solution)/shard_map/ppermute | solution.py:108
  99.1 6.4 %collective-permute-start.20 = (bf16[224,1024]{1,0:T(8,128)(2,1)S(1)}, bf16[224,1024]{1,0:T(8,128)(2,1)S(1)}, u32[]{:S(2)}, u32[]{:S(2)}) collective-permute-start(bf16[224,1024]{1,0:T(8,128)(2,1)S(1)} %grads.7.own), channel_id=1, source_target_pairs={{0,1},{1,0},{2,3},{3,2},{4,5},{5,4},{6,7},{7,6},{8,9},{9,8},{10,11... | collective-permute-start | bytes 1376264 | tf_op jit(solution)/shard_map/ppermute | solution.py:108
  99.6 13.1 %collective-permute-start.19 = (bf16[192,1792]{1,0:T(8,128)(2,1)S(1)}, bf16[192,1792]{1,0:T(8,128)(2,1)S(1)}, u32[]{:S(2)}, u32[]{:S(2)}) collective-permute-start(bf16[192,1792]{1,0:T(8,128)(2,1)S(1)} %collective-permute-done.16.slots), channel_id=1, source_target_pairs={{0,1},{1,0},{2,3},{3,2},{4,5},{5,4},{6,7},{7,6},{8,9},{9,8},{10,11... | collective-permute-start | bytes 2064392 | tf_op jit(solution)/shard_map/ppermute | solution.py:108
  100.4 15.2 %collective-permute-start.17 = (bf16[192,1792]{1,0:T(8,128)(2,1)S(1)}, bf16[192,1792]{1,0:T(8,128)(2,1)S(1)}, u32[]{:S(2)}, u32[]{:S(2)}) collective-permute-start(bf16[192,1792]{1,0:T(8,128)(2,1)S(1)} %pick.9.rest_0_), channel_id=1, source_target_pairs={{0,2},{2,0},{12,14},{14,12},{1,3},{3,1},{13,15},{15,13},{16,18},{1... | collective-permute-start | bytes 2064392 | tf_op jit(solution)/shard_map/ppermute | solution.py:104
  105.5 12.0 %collective-permute-start.22 = (bf16[96,1792]{1,0:T(8,128)(2,1)S(1)}, bf16[96,1792]{1,0:T(8,128)(2,1)S(1)}, u32[]{:S(2)}, u32[]{:S(2)}) collective-permute-start(bf16[96,1792]{1,0:T(8,128)(2,1)S(1)} %get-tuple-element.68), channel_id=1, source_target_pairs={{4,6},{6,4},{8,10},{10,8},{12,14},{14,12},{5,7},{7,5},{9,11},{11,9... | collective-permute-start | bytes 1032200 | tf_op jit(solution)/shard_map/ppermute | solution.py:104
  117.5 7.5 %collective-permute-start.26 = (bf16[192,1792]{1,0:T(8,128)(2,1)S(1)}, bf16[192,1792]{1,0:T(8,128)(2,1)S(1)}, u32[]{:S(2)}, u32[]{:S(2)}) collective-permute-start(bf16[192,1792]{1,0:T(8,128)(2,1)S(1)} %collective-permute-done.17.slots), channel_id=1, source_target_pairs={{0,1},{1,0},{2,3},{3,2},{4,5},{5,4},{6,7},{7,6},{8,9},{9,8},{10,11... | collective-permute-start | bytes 2064392 | tf_op jit(solution)/shard_map/ppermute | solution.py:108
  117.5 3.1 %collective-permute-start.25 = (bf16[224,1024]{1,0:T(8,128)(2,1)S(1)}, bf16[224,1024]{1,0:T(8,128)(2,1)S(1)}, u32[]{:S(2)}, u32[]{:S(2)}) collective-permute-start(bf16[224,1024]{1,0:T(8,128)(2,1)S(1)} %grads.8.own), channel_id=1, source_target_pairs={{0,1},{1,0},{2,3},{3,2},{4,5},{5,4},{6,7},{7,6},{8,9},{9,8},{10,11... | collective-permute-start | bytes 1376264 | tf_op jit(solution)/shard_map/ppermute | solution.py:108
  118.0 11.9 %collective-permute-start.24 = (bf16[96,1792]{1,0:T(8,128)(2,1)S(1)}, bf16[96,1792]{1,0:T(8,128)(2,1)S(1)}, u32[]{:S(2)}, u32[]{:S(2)}) collective-permute-start(bf16[96,1792]{1,0:T(8,128)(2,1)S(1)} %get-tuple-element.70), channel_id=1, source_target_pairs={{0,2},{2,0},{4,6},{6,4},{8,10},{10,8},{1,3},{3,1},{5,7},{7,5},{9,1... | collective-permute-start | bytes 1032200 | tf_op jit(solution)/shard_map/ppermute | solution.py:104
  129.9 1.8 collective-permute-start.27
  129.9 17.4 %collective-permute-start.31 = (bf16[96,1792]{1,0:T(8,128)(2,1)S(1)}, bf16[96,1792]{1,0:T(8,128)(2,1)S(1)}, u32[]{:S(2)}, u32[]{:S(2)}) collective-permute-start(bf16[96,1792]{1,0:T(8,128)(2,1)S(1)} %get-tuple-element.83), channel_id=1, source_target_pairs={{0,2},{2,0},{4,6},{6,4},{8,10},{10,8},{12,14},{14,12},{1,3},{3,1},... | collective-permute-start | bytes 1032200 | tf_op jit(solution)/shard_map/ppermute | solution.py:104
  136.1 28.0 %copy-start.4 = (bf16[128,1792]{1,0:T(8,128)(2,1)S(1)}, bf16[128,1792]{1,0:T(8,128)(2,1)}, u32[]{:S(2)}) copy-start(bf16[128,1792]{1,0:T(8,128)(2,1)} %rest_0_.1) | copy-start | bytes 1376260
  136.1 17.4 %collective-permute-start.33 = (bf16[96,1792]{1,0:T(8,128)(2,1)S(1)}, bf16[96,1792]{1,0:T(8,128)(2,1)S(1)}, u32[]{:S(2)}, u32[]{:S(2)}) collective-permute-start(bf16[96,1792]{1,0:T(8,128)(2,1)S(1)} %get-tuple-element.84), channel_id=1, source_target_pairs={{0,2},{2,0},{12,14},{14,12},{1,3},{3,1},{13,15},{15,13},{16,18},{1... | collective-permute-start | bytes 1032200 | tf_op jit(solution)/shard_map/ppermute | solution.py:104
  137.3 27.2 %collective-permute-start.29 = (bf16[128,1792]{1,0:T(8,128)(2,1)S(1)}, bf16[128,1792]{1,0:T(8,128)(2,1)S(1)}, u32[]{:S(2)}, u32[]{:S(2)}) collective-permute-start(bf16[128,1792]{1,0:T(8,128)(2,1)S(1)} %join.6), channel_id=1, source_target_pairs={{4,0},{6,2},{8,4},{10,6},{12,8},{14,10},{5,1},{7,3},{9,5},{11,7},{... | collective-permute-start | bytes 1376264 | tf_op jit(solution)/shard_map/ppermute | solution.py:104
  145.4 19.1 %collective-permute-start.30 = (bf16[128,1792]{1,0:T(8,128)(2,1)S(1)}, bf16[128,1792]{1,0:T(8,128)(2,1)S(1)}, u32[]{:S(2)}, u32[]{:S(2)}) collective-permute-start(bf16[128,1792]{1,0:T(8,128)(2,1)S(1)} %join.7), channel_id=1, source_target_pairs={{0,4},{2,6},{4,8},{6,10},{8,12},{10,14},{1,5},{3,7},{5,9},{7,11},{... | collective-permute-start | bytes 1376264 | tf_op jit(solution)/shard_map/ppermute | solution.py:104
  147.7 39.0 %collective-permute-start.32 = (bf16[128,1792]{1,0:T(8,128)(2,1)S(1)}, bf16[128,1792]{1,0:T(8,128)(2,1)S(1)}, u32[]{:S(2)}, u32[]{:S(2)}) collective-permute-start(bf16[128,1792]{1,0:T(8,128)(2,1)S(1)} %join.8), channel_id=1, source_target_pairs={{0,8},{2,10},{4,12},{6,14},{8,0},{10,2},{12,4},{14,6},{1,9},{3,11}... | collective-permute-start | bytes 1376264 | tf_op jit(solution)/shard_map/ppermute | solution.py:104
  153.8 32.8 %collective-permute-start.34 = (bf16[128,1792]{1,0:T(8,128)(2,1)S(1)}, bf16[128,1792]{1,0:T(8,128)(2,1)S(1)}, u32[]{:S(2)}, u32[]{:S(2)}) collective-permute-start(bf16[128,1792]{1,0:T(8,128)(2,1)S(1)} %join.9), channel_id=1, source_target_pairs={{0,12},{2,14},{12,0},{14,2},{1,13},{3,15},{13,1},{15,3},{16,28},{1... | collective-permute-start | bytes 1376264 | tf_op jit(solution)/shard_map/ppermute | solution.py:104
  154.5 9.6 %collective-permute-start.28 = (bf16[96,1792]{1,0:T(8,128)(2,1)S(1)}, bf16[96,1792]{1,0:T(8,128)(2,1)S(1)}, u32[]{:S(2)}, u32[]{:S(2)}) collective-permute-start(bf16[96,1792]{1,0:T(8,128)(2,1)S(1)} %get-tuple-element.79), channel_id=1, source_target_pairs={{0,2},{2,0},{4,6},{6,4},{8,10},{10,8},{12,14},{14,12},{1,3},{3,1},... | collective-permute-start | bytes 1032200 | tf_op jit(solution)/shard_map/ppermute | solution.py:104

commit v3 on v2

--- a/solution.py
+++ b/solution.py
@@ -135,103 +135,153 @@
     return jnp.where(slots == place, 1.0, 0.0).astype(F32)
 
 
-def routes_kernel(capacity, at, routes, place_out, weight_out):
-    z, y = at[0], at[1]
-    first = y == 0
-    tokens = routes.shape[-1]
-    sent, dense, slots = [], [], []
-    for where in (z, z + 3, z + 1, z ^ 2, 3 - z):
-        where = lax.rem(where, 4)
-        mine, theirs = routes[2 * where + y], routes[2 * where + 1 - y]
-        dense.append(jnp.where(first, mine[0:1], mine[1:2]))
-        sent.append(jnp.where(first, mine[1:2], mine[0:1]))
-        slots.append(jnp.where(first, theirs[0:1], theirs[1:2]))
-    pad = [jnp.zeros((16 - 2 * SLOTS, tokens), F32)]
-    place = places_of(jnp.concatenate(sent + slots + pad, axis=0))
+def stack_kernel(feat, cot, table, out):
+    tokens, half = feat.shape
+    out[:tokens] = feat[...]
+    out[tokens : 2 * tokens] = cot[...]
+    value = table[...]
+    high = value.astype(BF).astype(F32)
+    middle = (value - high).astype(BF).astype(F32)
+    low = value - high - middle
+    upper = jnp.concatenate([high, low], axis=1)
+    lower = jnp.concatenate([middle, jnp.zeros_like(low)], axis=1)
+    rows = jnp.concatenate([upper, lower], axis=0)
+    rest = jnp.zeros((rows.shape[0], half - rows.shape[1]), F32)
+    out[2 * tokens :] = jnp.concatenate([rows, rest], axis=1).astype(BF)
+
+
+def stacked(feat, cot, table):
+    tokens, half = feat.shape
+    return pl.pallas_call(
+        stack_kernel,
+        out_shape=jax.ShapeDtypeStruct((2 * tokens + 2 * table.shape[0], half), BF),
+        in_specs=[ON_CHIP] * 3,
+        out_specs=ON_CHIP,
+        compiler_params=params(),
+        cost_estimate=SMALL,
+        name="stack",
+    )(feat, cot, table)
+
+
+def route_row(ref, first, height, tokens, expert):
+    rows = ref[first : first + height, : 2 * tokens].astype(F32)
+    count = rows.shape[0] // 2
+    table = rows[:count, :tokens] + rows[count:, :tokens] + rows[:count, tokens:]
+    chosen = lax.broadcasted_iota(jnp.int32, table.shape, 0) == expert
+    return jnp.sum(jnp.where(chosen, table, 0.0), axis=0, keepdims=True)
+
+
+def place_of(weights):
+    rows = jnp.broadcast_to(weights, (16, weights.shape[1]))
+    return places_of(rows)[:1]
+
+
+def pick_kernel(capacity, tokens, me, both, *rest):
+    out, place_out = rest[-2:]
+    place = place_of(
+        route_row(both, 2 * tokens, both.shape[0] - 2 * tokens, tokens, me[0] ^ 1)
+    )
+    place_out[...] = place
+    pick = pick_of(place, capacity).astype(BF)
+    out[:capacity] = dot(pick, both[:tokens]).astype(BF)
+    out[capacity : 2 * capacity] = dot(pick, both[tokens : 2 * tokens]).astype(BF)
+    out[2 * capacity :] = both[2 * tokens :]
+
+
+def picked_rows(me, both, tokens, capacity, after=()):
+    table = both.shape[0] - 2 * tokens
+    return pl.pallas_call(
+        functools.partial(pick_kernel, capacity, tokens),
+        out_shape=[
+            jax.ShapeDtypeStruct((2 * capacity + table, both.shape[1]), BF),
+            jax.ShapeDtypeStruct((1, tokens), F32),
+        ],
+        in_specs=[ON_CHIP_SCALARS, ON_CHIP] + [ANYWHERE] * len(after),
+        out_specs=[ON_CHIP] * 2,
+        compiler_params=params(),
+        cost_estimate=SMALL,
+        name="pick",
+    )(me, both, *after)
+
+
+def grads_kernel(capacity, tokens, side, me, block, block_far, gate, up, down, *rest):
+    out = rest[-1]
+    half, ff = block.shape[1], gate.shape[1]
+    table = (block.shape[0] - 2 * tokens - 2 * capacity) // 2
+    slots = 2 * tokens + table
+    weights = route_row(block, 2 * tokens, table, tokens, me[0])
     same = lax.broadcasted_iota(jnp.int32, (tokens, tokens), 0) == lax.broadcasted_iota(
         jnp.int32, (tokens, tokens), 1
     )
-    for i in range(SLOTS):
-        place_out[i] = place[i : i + 1]
-        weight_out[i, :tokens] = jnp.sum(jnp.where(same, dense[i], 0.0), axis=1, keepdims=True)
-        pick = pick_of(place[SLOTS + i : SLOTS + i + 1], capacity)
-        weight_out[i, tokens:] = jnp.sum(pick * slots[i], axis=1, keepdims=True)
-
-
-def route_tables(at, routes, capacity):
-    tokens = routes.shape[-1]
-    return pl.pallas_call(
-        functools.partial(routes_kernel, capacity),
-        out_shape=[
-            jax.ShapeDtypeStruct((SLOTS, 1, tokens), F32),
-            jax.ShapeDtypeStruct((SLOTS, tokens + capacity, 1), F32),
-        ],
-        in_specs=[pl.BlockSpec(memory_space=pltpu.SMEM), pl.BlockSpec(memory_space=pltpu.VMEM)],
-        out_specs=[pl.BlockSpec(memory_space=pltpu.VMEM)] * 2,
-        compiler_params=params(),
-        cost_estimate=SMALL,
-        name="routes",
-    )(at, routes)
-
-
-def pick_kernel(capacity, place, both, *rest):
-    out = rest[-1]
-    tokens = place.shape[-1]
-    pick = pick_of(place[...], capacity).astype(BF)
-    out[:capacity] = dot(pick, both[:tokens]).astype(BF)
-    out[capacity:] = dot(pick, both[tokens:]).astype(BF)
-
-
-def picked_rows(place, both, capacity, after=()):
-    return pl.pallas_call(
-        functools.partial(pick_kernel, capacity),
-        out_shape=jax.ShapeDtypeStruct((2 * capacity, both.shape[1]), BF),
-        in_specs=[pl.BlockSpec(memory_space=pltpu.VMEM)] * 2 + [ANYWHERE] * len(after),
-        out_specs=pl.BlockSpec(memory_space=pltpu.VMEM),
-        compiler_params=params(),
-        cost_estimate=SMALL,
-        name="pick",
-    )(place, both, *after)
-
-
-def grads_kernel(side, block, block_far, slots, slots_far, weight, gate, up, down, *rest):
-    out = rest[-1]
-    capacity, tokens, half = slots.shape[0] // 2, block.shape[0] // 2, block.shape[1]
-    ff = gate.shape[1]
+    dense_weight = jnp.sum(jnp.where(same, weights, 0.0), axis=1, keepdims=True)
+    weights = route_row(block, slots + 2 * capacity, table, tokens, me[0])
+    slot_weight = jnp.sum(
+        pick_of(place_of(weights), capacity) * weights, axis=1, keepdims=True
+    )
+    weight = jnp.concatenate([dense_weight, slot_weight], axis=0)
     near = pl.ds(pl.multiple_of(side[0] * half, 256), half)
     far = pl.ds(pl.multiple_of((1 - side[0]) * half, 256), half)
 
-    def feats(block, slots):
-        return jnp.concatenate([block[:tokens], slots[:capacity]], axis=0)
-
-    def cots(block, slots):
-        return jnp.concatenate([block[tokens:], slots[capacity:]], axis=0)
+    def feats(block):
+        return jnp.concatenate([block[:tokens], block[slots : slots + capacity]], axis=0)
+
+    def cots(block):
+        second = slots + capacity
+        return jnp.concatenate(
+            [block[tokens : 2 * tokens], block[second : second + capacity]], axis=0
+        )
 
     width = ff // 2
     for at in range(0, ff, width):
         cols = slice(at, at + width)
-        rows, rows_far = feats(block, slots), feats(block_far, slots_far)
+        rows, rows_far = feats(block), feats(block_far)
         gate_pre = dot(rows, gate[near, cols]) + dot(rows_far, gate[far, cols])
         up_pre = dot(rows, up[near, cols]) + dot(rows_far, up[far, cols])
-        rows, rows_far = cots(block, slots), cots(block_far, slots_far)
+        rows, rows_far = cots(block), cots(block_far)
         hidden = dot_t(rows, down[cols, near]) + dot_t(rows_far, down[cols, far])
-        hidden = hidden * weight[...]
+        hidden = hidden * weight
         sig = jax.nn.sigmoid(gate_pre)
         out[:, cols] = (hidden * up_pre * sig * (1.0 + gate_pre * (1.0 - sig))).astype(BF)
         out[:, ff + at : ff + at + width] = (hidden * gate_pre * sig).astype(BF)
 
 
-def grads_of(side, block, slots, weight, mats, after=()):
-    rows = (block[0].shape[0] + slots[0].shape[0]) // 2
-    return pl.pallas_call(
-        grads_kernel,
-        out_shape=jax.ShapeDtypeStruct((rows, 2 * mats[0].shape[1]), BF),
-        in_specs=[ON_CHIP_SCALARS] + [ON_CHIP] * 8 + [ANYWHERE] * len(after),
+def grads_of(side, me, block, mats, tokens, capacity, after=()):
+    return pl.pallas_call(
+        functools.partial(grads_kernel, capacity, tokens),
+        out_shape=jax.ShapeDtypeStruct((tokens + capacity, 2 * mats[0].shape[1]), BF),
+        in_specs=[ON_CHIP_SCALARS] * 2 + [ON_CHIP] * 5 + [ANYWHERE] * len(after),
         out_specs=ON_CHIP,
         compiler_params=params(),
         cost_estimate=SMALL,
         name="grads",
-    )(side, *block, *slots, weight, *mats, *after)
+    )(side, me, *block, *mats, *after)
+
+
+def keep_kernel(side, gate, up, out, sems):
+    half = out.shape[1]
+    near = pl.ds(pl.multiple_of(side[0] * half, 256), half)
+    copies = [
+        pltpu.make_async_copy(ref.at[near], out.at[i], sems.at[i])
+        for i, ref in enumerate((gate, up))
+    ]
+    for copy in copies:
+        copy.start()
+    for copy in copies:
+        copy.wait()
+
+
+def kept(side, gate, up):
+    rows, ff = gate.shape
+    return pl.pallas_call(
+        keep_kernel,
+        out_shape=jax.ShapeDtypeStruct((2, rows // 2, ff), BF),
+        in_specs=[ON_CHIP_SCALARS] + [ANYWHERE] * 2,
+        out_specs=ON_CHIP,
+        scratch_shapes=[pltpu.SemaphoreType.DMA((2,))],
+        compiler_params=params(),
+        cost_estimate=SMALL,
+        name="keep",
+    )(side, gate, up)
 
 
 def back_kernel(side, own, other, gate, up, far, *rest):
@@ -294,14 +344,26 @@
     experts = lax.axis_size("node")
     top_count = expert_ids.shape[1]
     capacity = 3 * tok_rows * top_count // (2 * experts)
-    me = lax.axis_index("node")
-    z, y = me // 2, me % 2
-    at = jnp.stack([z, y]).astype(jnp.int32)
+    me = lax.axis_index("node").astype(jnp.int32)
+    z, me1 = me // 2, me[None]
     side = lax.axis_index("local").astype(jnp.int32)
     side1 = side[None]
-
-    both = jnp.concatenate([tokens, out_grad], axis=0)
-    b_up, b_down = move(both, UP1), move(both, DOWN1)
+    gate, up, down = w_gate[0], w_up[0], w_down[0]
+
+    def late(value, *before):
+        return lax.optimization_barrier((value, *before))[0]
+
+    def halves(block):
+        return block, swap(block)
+
+    def rows_across(block, after=()):
+        return picked_rows(me1, block, tok_rows, capacity, after)
+
+    def grads(block, after=()):
+        return grads_of(side1, me1, block, (gate, up, down), tok_rows, capacity, after)
+
+    def joint(block, slots):
+        return halves(jnp.concatenate([block, slots], axis=0))
 
     table = jnp.sum(
         jnp.where(
@@ -311,85 +373,61 @@
         ),
         axis=2,
     )
-    own_place = places_of(lax.dynamic_slice_in_dim(table, me ^ 1, 1, 0))
-    own_rows = picked_rows(own_place, both, capacity)
-    pairs = table.reshape(experts // 2, 1, 2, tok_rows)
-    routes = lax.all_to_all(
-        jnp.broadcast_to(pairs, (experts // 2, 2, 2, tok_rows)).reshape(experts, 2, tok_rows),
-        "node",
-        split_axis=0,
-        concat_axis=0,
-        tiled=True,
-    )
-    places, weights = route_tables(at, routes, capacity)
-
-    gate, up, down = w_gate[0], w_up[0], w_down[0]
-    gate_late, up_late, own_rows = lax.optimization_barrier((gate, up, own_rows))
-    other = lambda mat: lax.dynamic_slice_in_dim(mat, (1 - side) * half, half, 0)
-    far_mats = swap(jnp.stack([other(gate_late), other(up_late)]))
-
-    def halves(block):
-        return block, swap(block)
-
-    def late(value, *before):
-        return lax.optimization_barrier((value, *before))[0]
-
-    def back(own, other, after=()):
-        return back_of(side1, own, other, (gate, up), far_mats, tok_rows, after)
-
-    def grads(index, block, slots, after=()):
-        return grads_of(side1, block, slots, weights[index], (gate, up, down), after)
-
+    both = stacked(tokens, out_grad, table)
+    b_up, b_down = move(both, UP1), move(both, DOWN1)
+    own_rows, place0 = rows_across(both)
     own_y = move(own_rows, Y_ALL)
-    own_halves, own_slots = halves(both), halves(own_y)
-
-    b_up, b_down, places, *_ = lax.optimization_barrier(
-        (b_up, b_down, places, far_mats, own_halves, own_slots)
-    )
+    gate_far, up_far = swap(gate), swap(up)
+
+    def back(own, after=()):
+        return back_of(side1, *own, (gate, up), far_mats, tok_rows, after)
+
+    b_up, b_down, own_y, gate_far, up_far = lax.optimization_barrier(
+        (b_up, b_down, own_y, gate_far, up_far)
+    )
+    far_mats = kept(side1, gate_far, up_far)
     up_two, down_two = move(b_up, UP2), move(b_down, DOWN2)
-    up_rows = picked_rows(places[1], b_up, capacity)
+    up_rows, place1 = rows_across(b_up)
     up_y = move(up_rows, Y_UP)
-    down_rows = picked_rows(places[2], b_down, capacity, (up_rows,))
-    down_y = move(down_rows, Y_DOWN)
-    grads0 = grads(0, own_halves, own_slots, (down_rows,))
+    grads0 = grads(joint(both, own_y), (up_rows, far_mats))
 
     up_two, down_two, grads0, up_y = lax.optimization_barrier((up_two, down_two, grads0, up_y))
     b_two = jnp.where(z >= 2, up_two, down_two)
     b_far = move(b_two, ENDS)
-    two_rows = picked_rows(places[3], b_two, capacity)
+    down_rows, place2 = rows_across(b_down, (b_two,))
+    down_y = move(down_rows, Y_DOWN)
+    two_rows, place3 = rows_across(b_two, (down_rows,))
     two_y = move(two_rows, Y_ALL)
-    dense0, slots0 = back(grads0, swap(grads0), (two_rows,))
-    grads1 = grads(1, halves(late(b_up, up_two)), halves(up_y), (dense0,))
-    grads2 = grads(2, halves(late(b_down, up_two)), halves(down_y), (grads1,))
-
-    b_far, grads1, grads2, slots0, two_y = lax.optimization_barrier(
-        (b_far, grads1, grads2, slots0, two_y)
-    )
-    far_rows = picked_rows(places[4], b_far, capacity)
+    dense0, slots0 = back(halves(grads0), (two_rows,))
+    grads1 = grads(joint(b_up, up_y), (dense0,))
+
+    b_far, slots0, grads1, two_y = lax.optimization_barrier((b_far, slots0, grads1, two_y))
+    far_rows, place4 = rows_across(b_far)
     far_y = move(far_rows, Y_ENDS)
-    dense1, slots1 = back(grads1, swap(grads1), (far_rows,))
+    dense1, slots1 = back(halves(late(grads1, far_rows)))
+    grads3 = grads(joint(b_two, late(two_y, far_rows)), (dense1,))
+    grads2 = grads(joint(b_down, late(down_y, far_rows)), (grads3,))
+
     came1 = move(slots1, Y_UP)
-    dense2, slots2 = back(grads2, swap(grads2), (dense1,))
-    grads3 = grads(3, halves(b_two), halves(two_y), (dense2,))
-    far_halves = halves(b_far)
-
-    far_y, grads3, came1, far_halves, dense2, slots2 = lax.optimization_barrier(
-        (far_y, grads3, came1, far_halves, dense2, slots2)
-    )
+    join1 = joined(place1, came1, dense1, after=(grads2,))
+
+    far_y, join1, grads2 = lax.optimization_barrier((far_y, join1, grads2))
+    home1 = move(join1, DOWN1)
+    dense3, slots3 = back(halves(late(grads3, far_y)))
+    came3 = move(slots3, Y_ALL)
+    grads4 = grads(joint(b_far, far_y), (dense3,))
+    dense2, slots2 = back(halves(grads2), (grads4,))
     came2 = move(slots2, Y_DOWN)
-    home1 = move(joined(places[1], came1, dense1), DOWN1)
-    dense3, slots3 = back(grads3, swap(grads3))
-    grads4 = grads(4, far_halves, halves(far_y), (dense3,))
-    came2, slots3, grads4 = lax.optimization_barrier((came2, slots3, grads4))
-    came3 = move(slots3, Y_ALL)
-    home2 = move(joined(places[2], came2, dense2), UP1)
-    dense4, slots4 = back(grads4, swap(grads4))
+    dense4, slots4 = back(halves(grads4), (dense2, home1))
     came4 = move(slots4, Y_ENDS)
-    home3 = move(joined(places[3], came3, dense3), SKIP)
+    join3 = joined(place3, came3, dense3, after=(dense4,))
+    home3 = move(join3, SKIP)
+    join2 = joined(place2, came2, dense2, after=(join3,))
+    home2 = move(join2, UP1)
+    home4 = move(joined(place4, came4, dense4, after=(join2,)), FAR)
     came0 = move(late(slots0, dense4), Y_ALL)
-    own = joined(own_place, came0, dense0, (out_grad,), F32)
-    summed = own + home1.astype(F32)
-    home4 = move(joined(places[4], came4, dense4), FAR)
+    join0 = joined(place0, came0, dense0, (out_grad, home1), F32, (join2,))
+    summed = join0
     for value in (home2, home3, home4):
         summed = summed + value.astype(F32)
     return summed.astype(BF)

time: 190 us -> 187 us (0.984)
  waiting for transfers between devices: 69.2 us -> 87.2 us
  starting transfers between devices: 55.4 us -> 44.2 us
  Pallas kernels: 43.2 us -> 37.6 us
    ppermute x19, waiting for transfers between devices: 62.7 us -> 83.8 us  [move(): return lax.ppermute(value, 'node', pairs)]
    pallas_call x5, Pallas kernels: 22.3 us -> 11.6 us  [back_of(): pl.pallas_call(back_kernel, out_shape=[jax.ShapeDtypeStruct((tokens, half...]
    all_to_all x1 -> x0, starting transfers between devices: 6.28 us -> none  [lines(): lax.all_to_all(jnp.broadcast_to(pairs, (experts // 2, 2, 2, tok_rows)).re...]
    pallas_call x11 -> x12, Pallas kernels: 19.3 us -> 24.3 us  [the longest x5 17.3 us: grads_of(): pl.pallas_call(functools.partial(grads_kernel, capacity, tokens), out_sha...]
    all_to_all x1 -> x0, waiting for transfers between devices: 4.94 us -> none  [lines(): lax.all_to_all(jnp.broadcast_to(pairs, (experts // 2, 2, 2, tok_rows)).re...]
    ppermute x19, starting transfers between devices: 46.3 us -> 42 us  [move(): return lax.ppermute(value, 'node', pairs)]
    another operation x1 -> x0, local copies, waits for them, and re-layouts: 2.3 us -> none  [lines(): far_mats = swap(jnp.stack([other(gate_late), other(up_late)]))]
    another operation x2 -> x0, other arithmetic: 2.17 us -> none  [the longest x1 2.1 us: lines(): far_mats = swap(jnp.stack([other(gate_late), other(up_late)]))]
  transfers between devices with their start and end apart: 36 -> 31, of which waited for: 12 -> 14; matrix products, arithmetic and copies ran while one was open for 2% -> 4% of each run, Pallas kernels for 23% -> 20%
where the time goes in v3:
time: 187 us; the launch traced here: 185 us
  waiting for transfers between devices  87.2 us (47%)
  starting transfers between devices  44.2 us (24%)
  Pallas kernels  37.6 us (20%)
  local copies, waits for them, and re-layouts  12.6 us (7%)
  other arithmetic  3.38 us (2%)
    ppermute x19, waiting for transfers between devices, move(): return lax.ppermute(value, 'node', pairs)  83.8 us
    ppermute x19, starting transfers between devices, move(): return lax.ppermute(value, 'node', pairs)  42 us
    pallas_call x5, Pallas kernels, grads_of(): pl.pallas_call(functools.partial(grads_kernel, capacity, tokens), out_sha...  17.3 us
    pallas_call x5, Pallas kernels, back_of(): pl.pallas_call(back_kernel, out_shape=[jax.ShapeDtypeStruct((tokens, half...  11.6 us
    unnamed x27, local copies, waits for them, and re-layouts  10.4 us
    pallas_call x5, Pallas kernels, picked_rows(): pl.pallas_call(functools.partial(pick_kernel, capacity, tokens), out_shap...  4.69 us
  transfers between devices with their start and end apart: 31, of which 14 were waited for; matrix products, arithmetic and copies ran while one was open for 4% of the time, Pallas kernels for 20%

profile of v3, /device:TPU:8, one launch (start us, length us, event | category | flops | bytes accessed | tf_op | source)
XLA Modules:
  0.0 185.5 jit_solution(1382477672494781425)
XLA Ops:
  1.2 1.0 copy-done.9
  2.2 1.0 copy-done.11
  3.3 3.5 %collective-permute-start = (bf16[272,1792]{1,0:T(8,128)(2,1)S(1)}, bf16[272,1792]{1,0:T(8,128)(2,1)}, u32[]{:S(2)}, u32[]{:S(2)}) collective-permute-start(bf16[272,1792]{1,0:T(8,128)(2,1)S(1)} %stack.1.both), channel_id=1, source_target_pairs={{0,4},{2,6},{4,8},{6,10},{8,12},{10,14},{1,5},{3,7},{5,9},{7,11},{... | collective-permute-start | bytes 2924552 | tf_op jit(solution)/shard_map/ppermute | solution.py:104
  6.8 3.4 %collective-permute-start.1 = (bf16[272,1792]{1,0:T(8,128)(2,1)S(1)}, bf16[272,1792]{1,0:T(8,128)(2,1)}, u32[]{:S(2)}, u32[]{:S(2)}) collective-permute-start(bf16[272,1792]{1,0:T(8,128)(2,1)S(1)} %stack.1.both), channel_id=1, source_target_pairs={{4,0},{6,2},{8,4},{10,6},{12,8},{14,10},{5,1},{7,3},{9,5},{11,7},{... | collective-permute-start | bytes 2924552 | tf_op jit(solution)/shard_map/ppermute | solution.py:104
  10.7 1.6 collective-permute-start.2
  12.3 16.5 %collective-permute-done.2 = bf16[208,1792]{1,0:T(8,128)(2,1)S(1)} collective-permute-done((bf16[208,1792]{1,0:T(8,128)(2,1)S(1)}, bf16[208,1792]{1,0:T(8,128)(2,1)S(1)}, u32[]{:S(2)}, u32[]{:S(2)}) %collective-permute-start.2) | collective-permute-done | bytes 745504 | tf_op jit(solution)/shard_map/ppermute | solution.py:104
  28.8 3.2 %collective-permute-done.1.both = bf16[272,1792]{1,0:T(8,128)(2,1)} collective-permute-done((bf16[272,1792]{1,0:T(8,128)(2,1)S(1)}, bf16[272,1792]{1,0:T(8,128)(2,1)}, u32[]{:S(2)}, u32[]{:S(2)}) %collective-permute-start.1) | collective-permute-done | bytes 974880 | tf_op jit(solution)/shard_map/ppermute | solution.py:104
  32.2 4.4 %collective-permute-start.5 = (bf16[272,1792]{1,0:T(8,128)(2,1)}, bf16[272,1792]{1,0:T(8,128)(2,1)}, u32[]{:S(2)}, u32[]{:S(2)}) collective-permute-start(bf16[272,1792]{1,0:T(8,128)(2,1)} %collective-permute-done.both), channel_id=1, source_target_pairs={{4,8},{6,10},{8,12},{10,14},{5,9},{7,11},{9,13},{11,15},{20,24},{2... | collective-permute-start | bytes 2924552 | tf_op jit(solution)/shard_map/ppermute | solution.py:104
  36.7 1.9 %collective-permute-start.6 = (bf16[272,1792]{1,0:T(8,128)(2,1)}, bf16[272,1792]{1,0:T(8,128)(2,1)}, u32[]{:S(2)}, u32[]{:S(2)}) collective-permute-start(bf16[272,1792]{1,0:T(8,128)(2,1)} %collective-permute-done.1.both), channel_id=1, source_target_pairs={{8,4},{10,6},{4,0},{6,2},{9,5},{11,7},{5,1},{7,3},{24,20},{26,22},... | collective-permute-start | bytes 2924552 | tf_op jit(solution)/shard_map/ppermute | solution.py:104
  38.6 1.7 pick.6
  40.3 3.4 %collective-permute-start.8 = (bf16[208,1792]{1,0:T(8,128)(2,1)S(1)}, bf16[208,1792]{1,0:T(8,128)(2,1)}, u32[]{:S(2)}, u32[]{:S(2)}) collective-permute-start(bf16[208,1792]{1,0:T(8,128)(2,1)S(1)} %get-tuple-element.51.rest_0_), channel_id=1, source_target_pairs={{4,6},{6,4},{8,10},{10,8},{12,14},{14,12},{5,7},{7,5},{9,11},{11,9... | collective-permute-start | bytes 2236424 | tf_op jit(solution)/shard_map/ppermute | solution.py:104
  43.7 2.2 %keep.1.rest_1_.far = bf16[2,1792,512]{2,1,0:T(8,128)(2,1)S(1)} custom-call(s32[1]{0:T(128)} %bitcast.3.side, bf16[3584,512]{1,0:T(8,128)(2,1)} %collective-permute-done.3.gate, bf16[3584,512]{1,0:T(8,128)(2,1)} %collective-permute-done.4.up), custom_call_target="tpu_custom_call" | custom-call | flops 1024 | bytes 1024 | tf_op jit(solution)/shard_map/keep/pallas_call | solution.py:275
  46.0 4.3 %constant_dynamic-update-slice_fusion.1 = bf16[480,1792]{1,0:T(8,128)(2,1)} fusion(bf16[272,1792]{1,0:T(8,128)(2,1)} %collective-permute-done.both), kind=kLoop, calls=%fused_computation.7 | loop fusion | bytes 1949696
  51.0 4.3 %grads.5.own = bf16[224,1024]{1,0:T(8,128)(2,1)S(1)} custom-call(s32[1]{0:T(128)} %bitcast.3.side, s32[1]{0:T(128)} %bitcast.me, bf16[480,1792]{1,0:T(8,128)(2,1)S(1)} %pad_maximum_fusion.block, bf16[480,1792]{1,0:T(8,128)(2,1)} %collective-permute-done.7.block_far, bf16[3584,512]{1,0:T(8,128)(2,1)S(1)} %bitcast.6, bf16[3584,512]{1,0:T(8,128)(2,1)S(1)} %bitcast.17, ...), custom_call_target="tpu_custom_call" | custom-call | flops 1024 | bytes 1024 | tf_op jit(solution)/shard_map/grads/pallas_call | solution.py:249
  55.3 5.7 %collective-permute-done.8 = bf16[208,1792]{1,0:T(8,128)(2,1)} collective-permute-done((bf16[208,1792]{1,0:T(8,128)(2,1)S(1)}, bf16[208,1792]{1,0:T(8,128)(2,1)}, u32[]{:S(2)}, u32[]{:S(2)}) %collective-permute-start.8) | collective-permute-done | bytes 745504 | tf_op jit(solution)/shard_map/ppermute | solution.py:104
  61.0 1.5 collective-permute-done.6
  62.6 2.1 %constant_dynamic-update-slice_fusion.block = bf16[480,1792]{1,0:T(8,128)(2,1)} fusion(bf16[480,1792]{1,0:T(8,128)(2,1)} %constant_dynamic-update-slice_fusion.1, bf16[208,1792]{1,0:T(8,128)(2,1)} %collective-permute-done.8), kind=kLoop, calls=%fused_computation.6 | loop fusion | bytes 1490944 | tf_op jit(solution)/shard_map/concatenate | solution.py:366
  64.6 1.5 broadcast_select_fusion.rest_0_.both
  66.1 2.3 %collective-permute-start.9 = (bf16[272,1792]{1,0:T(8,128)(2,1)S(1)}, bf16[272,1792]{1,0:T(8,128)(2,1)S(1)}, u32[]{:S(2)}, u32[]{:S(2)}) collective-permute-start(bf16[272,1792]{1,0:T(8,128)(2,1)S(1)} %broadcast_select_fusion.rest_0_.both), channel_id=1, source_target_pairs={{8,12},{10,14},{4,0},{6,2},{9,13},{11,15},{5,1},{7,3},{24,28},{26,... | collective-permute-start | bytes 2924552 | tf_op jit(solution)/shard_map/ppermute | solution.py:104
  68.4 1.7 pick.7
  70.5 1.6 collective-permute-start.12
  72.1 2.5 %collective-permute-start.16 = (bf16[208,1792]{1,0:T(8,128)(2,1)S(1)}, bf16[208,1792]{1,0:T(8,128)(2,1)S(1)}, u32[]{:S(2)}, u32[]{:S(2)}) collective-permute-start(bf16[208,1792]{1,0:T(8,128)(2,1)S(1)} %get-tuple-element.57.rest_0_), channel_id=1, source_target_pairs={{0,2},{2,0},{4,6},{6,4},{8,10},{10,8},{1,3},{3,1},{5,7},{7,5},{9,1... | collective-permute-start | bytes 2236424 | tf_op jit(solution)/shard_map/ppermute | solution.py:104
  74.7 1.3 constant_dynamic-update-slice_fusion.3
  76.5 2.0 %copy-done.5 = bf16[2,1792,512]{2,1,0:T(8,128)(2,1)S(1)} copy-done((bf16[2,1792,512]{2,1,0:T(8,128)(2,1)S(1)}, bf16[2,1792,512]{2,1,0:T(8,128)(2,1)}, u32[]{:S(2)}) %copy-start.5) | copy-done | bytes 3670040
  78.6 2.3 %back.5 = (f32[128,1792]{1,0:T(8,128)S(1)}, bf16[96,1792]{1,0:T(8,128)(2,1)S(1)}) custom-call(s32[1]{0:T(128)} %bitcast.3.side, bf16[224,1024]{1,0:T(8,128)(2,1)S(1)} %grads.5.own, bf16[224,1024]{1,0:T(8,128)(2,1)S(1)} %collective-permute-done.10.other, bf16[3584,512]{1,0:T(8,128)(2,1)S(1)} %bitcast.7, bf16[3584,512]{1,0:T(8,128)(2,1)S(1)} %bitcast.18, ...), custom_call_target="tpu_custom_call" | custom-call | flops 1024 | bytes 1024 | tf_op jit(solution)/shard_map/back/pallas_call | solution.py:302
  80.9 4.4 %grads.6.own = bf16[224,1024]{1,0:T(8,128)(2,1)S(1)} custom-call(s32[1]{0:T(128)} %bitcast.3.side, s32[1]{0:T(128)} %bitcast.me, bf16[480,1792]{1,0:T(8,128)(2,1)} %constant_dynamic-update-slice_fusion.block, bf16[480,1792]{1,0:T(8,128)(2,1)S(1)} %collective-permute-done.11.block_far, bf16[3584,512]{1,0:T(8,128)(2,1)S(1)} %bitcast.8, ...), custom_call_target="tpu_custom_call" | custom-call | flops 1024 | bytes 1024 | tf_op jit(solution)/shard_map/grads/pallas_call | solution.py:249
  85.3 4.8 %collective-permute-done.12 = bf16[208,1792]{1,0:T(8,128)(2,1)S(1)} collective-permute-done((bf16[208,1792]{1,0:T(8,128)(2,1)S(1)}, bf16[208,1792]{1,0:T(8,128)(2,1)S(1)}, u32[]{:S(2)}, u32[]{:S(2)}) %collective-permute-start.12) | collective-permute-done | bytes 745504 | tf_op jit(solution)/shard_map/ppermute | solution.py:104
  90.8 14.6 %collective-permute-done.16 = bf16[208,1792]{1,0:T(8,128)(2,1)S(1)} collective-permute-done((bf16[208,1792]{1,0:T(8,128)(2,1)S(1)}, bf16[208,1792]{1,0:T(8,128)(2,1)S(1)}, u32[]{:S(2)}, u32[]{:S(2)}) %collective-permute-start.16) | collective-permute-done | bytes 745504 | tf_op jit(solution)/shard_map/ppermute | solution.py:104
  106.9 2.9 %collective-permute-done.14.other = bf16[224,1024]{1,0:T(8,128)(2,1)S(1)} collective-permute-done((bf16[224,1024]{1,0:T(8,128)(2,1)S(1)}, bf16[224,1024]{1,0:T(8,128)(2,1)S(1)}, u32[]{:S(2)}, u32[]{:S(2)}) %collective-permute-start.14) | collective-permute-done | bytes 458784 | tf_op jit(solution)/shard_map/ppermute | solution.py:108
  109.7 2.3 %back.6 = (f32[128,1792]{1,0:T(8,128)S(1)}, bf16[96,1792]{1,0:T(8,128)(2,1)S(1)}) custom-call(s32[1]{0:T(128)} %bitcast.3.side, bf16[224,1024]{1,0:T(8,128)(2,1)S(1)} %grads.6.own, bf16[224,1024]{1,0:T(8,128)(2,1)S(1)} %collective-permute-done.14.other, bf16[3584,512]{1,0:T(8,128)(2,1)S(1)} %bitcast.9, bf16[3584,512]{1,0:T(8,128)(2,1)S(1)} %bitcast.20, ...), custom_call_target="tpu_custom_call" | custom-call | flops 1024 | bytes 1024 | tf_op jit(solution)/shard_map/back/pallas_call | solution.py:302
  112.1 3.4 %collective-permute-start.15 = (bf16[96,1792]{1,0:T(8,128)(2,1)S(1)}, bf16[96,1792]{1,0:T(8,128)(2,1)S(1)}, u32[]{:S(2)}, u32[]{:S(2)}) collective-permute-start(bf16[96,1792]{1,0:T(8,128)(2,1)S(1)} %get-tuple-element.68), channel_id=1, source_target_pairs={{4,6},{6,4},{8,10},{10,8},{12,14},{14,12},{5,7},{7,5},{9,11},{11,9... | collective-permute-start | bytes 1032200 | tf_op jit(solution)/shard_map/ppermute | solution.py:104
  115.6 2.9 %grads.7.rest_0_.own = bf16[224,1024]{1,0:T(8,128)(2,1)S(1)} custom-call(s32[1]{0:T(128)} %bitcast.3.side, s32[1]{0:T(128)} %bitcast.me, bf16[480,1792]{1,0:T(8,128)(2,1)S(1)} %pad_maximum_fusion.1.block, bf16[480,1792]{1,0:T(8,128)(2,1)S(1)} %collective-permute-done.18.block_far, bf16[3584,512]{1,0:T(8,128)(2,1)S(1)} %bitcast.10, ...), custom_call_target="tpu_custom_call" | custom-call | flops 1024 | bytes 1024 | tf_op jit(solution)/shard_map/grads/pallas_call | solution.py:249
  118.5 2.9 %grads.8.rest_0_.own = bf16[224,1024]{1,0:T(8,128)(2,1)S(1)} custom-call(s32[1]{0:T(128)} %bitcast.3.side, s32[1]{0:T(128)} %bitcast.me, bf16[480,1792]{1,0:T(8,128)(2,1)S(1)} %constant_dynamic-update-slice_fusion.2.block, bf16[480,1792]{1,0:T(8,128)(2,1)S(1)} %collective-permute-done.17.block_far, bf16[3584,512]{1,0:T(8,128)(2,1)S(1)} %bitcast.11, ...), custom_call_target="tpu_custom_call" | custom-call | flops 1024 | bytes 1024 | tf_op jit(solution)/shard_map/grads/pallas_call | solution.py:249
  121.3 2.7 %collective-permute-done.15.came = bf16[96,1792]{1,0:T(8,128)(2,1)S(1)} collective-permute-done((bf16[96,1792]{1,0:T(8,128)(2,1)S(1)}, bf16[96,1792]{1,0:T(8,128)(2,1)S(1)}, u32[]{:S(2)}, u32[]{:S(2)}) %collective-permute-start.15) | collective-permute-done | bytes 344096 | tf_op jit(solution)/shard_map/ppermute | solution.py:104
  125.1 3.8 %collective-permute-start.23 = (bf16[128,1792]{1,0:T(8,128)(2,1)S(1)}, bf16[128,1792]{1,0:T(8,128)(2,1)S(1)}, u32[]{:S(2)}, u32[]{:S(2)}) collective-permute-start(bf16[128,1792]{1,0:T(8,128)(2,1)S(1)} %join.5), channel_id=1, source_target_pairs={{4,0},{6,2},{8,4},{10,6},{12,8},{14,10},{5,1},{7,3},{9,5},{11,7},{... | collective-permute-start | bytes 1376264 | tf_op jit(solution)/shard_map/ppermute | solution.py:104
  129.0 2.3 %back.7 = (f32[128,1792]{1,0:T(8,128)S(1)}, bf16[96,1792]{1,0:T(8,128)(2,1)S(1)}) custom-call(s32[1]{0:T(128)} %bitcast.3.side, bf16[224,1024]{1,0:T(8,128)(2,1)S(1)} %grads.7.rest_0_.own, bf16[224,1024]{1,0:T(8,128)(2,1)S(1)} %collective-permute-done.20.other, bf16[3584,512]{1,0:T(8,128)(2,1)S(1)} %bitcast.12, bf16[3584,512]{1,0:T(8,128)(2,1)S(1)} %bitcast.23, ...), custom_call_target="tpu_custom_call" | custom-call | flops 1024 | bytes 1024 | tf_op jit(solution)/shard_map/back/pallas_call | solution.py:302
  131.3 2.9 %grads.9.rest_0_.own = bf16[224,1024]{1,0:T(8,128)(2,1)S(1)} custom-call(s32[1]{0:T(128)} %bitcast.3.side, s32[1]{0:T(128)} %bitcast.me, bf16[480,1792]{1,0:T(8,128)(2,1)S(1)} %constant_dynamic-update-slice_fusion.4.block, bf16[480,1792]{1,0:T(8,128)(2,1)S(1)} %collective-permute-done.19.block_far, bf16[3584,512]{1,0:T(8,128)(2,1)S(1)} %bitcast.13, ...), custom_call_target="tpu_custom_call" | custom-call | flops 1024 | bytes 1024 | tf_op jit(solution)/shard_map/grads/pallas_call | solution.py:249
  134.4 1.5 collective-permute-start.26
  135.9 2.3 %back.8 = (f32[128,1792]{1,0:T(8,128)S(1)}, bf16[96,1792]{1,0:T(8,128)(2,1)S(1)}) custom-call(s32[1]{0:T(128)} %bitcast.3.side, bf16[224,1024]{1,0:T(8,128)(2,1)S(1)} %grads.8.rest_0_.own, bf16[224,1024]{1,0:T(8,128)(2,1)S(1)} %collective-permute-done.22.other, bf16[3584,512]{1,0:T(8,128)(2,1)S(1)} %bitcast.14, bf16[3584,512]{1,0:T(8,128)(2,1)S(1)} %bitcast.25, ...), custom_call_target="tpu_custom_call" | custom-call | flops 1024 | bytes 1024 | tf_op jit(solution)/shard_map/back/pallas_call | solution.py:302
  138.3 2.4 %collective-permute-start.25 = (bf16[96,1792]{1,0:T(8,128)(2,1)S(1)}, bf16[96,1792]{1,0:T(8,128)(2,1)S(1)}, u32[]{:S(2)}, u32[]{:S(2)}) collective-permute-start(bf16[96,1792]{1,0:T(8,128)(2,1)S(1)} %get-tuple-element.82), channel_id=1, source_target_pairs={{0,2},{2,0},{4,6},{6,4},{8,10},{10,8},{1,3},{3,1},{5,7},{7,5},{9,1... | collective-permute-start | bytes 1032200 | tf_op jit(solution)/shard_map/ppermute | solution.py:104
  140.7 2.3 %back.9 = (f32[128,1792]{1,0:T(8,128)S(1)}, bf16[96,1792]{1,0:T(8,128)(2,1)S(1)}) custom-call(s32[1]{0:T(128)} %bitcast.3.side, bf16[224,1024]{1,0:T(8,128)(2,1)S(1)} %grads.9.rest_0_.own, bf16[224,1024]{1,0:T(8,128)(2,1)S(1)} %collective-permute-done.21.other, bf16[3584,512]{1,0:T(8,128)(2,1)S(1)} %bitcast.15, bf16[3584,512]{1,0:T(8,128)(2,1)S(1)} %bitcast.26, ...), custom_call_target="tpu_custom_call" | custom-call | flops 1024 | bytes 1024 | tf_op jit(solution)/shard_map/back/pallas_call | solution.py:302
  143.8 1.5 collective-permute-done.26.came
  145.7 6.4 %collective-permute-done.25.came = bf16[96,1792]{1,0:T(8,128)(2,1)S(1)} collective-permute-done((bf16[96,1792]{1,0:T(8,128)(2,1)S(1)}, bf16[96,1792]{1,0:T(8,128)(2,1)S(1)}, u32[]{:S(2)}, u32[]{:S(2)}) %collective-permute-start.25) | collective-permute-done | bytes 344096 | tf_op jit(solution)/shard_map/ppermute | solution.py:104
  152.4 2.3 %collective-permute-start.27 = (bf16[128,1792]{1,0:T(8,128)(2,1)S(1)}, bf16[128,1792]{1,0:T(8,128)(2,1)S(1)}, u32[]{:S(2)}, u32[]{:S(2)}) collective-permute-start(bf16[128,1792]{1,0:T(8,128)(2,1)S(1)} %join.7.rest_2_.rest_0_), channel_id=1, source_target_pairs={{0,4},{2,6},{4,8},{6,10},{8,12},{10,14},{1,5},{3,7},{5,9},{7,11},{... | collective-permute-start | bytes 1376264 | tf_op jit(solution)/shard_map/ppermute | solution.py:104
  155.8 1.6 collective-permute-start.24
  157.3 7.8 %collective-permute-done.24.came = bf16[96,1792]{1,0:T(8,128)(2,1)S(1)} collective-permute-done((bf16[96,1792]{1,0:T(8,128)(2,1)S(1)}, bf16[96,1792]{1,0:T(8,128)(2,1)S(1)}, u32[]{:S(2)}, u32[]{:S(2)}) %collective-permute-start.24) | collective-permute-done | bytes 344096 | tf_op jit(solution)/shard_map/ppermute | solution.py:104
  165.5 19.0 %collective-permute-done.27 = bf16[128,1792]{1,0:T(8,128)(2,1)S(1)} collective-permute-done((bf16[128,1792]{1,0:T(8,128)(2,1)S(1)}, bf16[128,1792]{1,0:T(8,128)(2,1)S(1)}, u32[]{:S(2)}, u32[]{:S(2)}) %collective-permute-start.27) | collective-permute-done | bytes 458784 | tf_op jit(solution)/shard_map/ppermute | solution.py:104
  184.5 1.0 add_convert_fusion
  (71 shorter events, 10.1 us)
Async XLA Ops:
  0.0 32.0 %collective-permute-start.3 = (bf16[3584,512]{1,0:T(8,128)(2,1)}, bf16[3584,512]{1,0:T(8,128)(2,1)}, u32[]{:S(2)}, u32[]{:S(2)}) collective-permute-start(bf16[3584,512]{1,0:T(8,128)(2,1)} %bitcast.5), channel_id=1, source_target_pairs={{0,1},{1,0},{2,3},{3,2},{4,5},{5,4},{6,7},{7,6},{8,9},{9,8},{10,11... | collective-permute-start | bytes 11010056 | tf_op jit(solution)/shard_map/ppermute | solution.py:108
  0.0 32.0 %collective-permute-start.4 = (bf16[3584,512]{1,0:T(8,128)(2,1)}, bf16[3584,512]{1,0:T(8,128)(2,1)}, u32[]{:S(2)}, u32[]{:S(2)}) collective-permute-start(bf16[3584,512]{1,0:T(8,128)(2,1)} %bitcast.16), channel_id=1, source_target_pairs={{0,1},{1,0},{2,3},{3,2},{4,5},{5,4},{6,7},{7,6},{8,9},{9,8},{10,11... | collective-permute-start | bytes 11010056 | tf_op jit(solution)/shard_map/ppermute | solution.py:108
  1.2 1.0 copy-start.9
  2.2 1.0 copy-start.11
  3.3 25.5 %collective-permute-start = (bf16[272,1792]{1,0:T(8,128)(2,1)S(1)}, bf16[272,1792]{1,0:T(8,128)(2,1)}, u32[]{:S(2)}, u32[]{:S(2)}) collective-permute-start(bf16[272,1792]{1,0:T(8,128)(2,1)S(1)} %stack.1.both), channel_id=1, source_target_pairs={{0,4},{2,6},{4,8},{6,10},{8,12},{10,14},{1,5},{3,7},{5,9},{7,11},{... | collective-permute-start | bytes 2924552 | tf_op jit(solution)/shard_map/ppermute | solution.py:104
  6.8 25.2 %collective-permute-start.1 = (bf16[272,1792]{1,0:T(8,128)(2,1)S(1)}, bf16[272,1792]{1,0:T(8,128)(2,1)}, u32[]{:S(2)}, u32[]{:S(2)}) collective-permute-start(bf16[272,1792]{1,0:T(8,128)(2,1)S(1)} %stack.1.both), channel_id=1, source_target_pairs={{4,0},{6,2},{8,4},{10,6},{12,8},{14,10},{5,1},{7,3},{9,5},{11,7},{... | collective-permute-start | bytes 2924552 | tf_op jit(solution)/shard_map/ppermute | solution.py:104
  10.7 18.1 %collective-permute-start.2 = (bf16[208,1792]{1,0:T(8,128)(2,1)S(1)}, bf16[208,1792]{1,0:T(8,128)(2,1)S(1)}, u32[]{:S(2)}, u32[]{:S(2)}) collective-permute-start(bf16[208,1792]{1,0:T(8,128)(2,1)S(1)} %get-tuple-element.47), channel_id=1, source_target_pairs={{0,2},{2,0},{4,6},{6,4},{8,10},{10,8},{12,14},{14,12},{1,3},{3,1},... | collective-permute-start | bytes 2236424 | tf_op jit(solution)/shard_map/ppermute | solution.py:104
  32.2 18.1 %collective-permute-start.7 = (bf16[480,1792]{1,0:T(8,128)(2,1)S(1)}, bf16[480,1792]{1,0:T(8,128)(2,1)}, u32[]{:S(2)}, u32[]{:S(2)}) collective-permute-start(bf16[480,1792]{1,0:T(8,128)(2,1)S(1)} %pad_maximum_fusion.block), channel_id=1, source_target_pairs={{0,1},{1,0},{2,3},{3,2},{4,5},{5,4},{6,7},{7,6},{8,9},{9,8},{10,11... | collective-permute-start | bytes 5160968 | tf_op jit(solution)/shard_map/ppermute | solution.py:108
  32.2 28.8 %collective-permute-start.5 = (bf16[272,1792]{1,0:T(8,128)(2,1)}, bf16[272,1792]{1,0:T(8,128)(2,1)}, u32[]{:S(2)}, u32[]{:S(2)}) collective-permute-start(bf16[272,1792]{1,0:T(8,128)(2,1)} %collective-permute-done.both), channel_id=1, source_target_pairs={{4,8},{6,10},{8,12},{10,14},{5,9},{7,11},{9,13},{11,15},{20,24},{2... | collective-permute-start | bytes 2924552 | tf_op jit(solution)/shard_map/ppermute | solution.py:104
  36.7 25.9 %collective-permute-start.6 = (bf16[272,1792]{1,0:T(8,128)(2,1)}, bf16[272,1792]{1,0:T(8,128)(2,1)}, u32[]{:S(2)}, u32[]{:S(2)}) collective-permute-start(bf16[272,1792]{1,0:T(8,128)(2,1)} %collective-permute-done.1.both), channel_id=1, source_target_pairs={{8,4},{10,6},{4,0},{6,2},{9,5},{11,7},{5,1},{7,3},{24,20},{26,22},... | collective-permute-start | bytes 2924552 | tf_op jit(solution)/shard_map/ppermute | solution.py:104
  40.3 20.8 %collective-permute-start.8 = (bf16[208,1792]{1,0:T(8,128)(2,1)S(1)}, bf16[208,1792]{1,0:T(8,128)(2,1)}, u32[]{:S(2)}, u32[]{:S(2)}) collective-permute-start(bf16[208,1792]{1,0:T(8,128)(2,1)S(1)} %get-tuple-element.51.rest_0_), channel_id=1, source_target_pairs={{4,6},{6,4},{8,10},{10,8},{12,14},{14,12},{5,7},{7,5},{9,11},{11,9... | collective-permute-start | bytes 2236424 | tf_op jit(solution)/shard_map/ppermute | solution.py:104
  43.7 6.6 %copy-start = (bf16[1,3584,512]{2,1,0:T(8,128)(2,1)S(1)}, bf16[1,3584,512]{2,1,0:T(8,128)(2,1)}, u32[]{:S(2)}) copy-start(bf16[1,3584,512]{2,1,0:T(8,128)(2,1)} %param.11) | copy-start | bytes 11010052
  43.7 6.6 %copy-start.2 = (bf16[1,3584,512]{2,1,0:T(8,128)(2,1)S(1)}, bf16[1,3584,512]{2,1,0:T(8,128)(2,1)}, u32[]{:S(2)}) copy-start(bf16[1,3584,512]{2,1,0:T(8,128)(2,1)} %param.12) | copy-start | bytes 11010052
  43.7 7.3 %copy-start.7 = (bf16[1,512,3584]{2,1,0:T(8,128)(2,1)S(1)}, bf16[1,512,3584]{2,1,0:T(8,128)(2,1)}, u32[]{:S(2)}) copy-start(bf16[1,512,3584]{2,1,0:T(8,128)(2,1)} %param.13) | copy-start | bytes 11010052
  46.0 9.3 %copy-start.4 = (bf16[2,1792,512]{2,1,0:T(8,128)(2,1)}, bf16[2,1792,512]{2,1,0:T(8,128)(2,1)S(1)}, u32[]{:S(2)}) copy-start(bf16[2,1792,512]{2,1,0:T(8,128)(2,1)S(1)} %keep.1.rest_1_.far) | copy-start | bytes 11010052
  64.6 16.3 %collective-permute-start.11 = (bf16[480,1792]{1,0:T(8,128)(2,1)}, bf16[480,1792]{1,0:T(8,128)(2,1)S(1)}, u32[]{:S(2)}, u32[]{:S(2)}) collective-permute-start(bf16[480,1792]{1,0:T(8,128)(2,1)} %constant_dynamic-update-slice_fusion.block), channel_id=1, source_target_pairs={{0,1},{1,0},{2,3},{3,2},{4,5},{5,4},{6,7},{7,6},{8,9},{9,8},{10,11... | collective-permute-start | bytes 5160968 | tf_op jit(solution)/shard_map/ppermute | solution.py:108
  64.6 11.9 %copy-start.3 = (bf16[1,3584,512]{2,1,0:T(8,128)(2,1)S(1)}, bf16[1,3584,512]{2,1,0:T(8,128)(2,1)}, u32[]{:S(2)}) copy-start(bf16[1,3584,512]{2,1,0:T(8,128)(2,1)} %param.12) | copy-start | bytes 11010052
  66.1 24.0 %collective-permute-start.9 = (bf16[272,1792]{1,0:T(8,128)(2,1)S(1)}, bf16[272,1792]{1,0:T(8,128)(2,1)S(1)}, u32[]{:S(2)}, u32[]{:S(2)}) collective-permute-start(bf16[272,1792]{1,0:T(8,128)(2,1)S(1)} %broadcast_select_fusion.rest_0_.both), channel_id=1, source_target_pairs={{8,12},{10,14},{4,0},{6,2},{9,13},{11,15},{5,1},{7,3},{24,28},{26,... | collective-permute-start | bytes 2924552 | tf_op jit(solution)/shard_map/ppermute | solution.py:104
  70.0 6.5 %copy-start.1 = (bf16[1,3584,512]{2,1,0:T(8,128)(2,1)S(1)}, bf16[1,3584,512]{2,1,0:T(8,128)(2,1)}, u32[]{:S(2)}) copy-start(bf16[1,3584,512]{2,1,0:T(8,128)(2,1)} %param.11) | copy-start | bytes 11010052
  70.5 19.6 %collective-permute-start.12 = (bf16[208,1792]{1,0:T(8,128)(2,1)S(1)}, bf16[208,1792]{1,0:T(8,128)(2,1)S(1)}, u32[]{:S(2)}, u32[]{:S(2)}) collective-permute-start(bf16[208,1792]{1,0:T(8,128)(2,1)S(1)} %get-tuple-element.58.rest_0_), channel_id=1, source_target_pairs={{0,2},{2,0},{4,6},{6,4},{8,10},{10,8},{12,14},{14,12},{1,3},{3,1},... | collective-permute-start | bytes 2236424 | tf_op jit(solution)/shard_map/ppermute | solution.py:104
  72.1 33.2 %collective-permute-start.16 = (bf16[208,1792]{1,0:T(8,128)(2,1)S(1)}, bf16[208,1792]{1,0:T(8,128)(2,1)S(1)}, u32[]{:S(2)}, u32[]{:S(2)}) collective-permute-start(bf16[208,1792]{1,0:T(8,128)(2,1)S(1)} %get-tuple-element.57.rest_0_), channel_id=1, source_target_pairs={{0,2},{2,0},{4,6},{6,4},{8,10},{10,8},{1,3},{3,1},{5,7},{7,5},{9,1... | collective-permute-start | bytes 2236424 | tf_op jit(solution)/shard_map/ppermute | solution.py:104
  74.6 1.9 %collective-permute-start.10 = (bf16[224,1024]{1,0:T(8,128)(2,1)S(1)}, bf16[224,1024]{1,0:T(8,128)(2,1)S(1)}, u32[]{:S(2)}, u32[]{:S(2)}) collective-permute-start(bf16[224,1024]{1,0:T(8,128)(2,1)S(1)} %grads.5.own), channel_id=1, source_target_pairs={{0,1},{1,0},{2,3},{3,2},{4,5},{5,4},{6,7},{7,6},{8,9},{9,8},{10,11... | collective-permute-start | bytes 1376264 | tf_op jit(solution)/shard_map/ppermute | solution.py:108
  76.5 2.0 %copy-start.5 = (bf16[2,1792,512]{2,1,0:T(8,128)(2,1)S(1)}, bf16[2,1792,512]{2,1,0:T(8,128)(2,1)}, u32[]{:S(2)}) copy-start(bf16[2,1792,512]{2,1,0:T(8,128)(2,1)} %copy-done.4) | copy-start | bytes 11010052
  78.6 2.3 %copy-start.8 = (bf16[1,512,3584]{2,1,0:T(8,128)(2,1)S(1)}, bf16[1,512,3584]{2,1,0:T(8,128)(2,1)}, u32[]{:S(2)}) copy-start(bf16[1,512,3584]{2,1,0:T(8,128)(2,1)} %param.13) | copy-start | bytes 11010052
  90.5 19.2 %copy-start.6 = (bf16[2,1792,512]{2,1,0:T(8,128)(2,1)S(1)}, bf16[2,1792,512]{2,1,0:T(8,128)(2,1)}, u32[]{:S(2)}) copy-start(bf16[2,1792,512]{2,1,0:T(8,128)(2,1)} %copy-done.4) | copy-start | bytes 11010052
  90.7 24.9 %collective-permute-start.18 = (bf16[480,1792]{1,0:T(8,128)(2,1)S(1)}, bf16[480,1792]{1,0:T(8,128)(2,1)S(1)}, u32[]{:S(2)}, u32[]{:S(2)}) collective-permute-start(bf16[480,1792]{1,0:T(8,128)(2,1)S(1)} %pad_maximum_fusion.1.block), channel_id=1, source_target_pairs={{0,1},{1,0},{2,3},{3,2},{4,5},{5,4},{6,7},{7,6},{8,9},{9,8},{10,11... | collective-permute-start | bytes 5160968 | tf_op jit(solution)/shard_map/ppermute | solution.py:108
  105.4 13.1 %collective-permute-start.17 = (bf16[480,1792]{1,0:T(8,128)(2,1)S(1)}, bf16[480,1792]{1,0:T(8,128)(2,1)S(1)}, u32[]{:S(2)}, u32[]{:S(2)}) collective-permute-start(bf16[480,1792]{1,0:T(8,128)(2,1)S(1)} %constant_dynamic-update-slice_fusion.2.block), channel_id=1, source_target_pairs={{0,1},{1,0},{2,3},{3,2},{4,5},{5,4},{6,7},{7,6},{8,9},{9,8},{10,11... | collective-permute-start | bytes 5160968 | tf_op jit(solution)/shard_map/ppermute | solution.py:108
  105.5 4.3 %collective-permute-start.14 = (bf16[224,1024]{1,0:T(8,128)(2,1)S(1)}, bf16[224,1024]{1,0:T(8,128)(2,1)S(1)}, u32[]{:S(2)}, u32[]{:S(2)}) collective-permute-start(bf16[224,1024]{1,0:T(8,128)(2,1)S(1)} %grads.6.own), channel_id=1, source_target_pairs={{0,1},{1,0},{2,3},{3,2},{4,5},{5,4},{6,7},{7,6},{8,9},{9,8},{10,11... | collective-permute-start | bytes 1376264 | tf_op jit(solution)/shard_map/ppermute | solution.py:108
  106.0 18.4 %collective-permute-start.13 = (bf16[208,1792]{1,0:T(8,128)(2,1)S(1)}, bf16[208,1792]{1,0:T(8,128)(2,1)S(1)}, u32[]{:S(2)}, u32[]{:S(2)}) collective-permute-start(bf16[208,1792]{1,0:T(8,128)(2,1)S(1)} %get-tuple-element.64), channel_id=1, source_target_pairs={{0,2},{2,0},{12,14},{14,12},{1,3},{3,1},{13,15},{15,13},{16,18},{1... | collective-permute-start | bytes 2236424 | tf_op jit(solution)/shard_map/ppermute | solution.py:104
  112.1 12.0 %collective-permute-start.15 = (bf16[96,1792]{1,0:T(8,128)(2,1)S(1)}, bf16[96,1792]{1,0:T(8,128)(2,1)S(1)}, u32[]{:S(2)}, u32[]{:S(2)}) collective-permute-start(bf16[96,1792]{1,0:T(8,128)(2,1)S(1)} %get-tuple-element.68), channel_id=1, source_target_pairs={{4,6},{6,4},{8,10},{10,8},{12,14},{14,12},{5,7},{7,5},{9,11},{11,9... | collective-permute-start | bytes 1032200 | tf_op jit(solution)/shard_map/ppermute | solution.py:104
  124.5 6.8 %collective-permute-start.19 = (bf16[480,1792]{1,0:T(8,128)(2,1)S(1)}, bf16[480,1792]{1,0:T(8,128)(2,1)S(1)}, u32[]{:S(2)}, u32[]{:S(2)}) collective-permute-start(bf16[480,1792]{1,0:T(8,128)(2,1)S(1)} %constant_dynamic-update-slice_fusion.4.block), channel_id=1, source_target_pairs={{0,1},{1,0},{2,3},{3,2},{4,5},{5,4},{6,7},{7,6},{8,9},{9,8},{10,11... | collective-permute-start | bytes 5160968 | tf_op jit(solution)/shard_map/ppermute | solution.py:108
  124.5 4.4 %collective-permute-start.20 = (bf16[224,1024]{1,0:T(8,128)(2,1)S(1)}, bf16[224,1024]{1,0:T(8,128)(2,1)S(1)}, u32[]{:S(2)}, u32[]{:S(2)}) collective-permute-start(bf16[224,1024]{1,0:T(8,128)(2,1)S(1)} %grads.7.rest_0_.own), channel_id=1, source_target_pairs={{0,1},{1,0},{2,3},{3,2},{4,5},{5,4},{6,7},{7,6},{8,9},{9,8},{10,11... | collective-permute-start | bytes 1376264 | tf_op jit(solution)/shard_map/ppermute | solution.py:108
  125.0 10.9 %collective-permute-start.22 = (bf16[224,1024]{1,0:T(8,128)(2,1)S(1)}, bf16[224,1024]{1,0:T(8,128)(2,1)S(1)}, u32[]{:S(2)}, u32[]{:S(2)}) collective-permute-start(bf16[224,1024]{1,0:T(8,128)(2,1)S(1)} %grads.8.rest_0_.own), channel_id=1, source_target_pairs={{0,1},{1,0},{2,3},{3,2},{4,5},{5,4},{6,7},{7,6},{8,9},{9,8},{10,11... | collective-permute-start | bytes 1376264 | tf_op jit(solution)/shard_map/ppermute | solution.py:108
  125.1 15.6 %collective-permute-start.23 = (bf16[128,1792]{1,0:T(8,128)(2,1)S(1)}, bf16[128,1792]{1,0:T(8,128)(2,1)S(1)}, u32[]{:S(2)}, u32[]{:S(2)}) collective-permute-start(bf16[128,1792]{1,0:T(8,128)(2,1)S(1)} %join.5), channel_id=1, source_target_pairs={{4,0},{6,2},{8,4},{10,6},{12,8},{14,10},{5,1},{7,3},{9,5},{11,7},{... | collective-permute-start | bytes 1376264 | tf_op jit(solution)/shard_map/ppermute | solution.py:104
  134.2 6.6 %collective-permute-start.21 = (bf16[224,1024]{1,0:T(8,128)(2,1)S(1)}, bf16[224,1024]{1,0:T(8,128)(2,1)S(1)}, u32[]{:S(2)}, u32[]{:S(2)}) collective-permute-start(bf16[224,1024]{1,0:T(8,128)(2,1)S(1)} %grads.9.rest_0_.own), channel_id=1, source_target_pairs={{0,1},{1,0},{2,3},{3,2},{4,5},{5,4},{6,7},{7,6},{8,9},{9,8},{10,11... | collective-permute-start | bytes 1376264 | tf_op jit(solution)/shard_map/ppermute | solution.py:108
  134.4 10.9 %collective-permute-start.26 = (bf16[96,1792]{1,0:T(8,128)(2,1)S(1)}, bf16[96,1792]{1,0:T(8,128)(2,1)S(1)}, u32[]{:S(2)}, u32[]{:S(2)}) collective-permute-start(bf16[96,1792]{1,0:T(8,128)(2,1)S(1)} %get-tuple-element.84), channel_id=1, source_target_pairs={{0,2},{2,0},{4,6},{6,4},{8,10},{10,8},{12,14},{14,12},{1,3},{3,1},... | collective-permute-start | bytes 1032200 | tf_op jit(solution)/shard_map/ppermute | solution.py:104
  138.3 13.8 %collective-permute-start.25 = (bf16[96,1792]{1,0:T(8,128)(2,1)S(1)}, bf16[96,1792]{1,0:T(8,128)(2,1)S(1)}, u32[]{:S(2)}, u32[]{:S(2)}) collective-permute-start(bf16[96,1792]{1,0:T(8,128)(2,1)S(1)} %get-tuple-element.82), channel_id=1, source_target_pairs={{0,2},{2,0},{4,6},{6,4},{8,10},{10,8},{1,3},{3,1},{5,7},{7,5},{9,1... | collective-permute-start | bytes 1032200 | tf_op jit(solution)/shard_map/ppermute | solution.py:104
  143.1 11.7 %collective-permute-start.29 = (bf16[96,1792]{1,0:T(8,128)(2,1)S(1)}, bf16[96,1792]{1,0:T(8,128)(2,1)S(1)}, u32[]{:S(2)}, u32[]{:S(2)}) collective-permute-start(bf16[96,1792]{1,0:T(8,128)(2,1)S(1)} %get-tuple-element.86), channel_id=1, source_target_pairs={{0,2},{2,0},{12,14},{14,12},{1,3},{3,1},{13,15},{15,13},{16,18},{1... | collective-permute-start | bytes 1032200 | tf_op jit(solution)/shard_map/ppermute | solution.py:104
  145.6 38.8 %collective-permute-start.28 = (bf16[128,1792]{1,0:T(8,128)(2,1)S(1)}, bf16[128,1792]{1,0:T(8,128)(2,1)S(1)}, u32[]{:S(2)}, u32[]{:S(2)}) collective-permute-start(bf16[128,1792]{1,0:T(8,128)(2,1)S(1)} %join.6.rest_0_), channel_id=1, source_target_pairs={{0,8},{2,10},{4,12},{6,14},{8,0},{10,2},{12,4},{14,6},{1,9},{3,11}... | collective-permute-start | bytes 1376264 | tf_op jit(solution)/shard_map/ppermute | solution.py:104
  152.1 13.0 %copy-start.10 = (bf16[128,1792]{1,0:T(8,128)(2,1)S(1)}, bf16[128,1792]{1,0:T(8,128)(2,1)}, u32[]{:S(2)}) copy-start(bf16[128,1792]{1,0:T(8,128)(2,1)} %rest_0_.1) | copy-start | bytes 1376260
  152.4 32.0 %collective-permute-start.27 = (bf16[128,1792]{1,0:T(8,128)(2,1)S(1)}, bf16[128,1792]{1,0:T(8,128)(2,1)S(1)}, u32[]{:S(2)}, u32[]{:S(2)}) collective-permute-start(bf16[128,1792]{1,0:T(8,128)(2,1)S(1)} %join.7.rest_2_.rest_0_), channel_id=1, source_target_pairs={{0,4},{2,6},{4,8},{6,10},{8,12},{10,14},{1,5},{3,7},{5,9},{7,11},{... | collective-permute-start | bytes 1376264 | tf_op jit(solution)/shard_map/ppermute | solution.py:104
  155.1 29.4 %collective-permute-start.30 = (bf16[128,1792]{1,0:T(8,128)(2,1)S(1)}, bf16[128,1792]{1,0:T(8,128)(2,1)S(1)}, u32[]{:S(2)}, u32[]{:S(2)}) collective-permute-start(bf16[128,1792]{1,0:T(8,128)(2,1)S(1)} %join.9), channel_id=1, source_target_pairs={{0,12},{2,14},{12,0},{14,2},{1,13},{3,15},{13,1},{15,3},{16,28},{1... | collective-permute-start | bytes 1376264 | tf_op jit(solution)/shard_map/ppermute | solution.py:104
  155.8 9.3 %collective-permute-start.24 = (bf16[96,1792]{1,0:T(8,128)(2,1)S(1)}, bf16[96,1792]{1,0:T(8,128)(2,1)S(1)}, u32[]{:S(2)}, u32[]{:S(2)}) collective-permute-start(bf16[96,1792]{1,0:T(8,128)(2,1)S(1)} %get-tuple-element.80), channel_id=1, source_target_pairs={{0,2},{2,0},{4,6},{6,4},{8,10},{10,8},{12,14},{14,12},{1,3},{3,1},... | collective-permute-start | bytes 1032200 | tf_op jit(solution)/shard_map/ppermute | solution.py:104

commit v4 on v3

--- a/solution.py
+++ b/solution.py
@@ -420,7 +420,7 @@
     came2 = move(slots2, Y_DOWN)
     dense4, slots4 = back(halves(grads4), (dense2, home1))
     came4 = move(slots4, Y_ENDS)
-    join3 = joined(place3, came3, dense3, after=(dense4,))
+    join3 = joined(place3, came3, dense3, after=(dense2,))
     home3 = move(join3, SKIP)
     join2 = joined(place2, came2, dense2, after=(join3,))
     home2 = move(join2, UP1)

time: 187 us -> 187 us (level)
  transfers between devices with their start and end apart: 31 -> 31, of which waited for: 14 -> 15; matrix products, arithmetic and copies ran while one was open for 4% -> 4% of each run, Pallas kernels for 20% -> 20%
where the time goes in v4:
time: 187 us; the launch traced here: 185 us
  waiting for transfers between devices  87.2 us (47%)
  starting transfers between devices  44.2 us (24%)
  Pallas kernels  37.6 us (20%)
  local copies, waits for them, and re-layouts  12.6 us (7%)
  other arithmetic  3.38 us (2%)
    ppermute x19, waiting for transfers between devices, move(): return lax.ppermute(value, 'node', pairs)  83.8 us
    ppermute x19, starting transfers between devices, move(): return lax.ppermute(value, 'node', pairs)  42 us
    pallas_call x5, Pallas kernels, grads_of(): pl.pallas_call(functools.partial(grads_kernel, capacity, tokens), out_sha...  17.3 us
    pallas_call x5, Pallas kernels, back_of(): pl.pallas_call(back_kernel, out_shape=[jax.ShapeDtypeStruct((tokens, half...  11.7 us
    unnamed x27, local copies, waits for them, and re-layouts  10.4 us
    pallas_call x5, Pallas kernels, picked_rows(): pl.pallas_call(functools.partial(pick_kernel, capacity, tokens), out_shap...  4.69 us
  transfers between devices with their start and end apart: 31, of which 15 were waited for; matrix products, arithmetic and copies ran while one was open for 4% of the time, Pallas kernels for 20%

profile of v4, /device:TPU:8, one launch (start us, length us, event | category | flops | bytes accessed | tf_op | source)
XLA Modules:
  0.0 185.5 jit_solution(12035379837675493877)
XLA Ops:
  1.2 1.0 copy-done.9
  2.2 1.0 copy-done.11
  3.3 3.5 %collective-permute-start = (bf16[272,1792]{1,0:T(8,128)(2,1)S(1)}, bf16[272,1792]{1,0:T(8,128)(2,1)}, u32[]{:S(2)}, u32[]{:S(2)}) collective-permute-start(bf16[272,1792]{1,0:T(8,128)(2,1)S(1)} %stack.1.both), channel_id=1, source_target_pairs={{0,4},{2,6},{4,8},{6,10},{8,12},{10,14},{1,5},{3,7},{5,9},{7,11},{... | collective-permute-start | bytes 2924552 | tf_op jit(solution)/shard_map/ppermute | solution.py:104
  6.8 3.4 %collective-permute-start.1 = (bf16[272,1792]{1,0:T(8,128)(2,1)S(1)}, bf16[272,1792]{1,0:T(8,128)(2,1)}, u32[]{:S(2)}, u32[]{:S(2)}) collective-permute-start(bf16[272,1792]{1,0:T(8,128)(2,1)S(1)} %stack.1.both), channel_id=1, source_target_pairs={{4,0},{6,2},{8,4},{10,6},{12,8},{14,10},{5,1},{7,3},{9,5},{11,7},{... | collective-permute-start | bytes 2924552 | tf_op jit(solution)/shard_map/ppermute | solution.py:104
  10.7 1.6 collective-permute-start.2
  12.3 16.5 %collective-permute-done.2 = bf16[208,1792]{1,0:T(8,128)(2,1)S(1)} collective-permute-done((bf16[208,1792]{1,0:T(8,128)(2,1)S(1)}, bf16[208,1792]{1,0:T(8,128)(2,1)S(1)}, u32[]{:S(2)}, u32[]{:S(2)}) %collective-permute-start.2) | collective-permute-done | bytes 745504 | tf_op jit(solution)/shard_map/ppermute | solution.py:104
  28.8 3.2 %collective-permute-done.1.both = bf16[272,1792]{1,0:T(8,128)(2,1)} collective-permute-done((bf16[272,1792]{1,0:T(8,128)(2,1)S(1)}, bf16[272,1792]{1,0:T(8,128)(2,1)}, u32[]{:S(2)}, u32[]{:S(2)}) %collective-permute-start.1) | collective-permute-done | bytes 974880 | tf_op jit(solution)/shard_map/ppermute | solution.py:104
  32.2 4.4 %collective-permute-start.5 = (bf16[272,1792]{1,0:T(8,128)(2,1)}, bf16[272,1792]{1,0:T(8,128)(2,1)}, u32[]{:S(2)}, u32[]{:S(2)}) collective-permute-start(bf16[272,1792]{1,0:T(8,128)(2,1)} %collective-permute-done.both), channel_id=1, source_target_pairs={{4,8},{6,10},{8,12},{10,14},{5,9},{7,11},{9,13},{11,15},{20,24},{2... | collective-permute-start | bytes 2924552 | tf_op jit(solution)/shard_map/ppermute | solution.py:104
  36.7 1.9 %collective-permute-start.6 = (bf16[272,1792]{1,0:T(8,128)(2,1)}, bf16[272,1792]{1,0:T(8,128)(2,1)}, u32[]{:S(2)}, u32[]{:S(2)}) collective-permute-start(bf16[272,1792]{1,0:T(8,128)(2,1)} %collective-permute-done.1.both), channel_id=1, source_target_pairs={{8,4},{10,6},{4,0},{6,2},{9,5},{11,7},{5,1},{7,3},{24,20},{26,22},... | collective-permute-start | bytes 2924552 | tf_op jit(solution)/shard_map/ppermute | solution.py:104
  38.6 1.7 pick.6
  40.3 3.4 %collective-permute-start.8 = (bf16[208,1792]{1,0:T(8,128)(2,1)S(1)}, bf16[208,1792]{1,0:T(8,128)(2,1)}, u32[]{:S(2)}, u32[]{:S(2)}) collective-permute-start(bf16[208,1792]{1,0:T(8,128)(2,1)S(1)} %get-tuple-element.51.rest_0_), channel_id=1, source_target_pairs={{4,6},{6,4},{8,10},{10,8},{12,14},{14,12},{5,7},{7,5},{9,11},{11,9... | collective-permute-start | bytes 2236424 | tf_op jit(solution)/shard_map/ppermute | solution.py:104
  43.7 2.2 %keep.1.rest_1_.far = bf16[2,1792,512]{2,1,0:T(8,128)(2,1)S(1)} custom-call(s32[1]{0:T(128)} %bitcast.3.side, bf16[3584,512]{1,0:T(8,128)(2,1)} %collective-permute-done.3.gate, bf16[3584,512]{1,0:T(8,128)(2,1)} %collective-permute-done.4.up), custom_call_target="tpu_custom_call" | custom-call | flops 1024 | bytes 1024 | tf_op jit(solution)/shard_map/keep/pallas_call | solution.py:275
  46.0 4.3 %constant_dynamic-update-slice_fusion.1 = bf16[480,1792]{1,0:T(8,128)(2,1)} fusion(bf16[272,1792]{1,0:T(8,128)(2,1)} %collective-permute-done.both), kind=kLoop, calls=%fused_computation.7 | loop fusion | bytes 1949696
  51.0 4.3 %grads.5.own = bf16[224,1024]{1,0:T(8,128)(2,1)S(1)} custom-call(s32[1]{0:T(128)} %bitcast.3.side, s32[1]{0:T(128)} %bitcast.me, bf16[480,1792]{1,0:T(8,128)(2,1)S(1)} %pad_maximum_fusion.block, bf16[480,1792]{1,0:T(8,128)(2,1)} %collective-permute-done.7.block_far, bf16[3584,512]{1,0:T(8,128)(2,1)S(1)} %bitcast.6, bf16[3584,512]{1,0:T(8,128)(2,1)S(1)} %bitcast.17, ...), custom_call_target="tpu_custom_call" | custom-call | flops 1024 | bytes 1024 | tf_op jit(solution)/shard_map/grads/pallas_call | solution.py:249
  55.3 5.7 %collective-permute-done.8 = bf16[208,1792]{1,0:T(8,128)(2,1)} collective-permute-done((bf16[208,1792]{1,0:T(8,128)(2,1)S(1)}, bf16[208,1792]{1,0:T(8,128)(2,1)}, u32[]{:S(2)}, u32[]{:S(2)}) %collective-permute-start.8) | collective-permute-done | bytes 745504 | tf_op jit(solution)/shard_map/ppermute | solution.py:104
  61.0 1.5 collective-permute-done.6
  62.6 2.1 %constant_dynamic-update-slice_fusion.block = bf16[480,1792]{1,0:T(8,128)(2,1)} fusion(bf16[480,1792]{1,0:T(8,128)(2,1)} %constant_dynamic-update-slice_fusion.1, bf16[208,1792]{1,0:T(8,128)(2,1)} %collective-permute-done.8), kind=kLoop, calls=%fused_computation.6 | loop fusion | bytes 1490944 | tf_op jit(solution)/shard_map/concatenate | solution.py:366
  64.6 1.5 broadcast_select_fusion.rest_0_.both
  66.1 2.3 %collective-permute-start.9 = (bf16[272,1792]{1,0:T(8,128)(2,1)S(1)}, bf16[272,1792]{1,0:T(8,128)(2,1)S(1)}, u32[]{:S(2)}, u32[]{:S(2)}) collective-permute-start(bf16[272,1792]{1,0:T(8,128)(2,1)S(1)} %broadcast_select_fusion.rest_0_.both), channel_id=1, source_target_pairs={{8,12},{10,14},{4,0},{6,2},{9,13},{11,15},{5,1},{7,3},{24,28},{26,... | collective-permute-start | bytes 2924552 | tf_op jit(solution)/shard_map/ppermute | solution.py:104
  68.4 1.7 pick.7
  70.5 1.6 collective-permute-start.12
  72.1 2.5 %collective-permute-start.16 = (bf16[208,1792]{1,0:T(8,128)(2,1)S(1)}, bf16[208,1792]{1,0:T(8,128)(2,1)S(1)}, u32[]{:S(2)}, u32[]{:S(2)}) collective-permute-start(bf16[208,1792]{1,0:T(8,128)(2,1)S(1)} %get-tuple-element.57.rest_0_), channel_id=1, source_target_pairs={{0,2},{2,0},{4,6},{6,4},{8,10},{10,8},{1,3},{3,1},{5,7},{7,5},{9,1... | collective-permute-start | bytes 2236424 | tf_op jit(solution)/shard_map/ppermute | solution.py:104
  74.7 1.3 constant_dynamic-update-slice_fusion.3
  76.5 2.0 %copy-done.5 = bf16[2,1792,512]{2,1,0:T(8,128)(2,1)S(1)} copy-done((bf16[2,1792,512]{2,1,0:T(8,128)(2,1)S(1)}, bf16[2,1792,512]{2,1,0:T(8,128)(2,1)}, u32[]{:S(2)}) %copy-start.5) | copy-done | bytes 3670040
  78.6 2.3 %back.5 = (f32[128,1792]{1,0:T(8,128)S(1)}, bf16[96,1792]{1,0:T(8,128)(2,1)S(1)}) custom-call(s32[1]{0:T(128)} %bitcast.3.side, bf16[224,1024]{1,0:T(8,128)(2,1)S(1)} %grads.5.own, bf16[224,1024]{1,0:T(8,128)(2,1)S(1)} %collective-permute-done.10.other, bf16[3584,512]{1,0:T(8,128)(2,1)S(1)} %bitcast.7, bf16[3584,512]{1,0:T(8,128)(2,1)S(1)} %bitcast.18, ...), custom_call_target="tpu_custom_call" | custom-call | flops 1024 | bytes 1024 | tf_op jit(solution)/shard_map/back/pallas_call | solution.py:302
  80.9 4.4 %grads.6.own = bf16[224,1024]{1,0:T(8,128)(2,1)S(1)} custom-call(s32[1]{0:T(128)} %bitcast.3.side, s32[1]{0:T(128)} %bitcast.me, bf16[480,1792]{1,0:T(8,128)(2,1)} %constant_dynamic-update-slice_fusion.block, bf16[480,1792]{1,0:T(8,128)(2,1)S(1)} %collective-permute-done.11.block_far, bf16[3584,512]{1,0:T(8,128)(2,1)S(1)} %bitcast.8, ...), custom_call_target="tpu_custom_call" | custom-call | flops 1024 | bytes 1024 | tf_op jit(solution)/shard_map/grads/pallas_call | solution.py:249
  85.3 4.8 %collective-permute-done.12 = bf16[208,1792]{1,0:T(8,128)(2,1)S(1)} collective-permute-done((bf16[208,1792]{1,0:T(8,128)(2,1)S(1)}, bf16[208,1792]{1,0:T(8,128)(2,1)S(1)}, u32[]{:S(2)}, u32[]{:S(2)}) %collective-permute-start.12) | collective-permute-done | bytes 745504 | tf_op jit(solution)/shard_map/ppermute | solution.py:104
  90.8 14.6 %collective-permute-done.16 = bf16[208,1792]{1,0:T(8,128)(2,1)S(1)} collective-permute-done((bf16[208,1792]{1,0:T(8,128)(2,1)S(1)}, bf16[208,1792]{1,0:T(8,128)(2,1)S(1)}, u32[]{:S(2)}, u32[]{:S(2)}) %collective-permute-start.16) | collective-permute-done | bytes 745504 | tf_op jit(solution)/shard_map/ppermute | solution.py:104
  106.9 2.9 %collective-permute-done.14.other = bf16[224,1024]{1,0:T(8,128)(2,1)S(1)} collective-permute-done((bf16[224,1024]{1,0:T(8,128)(2,1)S(1)}, bf16[224,1024]{1,0:T(8,128)(2,1)S(1)}, u32[]{:S(2)}, u32[]{:S(2)}) %collective-permute-start.14) | collective-permute-done | bytes 458784 | tf_op jit(solution)/shard_map/ppermute | solution.py:108
  109.7 2.3 %back.6 = (f32[128,1792]{1,0:T(8,128)S(1)}, bf16[96,1792]{1,0:T(8,128)(2,1)S(1)}) custom-call(s32[1]{0:T(128)} %bitcast.3.side, bf16[224,1024]{1,0:T(8,128)(2,1)S(1)} %grads.6.own, bf16[224,1024]{1,0:T(8,128)(2,1)S(1)} %collective-permute-done.14.other, bf16[3584,512]{1,0:T(8,128)(2,1)S(1)} %bitcast.9, bf16[3584,512]{1,0:T(8,128)(2,1)S(1)} %bitcast.20, ...), custom_call_target="tpu_custom_call" | custom-call | flops 1024 | bytes 1024 | tf_op jit(solution)/shard_map/back/pallas_call | solution.py:302
  112.1 3.4 %collective-permute-start.15 = (bf16[96,1792]{1,0:T(8,128)(2,1)S(1)}, bf16[96,1792]{1,0:T(8,128)(2,1)S(1)}, u32[]{:S(2)}, u32[]{:S(2)}) collective-permute-start(bf16[96,1792]{1,0:T(8,128)(2,1)S(1)} %get-tuple-element.68), channel_id=1, source_target_pairs={{4,6},{6,4},{8,10},{10,8},{12,14},{14,12},{5,7},{7,5},{9,11},{11,9... | collective-permute-start | bytes 1032200 | tf_op jit(solution)/shard_map/ppermute | solution.py:104
  115.6 2.9 %grads.7.rest_0_.own = bf16[224,1024]{1,0:T(8,128)(2,1)S(1)} custom-call(s32[1]{0:T(128)} %bitcast.3.side, s32[1]{0:T(128)} %bitcast.me, bf16[480,1792]{1,0:T(8,128)(2,1)S(1)} %pad_maximum_fusion.1.block, bf16[480,1792]{1,0:T(8,128)(2,1)S(1)} %collective-permute-done.18.block_far, bf16[3584,512]{1,0:T(8,128)(2,1)S(1)} %bitcast.10, ...), custom_call_target="tpu_custom_call" | custom-call | flops 1024 | bytes 1024 | tf_op jit(solution)/shard_map/grads/pallas_call | solution.py:249
  118.5 2.9 %grads.8.rest_0_.own = bf16[224,1024]{1,0:T(8,128)(2,1)S(1)} custom-call(s32[1]{0:T(128)} %bitcast.3.side, s32[1]{0:T(128)} %bitcast.me, bf16[480,1792]{1,0:T(8,128)(2,1)S(1)} %constant_dynamic-update-slice_fusion.2.block, bf16[480,1792]{1,0:T(8,128)(2,1)S(1)} %collective-permute-done.17.block_far, bf16[3584,512]{1,0:T(8,128)(2,1)S(1)} %bitcast.11, ...), custom_call_target="tpu_custom_call" | custom-call | flops 1024 | bytes 1024 | tf_op jit(solution)/shard_map/grads/pallas_call | solution.py:249
  121.3 2.7 %collective-permute-done.15.came = bf16[96,1792]{1,0:T(8,128)(2,1)S(1)} collective-permute-done((bf16[96,1792]{1,0:T(8,128)(2,1)S(1)}, bf16[96,1792]{1,0:T(8,128)(2,1)S(1)}, u32[]{:S(2)}, u32[]{:S(2)}) %collective-permute-start.15) | collective-permute-done | bytes 344096 | tf_op jit(solution)/shard_map/ppermute | solution.py:104
  125.1 3.8 %collective-permute-start.23 = (bf16[128,1792]{1,0:T(8,128)(2,1)S(1)}, bf16[128,1792]{1,0:T(8,128)(2,1)S(1)}, u32[]{:S(2)}, u32[]{:S(2)}) collective-permute-start(bf16[128,1792]{1,0:T(8,128)(2,1)S(1)} %join.5), channel_id=1, source_target_pairs={{4,0},{6,2},{8,4},{10,6},{12,8},{14,10},{5,1},{7,3},{9,5},{11,7},{... | collective-permute-start | bytes 1376264 | tf_op jit(solution)/shard_map/ppermute | solution.py:104
  129.0 2.3 %back.7 = (f32[128,1792]{1,0:T(8,128)S(1)}, bf16[96,1792]{1,0:T(8,128)(2,1)S(1)}) custom-call(s32[1]{0:T(128)} %bitcast.3.side, bf16[224,1024]{1,0:T(8,128)(2,1)S(1)} %grads.7.rest_0_.own, bf16[224,1024]{1,0:T(8,128)(2,1)S(1)} %collective-permute-done.20.other, bf16[3584,512]{1,0:T(8,128)(2,1)S(1)} %bitcast.12, bf16[3584,512]{1,0:T(8,128)(2,1)S(1)} %bitcast.23, ...), custom_call_target="tpu_custom_call" | custom-call | flops 1024 | bytes 1024 | tf_op jit(solution)/shard_map/back/pallas_call | solution.py:302
  131.3 2.9 %grads.9.rest_0_.own = bf16[224,1024]{1,0:T(8,128)(2,1)S(1)} custom-call(s32[1]{0:T(128)} %bitcast.3.side, s32[1]{0:T(128)} %bitcast.me, bf16[480,1792]{1,0:T(8,128)(2,1)S(1)} %constant_dynamic-update-slice_fusion.4.block, bf16[480,1792]{1,0:T(8,128)(2,1)S(1)} %collective-permute-done.19.block_far, bf16[3584,512]{1,0:T(8,128)(2,1)S(1)} %bitcast.13, ...), custom_call_target="tpu_custom_call" | custom-call | flops 1024 | bytes 1024 | tf_op jit(solution)/shard_map/grads/pallas_call | solution.py:249
  134.4 1.5 collective-permute-start.26
  135.9 2.3 %back.8 = (f32[128,1792]{1,0:T(8,128)S(1)}, bf16[96,1792]{1,0:T(8,128)(2,1)S(1)}) custom-call(s32[1]{0:T(128)} %bitcast.3.side, bf16[224,1024]{1,0:T(8,128)(2,1)S(1)} %grads.8.rest_0_.own, bf16[224,1024]{1,0:T(8,128)(2,1)S(1)} %collective-permute-done.22.other, bf16[3584,512]{1,0:T(8,128)(2,1)S(1)} %bitcast.14, bf16[3584,512]{1,0:T(8,128)(2,1)S(1)} %bitcast.25, ...), custom_call_target="tpu_custom_call" | custom-call | flops 1024 | bytes 1024 | tf_op jit(solution)/shard_map/back/pallas_call | solution.py:302
  138.3 2.4 %collective-permute-start.25 = (bf16[96,1792]{1,0:T(8,128)(2,1)S(1)}, bf16[96,1792]{1,0:T(8,128)(2,1)S(1)}, u32[]{:S(2)}, u32[]{:S(2)}) collective-permute-start(bf16[96,1792]{1,0:T(8,128)(2,1)S(1)} %get-tuple-element.82), channel_id=1, source_target_pairs={{0,2},{2,0},{4,6},{6,4},{8,10},{10,8},{1,3},{3,1},{5,7},{7,5},{9,1... | collective-permute-start | bytes 1032200 | tf_op jit(solution)/shard_map/ppermute | solution.py:104
  140.7 2.4 %back.9 = (f32[128,1792]{1,0:T(8,128)S(1)}, bf16[96,1792]{1,0:T(8,128)(2,1)S(1)}) custom-call(s32[1]{0:T(128)} %bitcast.3.side, bf16[224,1024]{1,0:T(8,128)(2,1)S(1)} %grads.9.rest_0_.own, bf16[224,1024]{1,0:T(8,128)(2,1)S(1)} %collective-permute-done.21.other, bf16[3584,512]{1,0:T(8,128)(2,1)S(1)} %bitcast.15, bf16[3584,512]{1,0:T(8,128)(2,1)S(1)} %bitcast.26, ...), custom_call_target="tpu_custom_call" | custom-call | flops 1024 | bytes 1024 | tf_op jit(solution)/shard_map/back/pallas_call | solution.py:302
  143.8 1.5 collective-permute-done.26.came
  145.7 6.4 %collective-permute-done.25.came = bf16[96,1792]{1,0:T(8,128)(2,1)S(1)} collective-permute-done((bf16[96,1792]{1,0:T(8,128)(2,1)S(1)}, bf16[96,1792]{1,0:T(8,128)(2,1)S(1)}, u32[]{:S(2)}, u32[]{:S(2)}) %collective-permute-start.25) | collective-permute-done | bytes 344096 | tf_op jit(solution)/shard_map/ppermute | solution.py:104
  152.4 2.3 %collective-permute-start.27 = (bf16[128,1792]{1,0:T(8,128)(2,1)S(1)}, bf16[128,1792]{1,0:T(8,128)(2,1)S(1)}, u32[]{:S(2)}, u32[]{:S(2)}) collective-permute-start(bf16[128,1792]{1,0:T(8,128)(2,1)S(1)} %join.7.rest_2_.rest_0_), channel_id=1, source_target_pairs={{0,4},{2,6},{4,8},{6,10},{8,12},{10,14},{1,5},{3,7},{5,9},{7,11},{... | collective-permute-start | bytes 1376264 | tf_op jit(solution)/shard_map/ppermute | solution.py:104
  155.8 1.6 collective-permute-start.24
  157.3 7.8 %collective-permute-done.24.came = bf16[96,1792]{1,0:T(8,128)(2,1)S(1)} collective-permute-done((bf16[96,1792]{1,0:T(8,128)(2,1)S(1)}, bf16[96,1792]{1,0:T(8,128)(2,1)S(1)}, u32[]{:S(2)}, u32[]{:S(2)}) %collective-permute-start.24) | collective-permute-done | bytes 344096 | tf_op jit(solution)/shard_map/ppermute | solution.py:104
  165.5 1.2 collective-permute-done.28
  166.6 17.8 %collective-permute-done.27 = bf16[128,1792]{1,0:T(8,128)(2,1)S(1)} collective-permute-done((bf16[128,1792]{1,0:T(8,128)(2,1)S(1)}, bf16[128,1792]{1,0:T(8,128)(2,1)S(1)}, u32[]{:S(2)}, u32[]{:S(2)}) %collective-permute-start.27) | collective-permute-done | bytes 458784 | tf_op jit(solution)/shard_map/ppermute | solution.py:104
  (71 shorter events, 11.1 us)
Async XLA Ops:
  0.0 32.0 %collective-permute-start.3 = (bf16[3584,512]{1,0:T(8,128)(2,1)}, bf16[3584,512]{1,0:T(8,128)(2,1)}, u32[]{:S(2)}, u32[]{:S(2)}) collective-permute-start(bf16[3584,512]{1,0:T(8,128)(2,1)} %bitcast.5), channel_id=1, source_target_pairs={{0,1},{1,0},{2,3},{3,2},{4,5},{5,4},{6,7},{7,6},{8,9},{9,8},{10,11... | collective-permute-start | bytes 11010056 | tf_op jit(solution)/shard_map/ppermute | solution.py:108
  0.0 32.0 %collective-permute-start.4 = (bf16[3584,512]{1,0:T(8,128)(2,1)}, bf16[3584,512]{1,0:T(8,128)(2,1)}, u32[]{:S(2)}, u32[]{:S(2)}) collective-permute-start(bf16[3584,512]{1,0:T(8,128)(2,1)} %bitcast.16), channel_id=1, source_target_pairs={{0,1},{1,0},{2,3},{3,2},{4,5},{5,4},{6,7},{7,6},{8,9},{9,8},{10,11... | collective-permute-start | bytes 11010056 | tf_op jit(solution)/shard_map/ppermute | solution.py:108
  1.2 1.0 copy-start.9
  2.2 1.0 copy-start.11
  3.3 25.5 %collective-permute-start = (bf16[272,1792]{1,0:T(8,128)(2,1)S(1)}, bf16[272,1792]{1,0:T(8,128)(2,1)}, u32[]{:S(2)}, u32[]{:S(2)}) collective-permute-start(bf16[272,1792]{1,0:T(8,128)(2,1)S(1)} %stack.1.both), channel_id=1, source_target_pairs={{0,4},{2,6},{4,8},{6,10},{8,12},{10,14},{1,5},{3,7},{5,9},{7,11},{... | collective-permute-start | bytes 2924552 | tf_op jit(solution)/shard_map/ppermute | solution.py:104
  6.8 25.2 %collective-permute-start.1 = (bf16[272,1792]{1,0:T(8,128)(2,1)S(1)}, bf16[272,1792]{1,0:T(8,128)(2,1)}, u32[]{:S(2)}, u32[]{:S(2)}) collective-permute-start(bf16[272,1792]{1,0:T(8,128)(2,1)S(1)} %stack.1.both), channel_id=1, source_target_pairs={{4,0},{6,2},{8,4},{10,6},{12,8},{14,10},{5,1},{7,3},{9,5},{11,7},{... | collective-permute-start | bytes 2924552 | tf_op jit(solution)/shard_map/ppermute | solution.py:104
  10.7 18.1 %collective-permute-start.2 = (bf16[208,1792]{1,0:T(8,128)(2,1)S(1)}, bf16[208,1792]{1,0:T(8,128)(2,1)S(1)}, u32[]{:S(2)}, u32[]{:S(2)}) collective-permute-start(bf16[208,1792]{1,0:T(8,128)(2,1)S(1)} %get-tuple-element.47), channel_id=1, source_target_pairs={{0,2},{2,0},{4,6},{6,4},{8,10},{10,8},{12,14},{14,12},{1,3},{3,1},... | collective-permute-start | bytes 2236424 | tf_op jit(solution)/shard_map/ppermute | solution.py:104
  32.2 18.1 %collective-permute-start.7 = (bf16[480,1792]{1,0:T(8,128)(2,1)S(1)}, bf16[480,1792]{1,0:T(8,128)(2,1)}, u32[]{:S(2)}, u32[]{:S(2)}) collective-permute-start(bf16[480,1792]{1,0:T(8,128)(2,1)S(1)} %pad_maximum_fusion.block), channel_id=1, source_target_pairs={{0,1},{1,0},{2,3},{3,2},{4,5},{5,4},{6,7},{7,6},{8,9},{9,8},{10,11... | collective-permute-start | bytes 5160968 | tf_op jit(solution)/shard_map/ppermute | solution.py:108
  32.2 28.8 %collective-permute-start.5 = (bf16[272,1792]{1,0:T(8,128)(2,1)}, bf16[272,1792]{1,0:T(8,128)(2,1)}, u32[]{:S(2)}, u32[]{:S(2)}) collective-permute-start(bf16[272,1792]{1,0:T(8,128)(2,1)} %collective-permute-done.both), channel_id=1, source_target_pairs={{4,8},{6,10},{8,12},{10,14},{5,9},{7,11},{9,13},{11,15},{20,24},{2... | collective-permute-start | bytes 2924552 | tf_op jit(solution)/shard_map/ppermute | solution.py:104
  36.7 25.9 %collective-permute-start.6 = (bf16[272,1792]{1,0:T(8,128)(2,1)}, bf16[272,1792]{1,0:T(8,128)(2,1)}, u32[]{:S(2)}, u32[]{:S(2)}) collective-permute-start(bf16[272,1792]{1,0:T(8,128)(2,1)} %collective-permute-done.1.both), channel_id=1, source_target_pairs={{8,4},{10,6},{4,0},{6,2},{9,5},{11,7},{5,1},{7,3},{24,20},{26,22},... | collective-permute-start | bytes 2924552 | tf_op jit(solution)/shard_map/ppermute | solution.py:104
  40.3 20.8 %collective-permute-start.8 = (bf16[208,1792]{1,0:T(8,128)(2,1)S(1)}, bf16[208,1792]{1,0:T(8,128)(2,1)}, u32[]{:S(2)}, u32[]{:S(2)}) collective-permute-start(bf16[208,1792]{1,0:T(8,128)(2,1)S(1)} %get-tuple-element.51.rest_0_), channel_id=1, source_target_pairs={{4,6},{6,4},{8,10},{10,8},{12,14},{14,12},{5,7},{7,5},{9,11},{11,9... | collective-permute-start | bytes 2236424 | tf_op jit(solution)/shard_map/ppermute | solution.py:104
  43.7 6.6 %copy-start = (bf16[1,3584,512]{2,1,0:T(8,128)(2,1)S(1)}, bf16[1,3584,512]{2,1,0:T(8,128)(2,1)}, u32[]{:S(2)}) copy-start(bf16[1,3584,512]{2,1,0:T(8,128)(2,1)} %param.11) | copy-start | bytes 11010052
  43.7 6.6 %copy-start.2 = (bf16[1,3584,512]{2,1,0:T(8,128)(2,1)S(1)}, bf16[1,3584,512]{2,1,0:T(8,128)(2,1)}, u32[]{:S(2)}) copy-start(bf16[1,3584,512]{2,1,0:T(8,128)(2,1)} %param.12) | copy-start | bytes 11010052
  43.7 7.3 %copy-start.7 = (bf16[1,512,3584]{2,1,0:T(8,128)(2,1)S(1)}, bf16[1,512,3584]{2,1,0:T(8,128)(2,1)}, u32[]{:S(2)}) copy-start(bf16[1,512,3584]{2,1,0:T(8,128)(2,1)} %param.13) | copy-start | bytes 11010052
  46.0 9.3 %copy-start.4 = (bf16[2,1792,512]{2,1,0:T(8,128)(2,1)}, bf16[2,1792,512]{2,1,0:T(8,128)(2,1)S(1)}, u32[]{:S(2)}) copy-start(bf16[2,1792,512]{2,1,0:T(8,128)(2,1)S(1)} %keep.1.rest_1_.far) | copy-start | bytes 11010052
  64.6 16.3 %collective-permute-start.11 = (bf16[480,1792]{1,0:T(8,128)(2,1)}, bf16[480,1792]{1,0:T(8,128)(2,1)S(1)}, u32[]{:S(2)}, u32[]{:S(2)}) collective-permute-start(bf16[480,1792]{1,0:T(8,128)(2,1)} %constant_dynamic-update-slice_fusion.block), channel_id=1, source_target_pairs={{0,1},{1,0},{2,3},{3,2},{4,5},{5,4},{6,7},{7,6},{8,9},{9,8},{10,11... | collective-permute-start | bytes 5160968 | tf_op jit(solution)/shard_map/ppermute | solution.py:108
  64.6 11.9 %copy-start.3 = (bf16[1,3584,512]{2,1,0:T(8,128)(2,1)S(1)}, bf16[1,3584,512]{2,1,0:T(8,128)(2,1)}, u32[]{:S(2)}) copy-start(bf16[1,3584,512]{2,1,0:T(8,128)(2,1)} %param.12) | copy-start | bytes 11010052
  66.1 24.0 %collective-permute-start.9 = (bf16[272,1792]{1,0:T(8,128)(2,1)S(1)}, bf16[272,1792]{1,0:T(8,128)(2,1)S(1)}, u32[]{:S(2)}, u32[]{:S(2)}) collective-permute-start(bf16[272,1792]{1,0:T(8,128)(2,1)S(1)} %broadcast_select_fusion.rest_0_.both), channel_id=1, source_target_pairs={{8,12},{10,14},{4,0},{6,2},{9,13},{11,15},{5,1},{7,3},{24,28},{26,... | collective-permute-start | bytes 2924552 | tf_op jit(solution)/shard_map/ppermute | solution.py:104
  70.0 6.5 %copy-start.1 = (bf16[1,3584,512]{2,1,0:T(8,128)(2,1)S(1)}, bf16[1,3584,512]{2,1,0:T(8,128)(2,1)}, u32[]{:S(2)}) copy-start(bf16[1,3584,512]{2,1,0:T(8,128)(2,1)} %param.11) | copy-start | bytes 11010052
  70.5 19.6 %collective-permute-start.12 = (bf16[208,1792]{1,0:T(8,128)(2,1)S(1)}, bf16[208,1792]{1,0:T(8,128)(2,1)S(1)}, u32[]{:S(2)}, u32[]{:S(2)}) collective-permute-start(bf16[208,1792]{1,0:T(8,128)(2,1)S(1)} %get-tuple-element.58.rest_0_), channel_id=1, source_target_pairs={{0,2},{2,0},{4,6},{6,4},{8,10},{10,8},{12,14},{14,12},{1,3},{3,1},... | collective-permute-start | bytes 2236424 | tf_op jit(solution)/shard_map/ppermute | solution.py:104
  72.1 33.2 %collective-permute-start.16 = (bf16[208,1792]{1,0:T(8,128)(2,1)S(1)}, bf16[208,1792]{1,0:T(8,128)(2,1)S(1)}, u32[]{:S(2)}, u32[]{:S(2)}) collective-permute-start(bf16[208,1792]{1,0:T(8,128)(2,1)S(1)} %get-tuple-element.57.rest_0_), channel_id=1, source_target_pairs={{0,2},{2,0},{4,6},{6,4},{8,10},{10,8},{1,3},{3,1},{5,7},{7,5},{9,1... | collective-permute-start | bytes 2236424 | tf_op jit(solution)/shard_map/ppermute | solution.py:104
  74.6 1.9 %collective-permute-start.10 = (bf16[224,1024]{1,0:T(8,128)(2,1)S(1)}, bf16[224,1024]{1,0:T(8,128)(2,1)S(1)}, u32[]{:S(2)}, u32[]{:S(2)}) collective-permute-start(bf16[224,1024]{1,0:T(8,128)(2,1)S(1)} %grads.5.own), channel_id=1, source_target_pairs={{0,1},{1,0},{2,3},{3,2},{4,5},{5,4},{6,7},{7,6},{8,9},{9,8},{10,11... | collective-permute-start | bytes 1376264 | tf_op jit(solution)/shard_map/ppermute | solution.py:108
  76.5 2.0 %copy-start.5 = (bf16[2,1792,512]{2,1,0:T(8,128)(2,1)S(1)}, bf16[2,1792,512]{2,1,0:T(8,128)(2,1)}, u32[]{:S(2)}) copy-start(bf16[2,1792,512]{2,1,0:T(8,128)(2,1)} %copy-done.4) | copy-start | bytes 11010052
  78.6 2.3 %copy-start.8 = (bf16[1,512,3584]{2,1,0:T(8,128)(2,1)S(1)}, bf16[1,512,3584]{2,1,0:T(8,128)(2,1)}, u32[]{:S(2)}) copy-start(bf16[1,512,3584]{2,1,0:T(8,128)(2,1)} %param.13) | copy-start | bytes 11010052
  90.5 19.2 %copy-start.6 = (bf16[2,1792,512]{2,1,0:T(8,128)(2,1)S(1)}, bf16[2,1792,512]{2,1,0:T(8,128)(2,1)}, u32[]{:S(2)}) copy-start(bf16[2,1792,512]{2,1,0:T(8,128)(2,1)} %copy-done.4) | copy-start | bytes 11010052
  90.7 24.9 %collective-permute-start.18 = (bf16[480,1792]{1,0:T(8,128)(2,1)S(1)}, bf16[480,1792]{1,0:T(8,128)(2,1)S(1)}, u32[]{:S(2)}, u32[]{:S(2)}) collective-permute-start(bf16[480,1792]{1,0:T(8,128)(2,1)S(1)} %pad_maximum_fusion.1.block), channel_id=1, source_target_pairs={{0,1},{1,0},{2,3},{3,2},{4,5},{5,4},{6,7},{7,6},{8,9},{9,8},{10,11... | collective-permute-start | bytes 5160968 | tf_op jit(solution)/shard_map/ppermute | solution.py:108
  105.4 13.1 %collective-permute-start.17 = (bf16[480,1792]{1,0:T(8,128)(2,1)S(1)}, bf16[480,1792]{1,0:T(8,128)(2,1)S(1)}, u32[]{:S(2)}, u32[]{:S(2)}) collective-permute-start(bf16[480,1792]{1,0:T(8,128)(2,1)S(1)} %constant_dynamic-update-slice_fusion.2.block), channel_id=1, source_target_pairs={{0,1},{1,0},{2,3},{3,2},{4,5},{5,4},{6,7},{7,6},{8,9},{9,8},{10,11... | collective-permute-start | bytes 5160968 | tf_op jit(solution)/shard_map/ppermute | solution.py:108
  105.5 4.3 %collective-permute-start.14 = (bf16[224,1024]{1,0:T(8,128)(2,1)S(1)}, bf16[224,1024]{1,0:T(8,128)(2,1)S(1)}, u32[]{:S(2)}, u32[]{:S(2)}) collective-permute-start(bf16[224,1024]{1,0:T(8,128)(2,1)S(1)} %grads.6.own), channel_id=1, source_target_pairs={{0,1},{1,0},{2,3},{3,2},{4,5},{5,4},{6,7},{7,6},{8,9},{9,8},{10,11... | collective-permute-start | bytes 1376264 | tf_op jit(solution)/shard_map/ppermute | solution.py:108
  106.0 18.4 %collective-permute-start.13 = (bf16[208,1792]{1,0:T(8,128)(2,1)S(1)}, bf16[208,1792]{1,0:T(8,128)(2,1)S(1)}, u32[]{:S(2)}, u32[]{:S(2)}) collective-permute-start(bf16[208,1792]{1,0:T(8,128)(2,1)S(1)} %get-tuple-element.64), channel_id=1, source_target_pairs={{0,2},{2,0},{12,14},{14,12},{1,3},{3,1},{13,15},{15,13},{16,18},{1... | collective-permute-start | bytes 2236424 | tf_op jit(solution)/shard_map/ppermute | solution.py:104
  112.1 12.0 %collective-permute-start.15 = (bf16[96,1792]{1,0:T(8,128)(2,1)S(1)}, bf16[96,1792]{1,0:T(8,128)(2,1)S(1)}, u32[]{:S(2)}, u32[]{:S(2)}) collective-permute-start(bf16[96,1792]{1,0:T(8,128)(2,1)S(1)} %get-tuple-element.68), channel_id=1, source_target_pairs={{4,6},{6,4},{8,10},{10,8},{12,14},{14,12},{5,7},{7,5},{9,11},{11,9... | collective-permute-start | bytes 1032200 | tf_op jit(solution)/shard_map/ppermute | solution.py:104
  124.5 6.8 %collective-permute-start.19 = (bf16[480,1792]{1,0:T(8,128)(2,1)S(1)}, bf16[480,1792]{1,0:T(8,128)(2,1)S(1)}, u32[]{:S(2)}, u32[]{:S(2)}) collective-permute-start(bf16[480,1792]{1,0:T(8,128)(2,1)S(1)} %constant_dynamic-update-slice_fusion.4.block), channel_id=1, source_target_pairs={{0,1},{1,0},{2,3},{3,2},{4,5},{5,4},{6,7},{7,6},{8,9},{9,8},{10,11... | collective-permute-start | bytes 5160968 | tf_op jit(solution)/shard_map/ppermute | solution.py:108
  124.5 4.4 %collective-permute-start.20 = (bf16[224,1024]{1,0:T(8,128)(2,1)S(1)}, bf16[224,1024]{1,0:T(8,128)(2,1)S(1)}, u32[]{:S(2)}, u32[]{:S(2)}) collective-permute-start(bf16[224,1024]{1,0:T(8,128)(2,1)S(1)} %grads.7.rest_0_.own), channel_id=1, source_target_pairs={{0,1},{1,0},{2,3},{3,2},{4,5},{5,4},{6,7},{7,6},{8,9},{9,8},{10,11... | collective-permute-start | bytes 1376264 | tf_op jit(solution)/shard_map/ppermute | solution.py:108
  125.0 10.9 %collective-permute-start.22 = (bf16[224,1024]{1,0:T(8,128)(2,1)S(1)}, bf16[224,1024]{1,0:T(8,128)(2,1)S(1)}, u32[]{:S(2)}, u32[]{:S(2)}) collective-permute-start(bf16[224,1024]{1,0:T(8,128)(2,1)S(1)} %grads.8.rest_0_.own), channel_id=1, source_target_pairs={{0,1},{1,0},{2,3},{3,2},{4,5},{5,4},{6,7},{7,6},{8,9},{9,8},{10,11... | collective-permute-start | bytes 1376264 | tf_op jit(solution)/shard_map/ppermute | solution.py:108
  125.1 15.6 %collective-permute-start.23 = (bf16[128,1792]{1,0:T(8,128)(2,1)S(1)}, bf16[128,1792]{1,0:T(8,128)(2,1)S(1)}, u32[]{:S(2)}, u32[]{:S(2)}) collective-permute-start(bf16[128,1792]{1,0:T(8,128)(2,1)S(1)} %join.5), channel_id=1, source_target_pairs={{4,0},{6,2},{8,4},{10,6},{12,8},{14,10},{5,1},{7,3},{9,5},{11,7},{... | collective-permute-start | bytes 1376264 | tf_op jit(solution)/shard_map/ppermute | solution.py:104
  134.2 6.6 %collective-permute-start.21 = (bf16[224,1024]{1,0:T(8,128)(2,1)S(1)}, bf16[224,1024]{1,0:T(8,128)(2,1)S(1)}, u32[]{:S(2)}, u32[]{:S(2)}) collective-permute-start(bf16[224,1024]{1,0:T(8,128)(2,1)S(1)} %grads.9.rest_0_.own), channel_id=1, source_target_pairs={{0,1},{1,0},{2,3},{3,2},{4,5},{5,4},{6,7},{7,6},{8,9},{9,8},{10,11... | collective-permute-start | bytes 1376264 | tf_op jit(solution)/shard_map/ppermute | solution.py:108
  134.4 10.9 %collective-permute-start.26 = (bf16[96,1792]{1,0:T(8,128)(2,1)S(1)}, bf16[96,1792]{1,0:T(8,128)(2,1)S(1)}, u32[]{:S(2)}, u32[]{:S(2)}) collective-permute-start(bf16[96,1792]{1,0:T(8,128)(2,1)S(1)} %get-tuple-element.84), channel_id=1, source_target_pairs={{0,2},{2,0},{4,6},{6,4},{8,10},{10,8},{12,14},{14,12},{1,3},{3,1},... | collective-permute-start | bytes 1032200 | tf_op jit(solution)/shard_map/ppermute | solution.py:104
  138.3 13.8 %collective-permute-start.25 = (bf16[96,1792]{1,0:T(8,128)(2,1)S(1)}, bf16[96,1792]{1,0:T(8,128)(2,1)S(1)}, u32[]{:S(2)}, u32[]{:S(2)}) collective-permute-start(bf16[96,1792]{1,0:T(8,128)(2,1)S(1)} %get-tuple-element.82), channel_id=1, source_target_pairs={{0,2},{2,0},{4,6},{6,4},{8,10},{10,8},{1,3},{3,1},{5,7},{7,5},{9,1... | collective-permute-start | bytes 1032200 | tf_op jit(solution)/shard_map/ppermute | solution.py:104
  143.1 11.6 %collective-permute-start.29 = (bf16[96,1792]{1,0:T(8,128)(2,1)S(1)}, bf16[96,1792]{1,0:T(8,128)(2,1)S(1)}, u32[]{:S(2)}, u32[]{:S(2)}) collective-permute-start(bf16[96,1792]{1,0:T(8,128)(2,1)S(1)} %get-tuple-element.86), channel_id=1, source_target_pairs={{0,2},{2,0},{12,14},{14,12},{1,3},{3,1},{13,15},{15,13},{16,18},{1... | collective-permute-start | bytes 1032200 | tf_op jit(solution)/shard_map/ppermute | solution.py:104
  145.6 21.0 %collective-permute-start.28 = (bf16[128,1792]{1,0:T(8,128)(2,1)S(1)}, bf16[128,1792]{1,0:T(8,128)(2,1)S(1)}, u32[]{:S(2)}, u32[]{:S(2)}) collective-permute-start(bf16[128,1792]{1,0:T(8,128)(2,1)S(1)} %join.6.rest_0_), channel_id=1, source_target_pairs={{0,8},{2,10},{4,12},{6,14},{8,0},{10,2},{12,4},{14,6},{1,9},{3,11}... | collective-permute-start | bytes 1376264 | tf_op jit(solution)/shard_map/ppermute | solution.py:104
  152.1 13.0 %copy-start.10 = (bf16[128,1792]{1,0:T(8,128)(2,1)S(1)}, bf16[128,1792]{1,0:T(8,128)(2,1)}, u32[]{:S(2)}) copy-start(bf16[128,1792]{1,0:T(8,128)(2,1)} %rest_0_.1) | copy-start | bytes 1376260
  152.4 32.0 %collective-permute-start.27 = (bf16[128,1792]{1,0:T(8,128)(2,1)S(1)}, bf16[128,1792]{1,0:T(8,128)(2,1)S(1)}, u32[]{:S(2)}, u32[]{:S(2)}) collective-permute-start(bf16[128,1792]{1,0:T(8,128)(2,1)S(1)} %join.7.rest_2_.rest_0_), channel_id=1, source_target_pairs={{0,4},{2,6},{4,8},{6,10},{8,12},{10,14},{1,5},{3,7},{5,9},{7,11},{... | collective-permute-start | bytes 1376264 | tf_op jit(solution)/shard_map/ppermute | solution.py:104
  155.1 29.4 %collective-permute-start.30 = (bf16[128,1792]{1,0:T(8,128)(2,1)S(1)}, bf16[128,1792]{1,0:T(8,128)(2,1)S(1)}, u32[]{:S(2)}, u32[]{:S(2)}) collective-permute-start(bf16[128,1792]{1,0:T(8,128)(2,1)S(1)} %join.9), channel_id=1, source_target_pairs={{0,12},{2,14},{12,0},{14,2},{1,13},{3,15},{13,1},{15,3},{16,28},{1... | collective-permute-start | bytes 1376264 | tf_op jit(solution)/shard_map/ppermute | solution.py:104
  155.8 9.3 %collective-permute-start.24 = (bf16[96,1792]{1,0:T(8,128)(2,1)S(1)}, bf16[96,1792]{1,0:T(8,128)(2,1)S(1)}, u32[]{:S(2)}, u32[]{:S(2)}) collective-permute-start(bf16[96,1792]{1,0:T(8,128)(2,1)S(1)} %get-tuple-element.80), channel_id=1, source_target_pairs={{0,2},{2,0},{4,6},{6,4},{8,10},{10,8},{12,14},{14,12},{1,3},{3,1},... | collective-permute-start | bytes 1032200 | tf_op jit(solution)/shard_map/ppermute | solution.py:104
